TPU v7x, 256 devices: a whole 4x4x8 slice. The times are simulated.
256 devices in a mesh: dp: 8 (over z_lo, x), seq: 32 (over z_hi, y, core).
Axes of the slice: x: 4, y: 4, z: 8 (z_hi: 4, z_lo: 2; z = z_hi * 2 + z_lo), core: 2. Of those that a mesh axis runs over, the one named last changes fastest.
Arguments:
- tokens: bfloat16 [8, 128, 256, 768], P('dp', 'seq'), may hold values from -6 to 6
- grad_out: bfloat16 [8, 128, 256, 768], P('dp', 'seq'), may hold values from -6 to 6
- right_blocks: bfloat16 [128, 256, 256], P('seq'), may hold values from -0.375 to 0.375
- left_blocks: bfloat16 [256, 128, 128], P('seq'), may hold values from -0.5 to 0.5
- in_weight: bfloat16 [768, 768], replicated, may hold values from -0.21875 to 0.21875
Outputs:
- mixed: bfloat16 [8, 128, 256, 768], P('dp', 'seq')
- grad_tokens: bfloat16 [8, 128, 256, 768], P('dp', 'seq')
- grad_left: bfloat16 [256, 128, 128], P('seq')
- grad_right: bfloat16 [128, 256, 256], P('seq')
- grad_weight: bfloat16 [768, 768], replicated
All inputs are finite; a program needn't handle non-finite values.
Results may differ from a plain program's by a relative error of at most 0.007.
Values may be sent and summed in bfloat16 or wider, within the bound.
No kernel may reach another device: no remote copies, remote signals or barrier semaphores. Data moves between devices by JAX's collectives and lax.ppermute only.
A program may use at most 128 MiB of HBM per device.

v0:
```python
import jax
import jax.numpy as jnp
from jax import lax
from jax.experimental import pallas as pl
from jax.experimental.pallas import tpu as pltpu
from jax.sharding import Mesh, PartitionSpec as P

F32 = jnp.float32
BF16 = jnp.bfloat16
CHIPS = ("zh", "y")
SIZES = {"zl": 2, "x": 4, "zh": 4, "y": 4, "c": 2}

LA, LJ, NCHIP, A, B, D = 4, 8, 16, 128, 256, 768
PARTS = jax.ShapeDtypeStruct((NCHIP, 2, LA * LJ, D), BF16)
WR, WCH = 576, 48
TWO = jax.ShapeDtypeStruct((NCHIP, 384 + WCH, 128), BF16)
VMEM = pl.BlockSpec(memory_space=pltpu.VMEM)
SMEM = pl.BlockSpec(memory_space=pltpu.SMEM)


def params(mib):
    return pltpu.CompilerParams(vmem_limit_bytes=mib * 1024 * 1024)


def cost(flops=1000, nbytes=1000):
    return pl.CostEstimate(flops=flops, bytes_accessed=nbytes, transcendentals=0)


def dot(a, b, ca, cb):
    return lax.dot_general(a, b, (((ca,), (cb,)), ((), ())), preferred_element_type=F32)


def grad_two_kernel(t_ref, g_ref, o_ref):
    for i in range(4):
        rows = pl.ds(i * 16, 16)
        v = t_ref[:, rows, :].astype(F32) * g_ref[:, rows, :].astype(F32)
        v = v.reshape(LA, 2, LJ, D)
        for core in range(2):
            o_ref[i, core] = v[:, core].reshape(LA * LJ, D).astype(BF16)


def grad_two_parts(tokens, grad_out):
    rows = pl.BlockSpec((LA, 64, D), lambda i: (0, i, 0))
    return pl.pallas_call(
        grad_two_kernel,
        grid=(4,),
        in_specs=[rows, rows],
        out_specs=pl.BlockSpec((4, 2, LA * LJ, D), lambda i: (i, 0, 0, 0)),
        out_shape=PARTS,
        compiler_params=params(60),
        name="grad_two",
    )(tokens, grad_out)


COLUMNS = pltpu.VMEM((6, A * LJ, 128), F32)


def put_rows(x_ref, rows, v):
    for k in range(6):
        x_ref[k, rows, :] = v[:, k * 128:(k + 1) * 128]


def get_rows(x_ref, rows):
    return jnp.concatenate([x_ref[k, rows, :] for k in range(6)], axis=1)


def to_parts(x_ref, o_ref):
    @pl.loop(0, NCHIP)
    def _(i):
        for core in range(2):
            o_ref[i, core] = get_rows(x_ref, pl.ds(i * 64 + core * 32, 32)).astype(BF16)


def front_kernel(t_ref, r_ref, w_ref, o_ref, p_ref, x_ref):
    for a in range(LA):
        t = t_ref[a]
        one = dot(r_ref[a], t, 1, 0)
        x_ref[:, pl.ds(a * LJ, LJ), :] = one.reshape(32, LJ, D)
        p_ref[a] = dot(t, w_ref[...], 1, 0).astype(BF16)

    @pl.loop(0, NCHIP)
    def _(i):
        o_ref[i] = x_ref[pl.ds(i * 2, 2)].astype(BF16)


def front(tokens, right_blocks, in_weight):
    return pl.pallas_call(
        front_kernel,
        in_specs=[VMEM] * 3,
        out_specs=[VMEM] * 2,
        out_shape=[PARTS, jax.ShapeDtypeStruct((LA, B, D), BF16)],
        scratch_shapes=[pltpu.VMEM((32, LA * LJ, D), F32)],
        compiler_params=params(18),
        cost_estimate=cost(),
        name="front",
    )(tokens, right_blocks, in_weight)


def load_columns(core, own_ref, other_ref, x_ref):
    @pl.loop(0, NCHIP)
    def _(i):
        put_rows(x_ref, pl.ds(i * 64 + core * 32, 32), own_ref[i, core].astype(F32))
        put_rows(x_ref, pl.ds(i * 64 + (1 - core) * 32, 32), other_ref[i, core].astype(F32))


def one_kernel(core_ref, own_ref, other_ref, l_ref, o_ref, gj_ref, oj_ref, x_ref):
    load_columns(core_ref[0], own_ref, other_ref, x_ref)
    for j in range(LJ):
        at = pl.ds(j, A, stride=LJ)
        g = get_rows(x_ref, at).astype(BF16)
        one = dot(l_ref[j], g, 0, 0)
        gj_ref[j] = g
        oj_ref[j] = one.astype(BF16)
        put_rows(x_ref, at, one)
    to_parts(x_ref, o_ref)


def grad_one_columns(core, own, other, left_blocks):
    by_j = jax.ShapeDtypeStruct((LJ, A, D), BF16)
    return pl.pallas_call(
        one_kernel,
        in_specs=[SMEM] + [VMEM] * 3,
        out_specs=[VMEM] * 3,
        out_shape=[PARTS, by_j, by_j],
        scratch_shapes=[COLUMNS],
        compiler_params=params(18),
        cost_estimate=cost(),
        name="grad_one_columns",
    )(core, own, other, left_blocks)


def weight_kernel(core_ref, own_ref, other_ref, oj_ref, t_ref, mine_ref, theirs_ref, x_ref):
    core = core_ref[0]
    load_columns(core, own_ref, other_ref, x_ref)
    for j in range(LJ):
        t_ref[pl.ds(j * A, A), :] = get_rows(x_ref, pl.ds(j, A, stride=LJ)).astype(BF16)
    for half, out in ((1 - core, theirs_ref), (core, mine_ref)):
        t = t_ref[:, pl.ds(pl.multiple_of(half * 384, 128), 384)]
        part = dot(t, oj_ref[...].reshape(A * LJ, D), 0, 0)
        for q in range(4):
            for k in range(6):
                piece = part[q * 96:(q + 1) * 96, k * 128:(k + 1) * 128]
                out[q, pl.ds(k * 96, 96), :] = piece.astype(out.dtype)


def weight_grad(core, own, other, by_j_one):
    half = (4, WR, 128)
    return pl.pallas_call(
        weight_kernel,
        in_specs=[SMEM] + [VMEM] * 3,
        out_specs=[VMEM] * 3,
        out_shape=[
            jax.ShapeDtypeStruct((A * LJ, D), BF16),
            jax.ShapeDtypeStruct(half, F32),
            jax.ShapeDtypeStruct(half, BF16),
        ],
        scratch_shapes=[COLUMNS],
        compiler_params=params(18),
        cost_estimate=cost(),
        name="weight_grad",
    )(core, own, other, by_j_one)


def two_kernel(t_ref, w_ref, l_ref, gj_ref, o_ref, lp_ref, x_ref, s_ref):
    @pl.loop(0, 4)
    def _(i):
        rows = pl.ds(i * 256, 256)
        s_ref[rows, :] = dot(t_ref[rows, :], w_ref[...], 1, 0).astype(BF16)

    for j in range(LJ):
        v = s_ref[pl.ds(j * A, A), :]
        lp_ref[j] = dot(gj_ref[j], v, 1, 1)
        put_rows(x_ref, pl.ds(j, A, stride=LJ), dot(l_ref[j], v, 1, 0))

    @pl.loop(0, NCHIP)
    def _(i):
        for c in range(2):
            for k in range(6):
                o_ref[i, c, pl.ds(k * 32, 32), :] = x_ref[k, pl.ds(i * 64 + c * 32, 32), :].astype(BF16)


def two_columns(by_j_token, in_weight, left_blocks, by_j_grad):
    return pl.pallas_call(
        two_kernel,
        in_specs=[VMEM] * 4,
        out_specs=[VMEM] * 2,
        out_shape=[
            jax.ShapeDtypeStruct((NCHIP, 2, 192, 128), BF16),
            jax.ShapeDtypeStruct((LJ, A, A), F32),
        ],
        scratch_shapes=[COLUMNS, pltpu.VMEM((A * LJ, D), BF16)],
        compiler_params=params(18),
        cost_estimate=cost(),
        name="two_columns",
    )(by_j_token, in_weight, left_blocks, by_j_grad)


def spread_kernel(x_index_ref, mine_ref, got_ref, own_ref, *send_refs):
    x = x_index_ref[0]
    for k in range(4):
        q = lax.rem(x + k, 4)
        out = own_ref if k == 0 else send_refs[k - 1]
        out[...] = (mine_ref[q] + got_ref[q].astype(F32)).astype(out.dtype)


def spread(x_index, mine, got):
    return pl.pallas_call(
        spread_kernel,
        in_specs=[SMEM] + [VMEM] * 2,
        out_specs=[VMEM] * 4,
        out_shape=[jax.ShapeDtypeStruct((WR, 128), F32)] + [jax.ShapeDtypeStruct((WR, 128), BF16)] * 3,
        compiler_params=params(8),
        cost_estimate=cost(),
        name="spread",
    )(x_index, mine, got)


def join_two_kernel(core_ref, own_ref, other_ref, sum_ref, a_ref, b_ref, c_ref, o_ref, w_ref):
    core = core_ref[0]
    w = (sum_ref[...] + a_ref[...].astype(F32)) + (b_ref[...].astype(F32) + c_ref[...].astype(F32))
    w_ref[...] = w.astype(BF16)
    mine = pl.ds(pl.multiple_of(core * 192, 16), 192)
    theirs = pl.ds(pl.multiple_of((1 - core) * 192, 16), 192)

    @pl.loop(0, NCHIP)
    def _(i):
        o_ref[i, mine, :] = own_ref[i, core]
        o_ref[i, theirs, :] = other_ref[i, core]

    for i in range(NCHIP):
        chunk = w_ref[pl.ds(i * WCH, WCH), :] if i < WR // WCH else jnp.zeros((WCH, 128), BF16)
        o_ref[i, pl.ds(384, WCH), :] = chunk


def join_two(core, own, other, total, got):
    return pl.pallas_call(
        join_two_kernel,
        in_specs=[SMEM] + [VMEM] * 6,
        out_specs=VMEM,
        out_shape=TWO,
        scratch_shapes=[pltpu.VMEM((WR, 128), BF16)],
        compiler_params=params(14),
        cost_estimate=cost(),
        name="join_two",
    )(core, own, other, total, *got)


def weight_sum_kernel(p_ref, o_ref):
    total = p_ref[0].astype(F32)
    for i in range(1, NCHIP):
        total = total + p_ref[i].astype(F32)
    o_ref[...] = total


def weight_sum(two_parts):
    return pl.pallas_call(
        weight_sum_kernel,
        grid=(1,),
        in_specs=[pl.BlockSpec((NCHIP, WCH, 128), lambda i: (0, 384 // WCH, 0))],
        out_specs=pl.BlockSpec((WCH, 128), lambda i: (0, 0)),
        out_shape=jax.ShapeDtypeStruct((WCH, 128), F32),
        compiler_params=params(6),
        cost_estimate=cost(),
        name="weight_sum",
    )(two_parts)


def blocks_kernel(x_index_ref, own_ref, a_ref, b_ref, c_ref, l_ref, r_ref):
    for k, ref in enumerate((own_ref, a_ref, b_ref, c_ref)):
        q = lax.rem(x_index_ref[0] + 4 - k, 4)
        for h in range(2):
            l_ref[q * 2 + h] = ref[pl.ds(h * A, A), :]
            r_ref[q, :, pl.ds(h * 128, 128)] = ref[pl.ds(2 * A + h * B, B), :]


def place_blocks(x_index, pieces):
    return pl.pallas_call(
        blocks_kernel,
        in_specs=[SMEM] + [VMEM] * 4,
        out_specs=[VMEM] * 2,
        out_shape=[jax.ShapeDtypeStruct((LJ, A, A), BF16), jax.ShapeDtypeStruct((LA, B, B), BF16)],
        compiler_params=params(6),
        cost_estimate=cost(),
        name="place_blocks",
    )(x_index, *pieces)


def place_kernel(at_ref, own_ref, other_ref, o_ref):
    x, core = at_ref[0], at_ref[1]
    for half, ref in ((core, own_ref), (1 - core, other_ref)):
        for kx in range(4):
            q = lax.rem(x + 4 - kx, 4)
            rows = pl.ds(pl.multiple_of(half * 384 + q * 96, 96), 96)
            for k in range(6):
                o_ref[rows, pl.ds(k * 128, 128)] = ref[kx, pl.ds(k * 96, 96), :]


def place_weight(at, own, other):
    return pl.pallas_call(
        place_kernel,
        in_specs=[SMEM] + [VMEM] * 2,
        out_specs=VMEM,
        out_shape=jax.ShapeDtypeStruct((D, D), BF16),
        compiler_params=params(6),
        cost_estimate=cost(),
        name="place_weight",
    )(at, own, other)


def join_kernel(core_ref, own_ref, other_ref, o_ref):
    core = core_ref[0]

    @pl.loop(0, NCHIP)
    def _(i):
        o_ref[i, core] = own_ref[i, core]
        o_ref[i, 1 - core] = other_ref[i, core]


def join_cores(core, own, other):
    return pl.pallas_call(
        join_kernel,
        in_specs=[SMEM] + [VMEM] * 2,
        out_specs=VMEM,
        out_shape=PARTS,
        compiler_params=params(10),
        cost_estimate=cost(),
        name="join_cores",
    )(core, own, other)


def right_kernel(x_index_ref, parts_ref, p_ref, l_ref, g_ref, own_ref, a_ref, b_ref, c_ref, x_ref):
    x = x_index_ref[0]

    @pl.loop(0, NCHIP)
    def _(i):
        x_ref[pl.ds(i * 2, 2)] = parts_ref[i].astype(F32)

    for k, out in enumerate((own_ref, a_ref, b_ref, c_ref)):
        a = lax.rem(x + k, 4)
        g = x_ref[:, pl.ds(pl.multiple_of(a * LJ, LJ), LJ), :].reshape(B, D).astype(BF16)
        g_ref[a] = g
        part = dot(g, p_ref[a], 1, 1).astype(out.dtype)
        for h in range(2):
            out[pl.ds(h * A, A), :] = l_ref[a * 2 + h].astype(out.dtype)
            out[pl.ds(2 * A + h * B, B), :] = part[:, h * 128:(h + 1) * 128]


def block_grads(x_index, one_parts, projected, left_part):
    rows = 2 * A + 2 * B
    return pl.pallas_call(
        right_kernel,
        in_specs=[SMEM] + [VMEM] * 3,
        out_specs=[VMEM] * 5,
        out_shape=[jax.ShapeDtypeStruct((LA, B, D), BF16), jax.ShapeDtypeStruct((rows, 128), F32)]
        + [jax.ShapeDtypeStruct((rows, 128), BF16)] * 3,
        scratch_shapes=[pltpu.VMEM((32, LA * LJ, D), F32)],
        compiler_params=params(16),
        cost_estimate=cost(),
        name="block_grads",
    )(x_index, one_parts, projected, left_part)


def back_kernel(g_ref, r_ref, w_ref, o_ref):
    proj = dot(r_ref[0], g_ref[0], 0, 0).astype(BF16)
    o_ref[0] = dot(proj, w_ref[...], 1, 1)


def back_projected(grad_one, right_blocks, in_weight):
    return pl.pallas_call(
        back_kernel,
        grid=(LA,),
        in_specs=[
            pl.BlockSpec((1, B, D), lambda a: (a, 0, 0)),
            pl.BlockSpec((1, B, B), lambda a: (a, 0, 0)),
            pl.BlockSpec((D, D), lambda a: (0, 0)),
        ],
        out_specs=pl.BlockSpec((1, B, D), lambda a: (a, 0, 0)),
        out_shape=jax.ShapeDtypeStruct((LA, B, D), F32),
        compiler_params=params(12),
        cost_estimate=cost(),
        name="back_projected",
    )(grad_one, right_blocks, in_weight)


def end_kernel(parts_ref, t_ref, g_ref, b_ref, m_ref, o_ref):
    for i in range(4):
        rows = pl.ds(i * 16, 16)
        two = parts_ref[i, pl.ds(0, 384), :].astype(F32)
        for a in range(LA):
            s = jnp.concatenate(
                [
                    jnp.concatenate([two[r + a * LJ:r + (a + 1) * LJ] for r in (k * 32, 192 + k * 32)], axis=0)
                    for k in range(6)
                ],
                axis=1,
            )
            m_ref[a, rows, :] = (s * t_ref[a, rows, :].astype(F32)).astype(BF16)
            o_ref[a, rows, :] = (g_ref[a, rows, :].astype(F32) * s + b_ref[a, rows, :]).astype(BF16)


def end(two_parts, tokens, grad_out, back_proj):
    rows = pl.BlockSpec((LA, 64, D), lambda i: (0, i, 0))
    out = jax.ShapeDtypeStruct((LA, B, D), BF16)
    return pl.pallas_call(
        end_kernel,
        grid=(4,),
        in_specs=[pl.BlockSpec((4, TWO.shape[1], 128), lambda i: (i, 0, 0)), rows, rows, rows],
        out_specs=[rows, rows],
        out_shape=[out, out],
        compiler_params=params(14),
        name="end",
    )(two_parts, tokens, grad_out, back_proj)


def exchange(v):
    return lax.all_to_all(v, CHIPS, split_axis=0, concat_axis=0, tiled=True)


def swap(v):
    return lax.ppermute(v, "c", [(0, 1), (1, 0)])


def send(v, axis, k):
    n = SIZES[axis]
    return lax.ppermute(v, axis, [(i, (i + k) % n) for i in range(n)])


def along(axis, pieces):
    return [send(v, axis, k + 1) for k, v in enumerate(pieces)]


def gather_from(v, axis):
    return jnp.stack([v] + along(axis, [v] * (SIZES[axis] - 1)))


def place_of(*axes):
    return jnp.stack([lax.axis_index(axis).astype(jnp.int32) for axis in axes])


def on_device(tokens, grad_out, right_blocks, left_blocks, in_weight):
    tokens, grad_out = tokens[0], grad_out[0]
    core, x_index = place_of("c"), place_of("x")

    grad_parts = exchange(grad_two_parts(tokens, grad_out))

    token_split, projected = front(tokens, right_blocks, in_weight)
    token_split, projected, grad_parts = lax.optimization_barrier((token_split, projected, grad_parts))
    token_parts = exchange(token_split)

    one_out, grad_j, one_j = grad_one_columns(core, grad_parts, swap(grad_parts), left_blocks)
    one_split = join_cores(core, one_out, swap(one_out))
    one_split, grad_j, one_j, token_parts = lax.optimization_barrier((one_split, grad_j, one_j, token_parts))
    one_parts = exchange(one_split)

    by_j_token, weight_mine, weight_theirs = weight_grad(core, token_parts, swap(token_parts), one_j)
    two_out, left_part = two_columns(by_j_token, in_weight, left_blocks, grad_j)
    total, *away = spread(x_index, weight_mine, swap(weight_theirs))
    two_split = join_two(core, two_out, swap(two_out), total, along("x", away))
    two_split, left_part, one_parts = lax.optimization_barrier((two_split, left_part, one_parts))
    two_parts = exchange(two_split)

    grad_one, blocks, *away = block_grads(x_index, one_parts, projected, left_part)
    got = along("x", away)
    blocks = (blocks + got[0].astype(F32)) + (got[1].astype(F32) + got[2].astype(F32))
    back_proj = back_projected(grad_one, right_blocks, in_weight)
    blocks = (blocks + send(blocks, "zl", 1)).astype(BF16)
    blocks, back_proj, two_parts = lax.optimization_barrier((blocks, back_proj, two_parts))

    weight = weight_sum(two_parts)
    weight = (weight + send(weight, "zl", 1)).astype(BF16)
    weight = exchange(jnp.broadcast_to(weight[None], (NCHIP, WCH, 128)))[:WR // WCH].reshape(WR, 128)
    grad_left, grad_right = place_blocks(x_index, [blocks] + along("x", [blocks] * 3))
    mixed, grad_tokens = end(two_parts, tokens, grad_out, back_proj)
    weight, grad_left, grad_right, mixed, grad_tokens = lax.optimization_barrier(
        (weight, grad_left, grad_right, mixed, grad_tokens)
    )
    weight = gather_from(weight, "x")
    grad_weight = place_weight(place_of("x", "c"), weight, swap(weight))
    return mixed[None], grad_tokens[None], grad_left, grad_right, grad_weight


def solution(mesh):
    fine = Mesh(mesh.devices.reshape(2, 4, 4, 4, 2), ("zl", "x", "zh", "y", "c"))
    dp, seq = ("zl", "x"), ("zh", "y", "c")
    rows = P(dp, seq, None, None)
    blocks = P(seq, None, None)
    return jax.shard_map(
        on_device,
        mesh=fine,
        in_specs=(rows, rows, blocks, blocks, P()),
        out_specs=(rows, rows, blocks, blocks, P()),
        check_vma=False,
    )
```

profile of v0, /device:TPU:1, one launch (start us, length us, event | category | flops | bytes accessed | tf_op | source)
XLA Modules:
  0.0 241.1 jit_solution(506907644282945112)
XLA Ops:
  0.6 4.0 %grad_two.1 = bf16[16,2,32,768]{3,2,1,0:T(8,128)(2,1)} custom-call(bf16[4,256,768]{2,1,0:T(8,128)(2,1)} %bitcast.11, bf16[4,256,768]{2,1,0:T(8,128)(2,1)} %bitcast.14), custom_call_target="tpu_custom_call" | custom-call | tf_op jit(solution)/shard_map/grad_two/pallas_call | solution.py:44
  4.7 12.1 %all-to-all-start = ((bf16[16,2,32,768]{3,2,1,0:T(8,128)(2,1)}), bf16[16,2,32,768]{3,2,1,0:T(8,128)(2,1)}, u32[]{:S(2)}, u32[]{:S(2)}) async-start(bf16[16,2,32,768]{3,2,1,0:T(8,128)(2,1)} %grad_two.1), calls=%async_computation | async-start | bytes 3145728 | tf_op jit(solution)/shard_map/all_to_all | solution.py:416
  16.8 2.0 front.1
  21.1 31.5 %all-to-all-done.own_ref = bf16[16,2,32,768]{3,2,1,0:T(8,128)(2,1)} async-done(((bf16[16,2,32,768]{3,2,1,0:T(8,128)(2,1)}), bf16[16,2,32,768]{3,2,1,0:T(8,128)(2,1)}, u32[]{:S(2)}, u32[]{:S(2)}) %all-to-all-start) | async-done | bytes 1572896 | tf_op jit(solution)/shard_map/all_to_all | solution.py:416
  52.6 4.3 %collective-permute-start = (bf16[16,2,32,768]{3,2,1,0:T(8,128)(2,1)}, bf16[16,2,32,768]{3,2,1,0:T(8,128)(2,1)}, u32[]{:S(2)}, u32[]{:S(2)}) collective-permute-start(bf16[16,2,32,768]{3,2,1,0:T(8,128)(2,1)} %all-to-all-done.own_ref), channel_id=1, source_target_pairs={{0,1},{1,0},{2,3},{3,2},{4,5},{5,4},{6,7},{7,6},{8,9},{9,8},{10,11... | collective-permute-start | bytes 4718600 | tf_op jit(solution)/shard_map/ppermute | solution.py:420
  57.0 5.4 %all-to-all-start.1 = ((bf16[16,2,32,768]{3,2,1,0:T(8,128)(2,1)}), bf16[16,2,32,768]{3,2,1,0:T(8,128)(2,1)}, u32[]{:S(2)}, u32[]{:S(2)}) async-start(bf16[16,2,32,768]{3,2,1,0:T(8,128)(2,1)} %copy-done.12), calls=%async_computation.1 | async-start | bytes 3145728 | tf_op jit(solution)/shard_map/all_to_all | solution.py:416
  62.4 3.8 %grad_one_columns.1 = (bf16[16,2,32,768]{3,2,1,0:T(8,128)(2,1)S(1)}, bf16[8,128,768]{2,1,0:T(8,128)(2,1)S(1)}, bf16[8,128,768]{2,1,0:T(8,128)(2,1)S(1)}) custom-call(s32[1]{0:T(128)} %bitcast.1.core_ref, bf16[16,2,32,768]{3,2,1,0:T(8,128)(2,1)} %all-to-all-done.own_ref, bf16[16,2,32,768]{3,2,1,0:T(8,128)(2,1)} %collective-permute-done.other_ref, ...), custom_call_target="tpu_custom_call" | custom-call | flops 1000 | bytes 1000 | tf_op jit(solution)/shard_map/grad_one_columns/pallas_call | solution.py:120
  67.4 1.2 copy-done.13
  69.1 3.0 %collective-permute-done.1.other_ref = bf16[16,2,32,768]{3,2,1,0:T(8,128)(2,1)S(1)} collective-permute-done((bf16[16,2,32,768]{3,2,1,0:T(8,128)(2,1)S(1)}, bf16[16,2,32,768]{3,2,1,0:T(8,128)(2,1)S(1)}, u32[]{:S(2)}, u32[]{:S(2)}) %collective-permute-start.1) | collective-permute-done | bytes 1572896 | tf_op jit(solution)/shard_map/ppermute | solution.py:420
  73.4 23.8 %all-to-all-done.1.own_ref = bf16[16,2,32,768]{3,2,1,0:T(8,128)(2,1)} async-done(((bf16[16,2,32,768]{3,2,1,0:T(8,128)(2,1)}), bf16[16,2,32,768]{3,2,1,0:T(8,128)(2,1)}, u32[]{:S(2)}, u32[]{:S(2)}) %all-to-all-start.1) | async-done | bytes 1572896 | tf_op jit(solution)/shard_map/all_to_all | solution.py:416
  97.2 1.9 collective-permute-start.2
  99.1 8.2 %all-to-all-start.2 = ((bf16[16,2,32,768]{3,2,1,0:T(8,128)(2,1)}), bf16[16,2,32,768]{3,2,1,0:T(8,128)(2,1)}, u32[]{:S(2)}, u32[]{:S(2)}) async-start(bf16[16,2,32,768]{3,2,1,0:T(8,128)(2,1)} %copy-done.6), calls=%async_computation.2 | async-start | bytes 3145728 | tf_op jit(solution)/shard_map/all_to_all | solution.py:416
  107.3 1.4 copy-done.11
  108.7 4.9 %weight_grad.1 = (bf16[1024,768]{1,0:T(8,128)(2,1)S(1)}, f32[4,576,128]{2,1,0:T(8,128)S(1)}, bf16[4,576,128]{2,1,0:T(8,128)(2,1)}) custom-call(s32[1]{0:T(128)} %bitcast.1.core_ref, bf16[16,2,32,768]{3,2,1,0:T(8,128)(2,1)} %all-to-all-done.1.own_ref, bf16[16,2,32,768]{3,2,1,0:T(8,128)(2,1)} %collective-permute-done.2.other_ref, ...), custom_call_target="tpu_custom_call" | custom-call | flops 1000 | bytes 1000 | tf_op jit(solution)/shard_map/weight_grad/pallas_call | solution.py:148
  113.6 4.4 %two_columns.1 = (bf16[16,2,192,128]{3,2,1,0:T(8,128)(2,1)}, f32[8,128,128]{2,1,0:T(8,128)S(1)}) custom-call(bf16[1024,768]{1,0:T(8,128)(2,1)S(1)} %get-tuple-element.55.t_ref, bf16[768,768]{1,0:T(8,128)(2,1)S(1)} %copy-done.3, bf16[8,128,128]{2,1,0:T(8,128)(2,1)S(1)} %copy-done.19, bf16[8,128,768]{2,1,0:T(8,128)(2,1)S(1)} %copy-done.14), custom_call_target="tpu_custom_call" | custom-call | flops 1000 | bytes 1000 | tf_op jit(solution)/shard_map/two_columns/pallas_call | solution.py:183
  119.2 4.1 %collective-permute-done.4.got_ref = bf16[4,576,128]{2,1,0:T(8,128)(2,1)} collective-permute-done((bf16[4,576,128]{2,1,0:T(8,128)(2,1)}, bf16[4,576,128]{2,1,0:T(8,128)(2,1)}, u32[]{:S(2)}, u32[]{:S(2)}) %collective-permute-start.4) | collective-permute-done | bytes 589856 | tf_op jit(solution)/shard_map/ppermute | solution.py:420
  123.3 1.3 copy-done.18
  125.8 1.3 collective-permute-start.5
  127.1 2.5 %collective-permute-start.6 = (bf16[576,128]{1,0:T(8,128)(2,1)S(1)}, bf16[576,128]{1,0:T(8,128)(2,1)S(1)}, u32[]{:S(2)}, u32[]{:S(2)}) collective-permute-start(bf16[576,128]{1,0:T(8,128)(2,1)S(1)} %get-tuple-element.62), channel_id=1, source_target_pairs={{0,64},{32,96},{64,0},{96,32},{1,65},{33,97},{65,1},{97,33},{2,66}... | collective-permute-start | bytes 442376 | tf_op jit(solution)/shard_map/ppermute | solution.py:425
  130.7 1.7 collective-permute-done.5.a_ref
  132.3 4.0 %collective-permute-done.6.b_ref = bf16[576,128]{1,0:T(8,128)(2,1)S(1)} collective-permute-done((bf16[576,128]{1,0:T(8,128)(2,1)S(1)}, bf16[576,128]{1,0:T(8,128)(2,1)S(1)}, u32[]{:S(2)}, u32[]{:S(2)}) %collective-permute-start.6) | collective-permute-done | bytes 147488 | tf_op jit(solution)/shard_map/ppermute | solution.py:425
  136.4 1.6 join_two.1
  138.0 1.2 copy-done.5
  139.5 9.2 %all-to-all-start.3 = ((bf16[16,432,128]{2,1,0:T(8,128)(2,1)}), bf16[16,432,128]{2,1,0:T(8,128)(2,1)S(1)}, u32[]{:S(2)}, u32[]{:S(2)}) async-start(bf16[16,432,128]{2,1,0:T(8,128)(2,1)} %copy-done.5), calls=%async_computation.3 | async-start | bytes 3538944 | tf_op jit(solution)/shard_map/all_to_all | solution.py:416
  148.7 1.4 copy-done.16
  151.1 2.4 block_grads.1
  153.5 2.3 collective-permute-start.10
  155.9 1.4 collective-permute-start.9
  157.2 1.3 collective-permute-done.10
  158.5 5.5 %collective-permute-done.8 = bf16[768,128]{1,0:T(8,128)(2,1)S(1)} collective-permute-done((bf16[768,128]{1,0:T(8,128)(2,1)S(1)}, bf16[768,128]{1,0:T(8,128)(2,1)S(1)}, u32[]{:S(2)}, u32[]{:S(2)}) %collective-permute-start.8) | collective-permute-done | bytes 196640 | tf_op jit(solution)/shard_map/ppermute | solution.py:425
  164.1 9.7 %collective-permute-start.11 = (f32[768,128]{1,0:T(8,128)S(1)}, f32[768,128]{1,0:T(8,128)S(1)}, u32[]{:S(2)}, u32[]{:S(2)}) collective-permute-start(f32[768,128]{1,0:T(8,128)S(1)} %add_add_fusion), channel_id=1, source_target_pairs={{0,128},{128,0},{1,129},{129,1},{2,130},{130,2},{3,131},{131,3},{4... | collective-permute-start | bytes 1179656 | tf_op jit(solution)/shard_map/ppermute | solution.py:425
  173.9 2.6 %back_projected.1.b_ref = f32[4,256,768]{2,1,0:T(8,128)S(1)} custom-call(bf16[4,256,768]{2,1,0:T(8,128)(2,1)S(1)} %get-tuple-element.73.g_ref, bf16[4,256,256]{2,1,0:T(8,128)(2,1)S(1)} %copy-done.9, bf16[768,768]{1,0:T(8,128)(2,1)S(1)} %copy-done.4), custom_call_target="tpu_custom_call" | custom-call | flops 1000 | bytes 1000 | tf_op jit(solution)/shard_map/back_projected/pallas_call | solution.py:369
  176.5 1.7 copy-done.1
  178.2 21.9 %collective-permute-done.11 = f32[768,128]{1,0:T(8,128)S(1)} collective-permute-done((f32[768,128]{1,0:T(8,128)S(1)}, f32[768,128]{1,0:T(8,128)S(1)}, u32[]{:S(2)}, u32[]{:S(2)}) %collective-permute-start.11) | collective-permute-done | bytes 393248 | tf_op jit(solution)/shard_map/ppermute | solution.py:425
  200.3 2.7 %collective-permute-done.12 = f32[48,128]{1,0:T(8,128)S(1)} collective-permute-done((f32[48,128]{1,0:T(8,128)S(1)}, f32[48,128]{1,0:T(8,128)S(1)}, u32[]{:S(2)}, u32[]{:S(2)}) %collective-permute-start.12) | collective-permute-done | bytes 24608 | tf_op jit(solution)/shard_map/ppermute | solution.py:425
  203.6 6.5 %all-to-all-start.4 = ((bf16[16,48,128]{2,1,0:T(8,128)(2,1)}), bf16[16,48,128]{2,1,0:T(8,128)(2,1)}, u32[]{:S(2)}, u32[]{:S(2)}) async-start(bf16[16,48,128]{2,1,0:T(8,128)(2,1)} %broadcast_in_dim.12), calls=%async_computation.4 | async-start | bytes 393216 | tf_op jit(solution)/shard_map/all_to_all | solution.py:416
  210.1 1.9 collective-permute-start.13
  212.1 2.4 %collective-permute-start.14 = (bf16[768,128]{1,0:T(8,128)(2,1)S(1)}, bf16[768,128]{1,0:T(8,128)(2,1)S(1)}, u32[]{:S(2)}, u32[]{:S(2)}) collective-permute-start(bf16[768,128]{1,0:T(8,128)(2,1)S(1)} %add_convert_fusion.own_ref), channel_id=1, source_target_pairs={{0,64},{32,96},{64,0},{96,32},{1,65},{33,97},{65,1},{97,33},{2,66}... | collective-permute-start | bytes 589832 | tf_op jit(solution)/shard_map/ppermute | solution.py:425
  214.6 1.9 copy-done.2
  216.5 1.4 copy-done.7
  217.9 2.7 %end.1 = (bf16[4,256,768]{2,1,0:T(8,128)(2,1)}, bf16[4,256,768]{2,1,0:T(8,128)(2,1)}) custom-call(bf16[16,432,128]{2,1,0:T(8,128)(2,1)S(1)} %all-to-all-done.3.p_ref.parts_ref, bf16[4,256,768]{2,1,0:T(8,128)(2,1)S(1)} %bitcast.13, bf16[4,256,768]{2,1,0:T(8,128)(2,1)S(1)} %bitcast.15, f32[4,256,768]{2,1,0:T(8,128)S(1)} %copy-done.2), custom_call_target="tpu_custom_call" | custom-call | tf_op jit(solution)/shard_map/end/pallas_call | solution.py:404
  220.6 1.2 collective-permute-done.14.b_ref
  223.7 3.2 %collective-permute-start.18 = (bf16[576,128]{1,0:T(8,128)(2,1)S(1)}, bf16[576,128]{1,0:T(8,128)(2,1)S(1)}, u32[]{:S(2)}, u32[]{:S(2)}) collective-permute-start(bf16[576,128]{1,0:T(8,128)(2,1)S(1)} %bitcast.16), channel_id=1, source_target_pairs={{0,96},{32,0},{64,32},{96,64},{1,97},{33,1},{65,33},{97,65},{2,98}... | collective-permute-start | bytes 442376 | tf_op jit(solution)/shard_map/ppermute | solution.py:425
  226.9 1.3 collective-permute-start.17
  229.0 6.9 %collective-permute-done.16 = bf16[576,128]{1,0:T(8,128)(2,1)S(1)} collective-permute-done((bf16[576,128]{1,0:T(8,128)(2,1)S(1)}, bf16[576,128]{1,0:T(8,128)(2,1)S(1)}, u32[]{:S(2)}, u32[]{:S(2)}) %collective-permute-start.16) | collective-permute-done | bytes 147488 | tf_op jit(solution)/shard_map/ppermute | solution.py:425
  236.0 1.7 collective-permute-start.19
  237.8 1.6 collective-permute-done.19.other_ref
  239.4 1.8 place_weight.1
  (67 shorter events, 14.1 us)
Async XLA Ops:
  0.6 16.1 %copy-start.8 = (bf16[4,256,256]{2,1,0:T(8,128)(2,1)S(1)}, bf16[4,256,256]{2,1,0:T(8,128)(2,1)}, u32[]{:S(2)}) copy-start(bf16[4,256,256]{2,1,0:T(8,128)(2,1)} %r_ref.3) | copy-start | bytes 1572868
  4.7 12.1 %copy-start = (bf16[1,4,256,768]{3,2,1,0:T(8,128)(2,1)S(1)}, bf16[1,4,256,768]{3,2,1,0:T(8,128)(2,1)}, u32[]{:S(2)}) copy-start(bf16[1,4,256,768]{3,2,1,0:T(8,128)(2,1)} %param.5) | copy-start | bytes 4718596
  4.7 12.1 %copy-start.3 = (bf16[768,768]{1,0:T(8,128)(2,1)S(1)}, bf16[768,768]{1,0:T(8,128)(2,1)}, u32[]{:S(2)}) copy-start(bf16[768,768]{1,0:T(8,128)(2,1)} %w_ref.5) | copy-start | bytes 3538948
  4.7 48.0 %all-to-all-start = ((bf16[16,2,32,768]{3,2,1,0:T(8,128)(2,1)}), bf16[16,2,32,768]{3,2,1,0:T(8,128)(2,1)}, u32[]{:S(2)}, u32[]{:S(2)}) async-start(bf16[16,2,32,768]{3,2,1,0:T(8,128)(2,1)} %grad_two.1), calls=%async_computation | async-start | bytes 3145728 | tf_op jit(solution)/shard_map/all_to_all | solution.py:416
  18.8 1.1 copy-start.12
  19.9 1.2 copy-start.15
  52.6 9.8 %copy-start.19 = (bf16[8,128,128]{2,1,0:T(8,128)(2,1)S(1)}, bf16[8,128,128]{2,1,0:T(8,128)(2,1)}, u32[]{:S(2)}) copy-start(bf16[8,128,128]{2,1,0:T(8,128)(2,1)} %l_ref.3) | copy-start | bytes 786436
  52.6 9.8 %collective-permute-start = (bf16[16,2,32,768]{3,2,1,0:T(8,128)(2,1)}, bf16[16,2,32,768]{3,2,1,0:T(8,128)(2,1)}, u32[]{:S(2)}, u32[]{:S(2)}) collective-permute-start(bf16[16,2,32,768]{3,2,1,0:T(8,128)(2,1)} %all-to-all-done.own_ref), channel_id=1, source_target_pairs={{0,1},{1,0},{2,3},{3,2},{4,5},{5,4},{6,7},{7,6},{8,9},{9,8},{10,11... | collective-permute-start | bytes 4718600 | tf_op jit(solution)/shard_map/ppermute | solution.py:420
  57.0 40.2 %all-to-all-start.1 = ((bf16[16,2,32,768]{3,2,1,0:T(8,128)(2,1)}), bf16[16,2,32,768]{3,2,1,0:T(8,128)(2,1)}, u32[]{:S(2)}, u32[]{:S(2)}) async-start(bf16[16,2,32,768]{3,2,1,0:T(8,128)(2,1)} %copy-done.12), calls=%async_computation.1 | async-start | bytes 3145728 | tf_op jit(solution)/shard_map/all_to_all | solution.py:416
  66.3 1.1 copy-start.10
  67.4 1.2 copy-start.13
  68.6 3.5 %collective-permute-start.1 = (bf16[16,2,32,768]{3,2,1,0:T(8,128)(2,1)S(1)}, bf16[16,2,32,768]{3,2,1,0:T(8,128)(2,1)S(1)}, u32[]{:S(2)}, u32[]{:S(2)}) collective-permute-start(bf16[16,2,32,768]{3,2,1,0:T(8,128)(2,1)S(1)} %get-tuple-element.49.own_ref), channel_id=1, source_target_pairs={{0,1},{1,0},{2,3},{3,2},{4,5},{5,4},{6,7},{7,6},{8,9},{9,8},{10,11... | collective-permute-start | bytes 4718600 | tf_op jit(solution)/shard_map/ppermute | solution.py:420
  72.3 1.2 copy-start.6
  97.2 10.1 %collective-permute-start.2 = (bf16[16,2,32,768]{3,2,1,0:T(8,128)(2,1)}, bf16[16,2,32,768]{3,2,1,0:T(8,128)(2,1)}, u32[]{:S(2)}, u32[]{:S(2)}) collective-permute-start(bf16[16,2,32,768]{3,2,1,0:T(8,128)(2,1)} %all-to-all-done.1.own_ref), channel_id=1, source_target_pairs={{0,1},{1,0},{2,3},{3,2},{4,5},{5,4},{6,7},{7,6},{8,9},{9,8},{10,11... | collective-permute-start | bytes 4718600 | tf_op jit(solution)/shard_map/ppermute | solution.py:420
  99.1 40.4 %all-to-all-start.2 = ((bf16[16,2,32,768]{3,2,1,0:T(8,128)(2,1)}), bf16[16,2,32,768]{3,2,1,0:T(8,128)(2,1)}, u32[]{:S(2)}, u32[]{:S(2)}) async-start(bf16[16,2,32,768]{3,2,1,0:T(8,128)(2,1)} %copy-done.6), calls=%async_computation.2 | async-start | bytes 3145728 | tf_op jit(solution)/shard_map/all_to_all | solution.py:416
  107.3 1.4 copy-start.11
  108.7 4.9 %copy-start.14 = (bf16[8,128,768]{2,1,0:T(8,128)(2,1)S(1)}, bf16[8,128,768]{2,1,0:T(8,128)(2,1)}, u32[]{:S(2)}) copy-start(bf16[8,128,768]{2,1,0:T(8,128)(2,1)} %copy-done.13) | copy-start | bytes 4718596
  113.6 4.4 %copy-start.17 = (f32[4,576,128]{2,1,0:T(8,128)}, f32[4,576,128]{2,1,0:T(8,128)S(1)}, u32[]{:S(2)}) copy-start(f32[4,576,128]{2,1,0:T(8,128)S(1)} %get-tuple-element.58.mine_ref) | copy-start | bytes 3538948
  117.9 0.8 copy-start.20
  118.7 17.6 %collective-permute-start.3 = (bf16[16,2,192,128]{3,2,1,0:T(8,128)(2,1)}, bf16[16,2,192,128]{3,2,1,0:T(8,128)(2,1)S(1)}, u32[]{:S(2)}, u32[]{:S(2)}) collective-permute-start(bf16[16,2,192,128]{3,2,1,0:T(8,128)(2,1)} %get-tuple-element.57.own_ref), channel_id=1, source_target_pairs={{0,1},{1,0},{2,3},{3,2},{4,5},{5,4},{6,7},{7,6},{8,9},{9,8},{10,11... | collective-permute-start | bytes 4718600 | tf_op jit(solution)/shard_map/ppermute | solution.py:420
  119.0 4.3 %collective-permute-start.4 = (bf16[4,576,128]{2,1,0:T(8,128)(2,1)}, bf16[4,576,128]{2,1,0:T(8,128)(2,1)}, u32[]{:S(2)}, u32[]{:S(2)}) collective-permute-start(bf16[4,576,128]{2,1,0:T(8,128)(2,1)} %get-tuple-element.59), channel_id=1, source_target_pairs={{0,1},{1,0},{2,3},{3,2},{4,5},{5,4},{6,7},{7,6},{8,9},{9,8},{10,11... | collective-permute-start | bytes 1769480 | tf_op jit(solution)/shard_map/ppermute | solution.py:420
  123.3 1.3 copy-start.18
  125.8 6.5 %collective-permute-start.5 = (bf16[576,128]{1,0:T(8,128)(2,1)S(1)}, bf16[576,128]{1,0:T(8,128)(2,1)S(1)}, u32[]{:S(2)}, u32[]{:S(2)}) collective-permute-start(bf16[576,128]{1,0:T(8,128)(2,1)S(1)} %get-tuple-element.61), channel_id=1, source_target_pairs={{0,32},{32,64},{64,96},{96,0},{1,33},{33,65},{65,97},{97,1},{2,34}... | collective-permute-start | bytes 442376 | tf_op jit(solution)/shard_map/ppermute | solution.py:425
  127.1 9.3 %collective-permute-start.6 = (bf16[576,128]{1,0:T(8,128)(2,1)S(1)}, bf16[576,128]{1,0:T(8,128)(2,1)S(1)}, u32[]{:S(2)}, u32[]{:S(2)}) collective-permute-start(bf16[576,128]{1,0:T(8,128)(2,1)S(1)} %get-tuple-element.62), channel_id=1, source_target_pairs={{0,64},{32,96},{64,0},{96,32},{1,65},{33,97},{65,1},{97,33},{2,66}... | collective-permute-start | bytes 442376 | tf_op jit(solution)/shard_map/ppermute | solution.py:425
  129.5 6.9 %collective-permute-start.7 = (bf16[576,128]{1,0:T(8,128)(2,1)S(1)}, bf16[576,128]{1,0:T(8,128)(2,1)S(1)}, u32[]{:S(2)}, u32[]{:S(2)}) collective-permute-start(bf16[576,128]{1,0:T(8,128)(2,1)S(1)} %get-tuple-element.63), channel_id=1, source_target_pairs={{0,96},{32,0},{64,32},{96,64},{1,97},{33,1},{65,33},{97,65},{2,98}... | collective-permute-start | bytes 442376 | tf_op jit(solution)/shard_map/ppermute | solution.py:425
  138.0 1.2 copy-start.5
  139.5 60.6 %all-to-all-start.3 = ((bf16[16,432,128]{2,1,0:T(8,128)(2,1)}), bf16[16,432,128]{2,1,0:T(8,128)(2,1)S(1)}, u32[]{:S(2)}, u32[]{:S(2)}) async-start(bf16[16,432,128]{2,1,0:T(8,128)(2,1)} %copy-done.5), calls=%async_computation.3 | async-start | bytes 3538944 | tf_op jit(solution)/shard_map/all_to_all | solution.py:416
  148.7 1.4 copy-start.16
  150.1 1.0 copy-start.21
  151.1 22.7 %copy-start.9 = (bf16[4,256,256]{2,1,0:T(8,128)(2,1)S(1)}, bf16[4,256,256]{2,1,0:T(8,128)(2,1)}, u32[]{:S(2)}) copy-start(bf16[4,256,256]{2,1,0:T(8,128)(2,1)} %r_ref.3) | copy-start | bytes 1572868
  153.5 20.3 %copy-start.4 = (bf16[768,768]{1,0:T(8,128)(2,1)S(1)}, bf16[768,768]{1,0:T(8,128)(2,1)}, u32[]{:S(2)}) copy-start(bf16[768,768]{1,0:T(8,128)(2,1)} %w_ref.5) | copy-start | bytes 3538948
  153.5 5.0 %collective-permute-start.10 = (bf16[768,128]{1,0:T(8,128)(2,1)S(1)}, bf16[768,128]{1,0:T(8,128)(2,1)S(1)}, u32[]{:S(2)}, u32[]{:S(2)}) collective-permute-start(bf16[768,128]{1,0:T(8,128)(2,1)S(1)} %get-tuple-element.72), channel_id=1, source_target_pairs={{0,96},{32,0},{64,32},{96,64},{1,97},{33,1},{65,33},{97,65},{2,98}... | collective-permute-start | bytes 589832 | tf_op jit(solution)/shard_map/ppermute | solution.py:425
  155.9 8.1 %collective-permute-start.8 = (bf16[768,128]{1,0:T(8,128)(2,1)S(1)}, bf16[768,128]{1,0:T(8,128)(2,1)S(1)}, u32[]{:S(2)}, u32[]{:S(2)}) collective-permute-start(bf16[768,128]{1,0:T(8,128)(2,1)S(1)} %get-tuple-element.70), channel_id=1, source_target_pairs={{0,32},{32,64},{64,96},{96,0},{1,33},{33,65},{65,97},{97,1},{2,34}... | collective-permute-start | bytes 589832 | tf_op jit(solution)/shard_map/ppermute | solution.py:425
  155.9 8.1 %collective-permute-start.9 = (bf16[768,128]{1,0:T(8,128)(2,1)S(1)}, bf16[768,128]{1,0:T(8,128)(2,1)S(1)}, u32[]{:S(2)}, u32[]{:S(2)}) collective-permute-start(bf16[768,128]{1,0:T(8,128)(2,1)S(1)} %get-tuple-element.71), channel_id=1, source_target_pairs={{0,64},{32,96},{64,0},{96,32},{1,65},{33,97},{65,1},{97,33},{2,66}... | collective-permute-start | bytes 589832 | tf_op jit(solution)/shard_map/ppermute | solution.py:425
  164.1 36.0 %collective-permute-start.11 = (f32[768,128]{1,0:T(8,128)S(1)}, f32[768,128]{1,0:T(8,128)S(1)}, u32[]{:S(2)}, u32[]{:S(2)}) collective-permute-start(f32[768,128]{1,0:T(8,128)S(1)} %add_add_fusion), channel_id=1, source_target_pairs={{0,128},{128,0},{1,129},{129,1},{2,130},{130,2},{3,131},{131,3},{4... | collective-permute-start | bytes 1179656 | tf_op jit(solution)/shard_map/ppermute | solution.py:425
  176.5 1.7 copy-start.1
  200.2 2.8 %collective-permute-start.12 = (f32[48,128]{1,0:T(8,128)S(1)}, f32[48,128]{1,0:T(8,128)S(1)}, u32[]{:S(2)}, u32[]{:S(2)}) collective-permute-start(f32[48,128]{1,0:T(8,128)S(1)} %weight_sum.1), channel_id=1, source_target_pairs={{0,128},{128,0},{1,129},{129,1},{2,130},{130,2},{3,131},{131,3},{4... | collective-permute-start | bytes 73736 | tf_op jit(solution)/shard_map/ppermute | solution.py:425
  203.6 19.2 %all-to-all-start.4 = ((bf16[16,48,128]{2,1,0:T(8,128)(2,1)}), bf16[16,48,128]{2,1,0:T(8,128)(2,1)}, u32[]{:S(2)}, u32[]{:S(2)}) async-start(bf16[16,48,128]{2,1,0:T(8,128)(2,1)} %broadcast_in_dim.12), calls=%async_computation.4 | async-start | bytes 393216 | tf_op jit(solution)/shard_map/all_to_all | solution.py:416
  210.1 10.4 %collective-permute-start.13 = (bf16[768,128]{1,0:T(8,128)(2,1)S(1)}, bf16[768,128]{1,0:T(8,128)(2,1)S(1)}, u32[]{:S(2)}, u32[]{:S(2)}) collective-permute-start(bf16[768,128]{1,0:T(8,128)(2,1)S(1)} %add_convert_fusion.own_ref), channel_id=1, source_target_pairs={{0,32},{32,64},{64,96},{96,0},{1,33},{33,65},{65,97},{97,1},{2,34}... | collective-permute-start | bytes 589832 | tf_op jit(solution)/shard_map/ppermute | solution.py:425
  212.1 9.7 %collective-permute-start.14 = (bf16[768,128]{1,0:T(8,128)(2,1)S(1)}, bf16[768,128]{1,0:T(8,128)(2,1)S(1)}, u32[]{:S(2)}, u32[]{:S(2)}) collective-permute-start(bf16[768,128]{1,0:T(8,128)(2,1)S(1)} %add_convert_fusion.own_ref), channel_id=1, source_target_pairs={{0,64},{32,96},{64,0},{96,32},{1,65},{33,97},{65,1},{97,33},{2,66}... | collective-permute-start | bytes 589832 | tf_op jit(solution)/shard_map/ppermute | solution.py:425
  214.5 7.3 %collective-permute-start.15 = (bf16[768,128]{1,0:T(8,128)(2,1)S(1)}, bf16[768,128]{1,0:T(8,128)(2,1)S(1)}, u32[]{:S(2)}, u32[]{:S(2)}) collective-permute-start(bf16[768,128]{1,0:T(8,128)(2,1)S(1)} %add_convert_fusion.own_ref), channel_id=1, source_target_pairs={{0,96},{32,0},{64,32},{96,64},{1,97},{33,1},{65,33},{97,65},{2,98}... | collective-permute-start | bytes 589832 | tf_op jit(solution)/shard_map/ppermute | solution.py:425
  214.6 1.9 copy-start.2
  216.5 1.4 copy-start.7
  223.7 5.3 %collective-permute-start.18 = (bf16[576,128]{1,0:T(8,128)(2,1)S(1)}, bf16[576,128]{1,0:T(8,128)(2,1)S(1)}, u32[]{:S(2)}, u32[]{:S(2)}) collective-permute-start(bf16[576,128]{1,0:T(8,128)(2,1)S(1)} %bitcast.16), channel_id=1, source_target_pairs={{0,96},{32,0},{64,32},{96,64},{1,97},{33,1},{65,33},{97,65},{2,98}... | collective-permute-start | bytes 442376 | tf_op jit(solution)/shard_map/ppermute | solution.py:425
  226.9 9.0 %collective-permute-start.16 = (bf16[576,128]{1,0:T(8,128)(2,1)S(1)}, bf16[576,128]{1,0:T(8,128)(2,1)S(1)}, u32[]{:S(2)}, u32[]{:S(2)}) collective-permute-start(bf16[576,128]{1,0:T(8,128)(2,1)S(1)} %bitcast.17), channel_id=1, source_target_pairs={{0,32},{32,64},{64,96},{96,0},{1,33},{33,65},{65,97},{97,1},{2,34}... | collective-permute-start | bytes 442376 | tf_op jit(solution)/shard_map/ppermute | solution.py:425
  226.9 9.0 %collective-permute-start.17 = (bf16[576,128]{1,0:T(8,128)(2,1)S(1)}, bf16[576,128]{1,0:T(8,128)(2,1)S(1)}, u32[]{:S(2)}, u32[]{:S(2)}) collective-permute-start(bf16[576,128]{1,0:T(8,128)(2,1)S(1)} %bitcast.18), channel_id=1, source_target_pairs={{0,64},{32,96},{64,0},{96,32},{1,65},{33,97},{65,1},{97,33},{2,66}... | collective-permute-start | bytes 442376 | tf_op jit(solution)/shard_map/ppermute | solution.py:425
  236.0 3.3 %collective-permute-start.19 = (bf16[4,576,128]{2,1,0:T(8,128)(2,1)S(1)}, bf16[4,576,128]{2,1,0:T(8,128)(2,1)S(1)}, u32[]{:S(2)}, u32[]{:S(2)}) collective-permute-start(bf16[4,576,128]{2,1,0:T(8,128)(2,1)S(1)} %pad_maximum_fusion.own_ref), channel_id=1, source_target_pairs={{0,1},{1,0},{2,3},{3,2},{4,5},{5,4},{6,7},{7,6},{8,9},{9,8},{10,11... | collective-permute-start | bytes 1769480 | tf_op jit(solution)/shard_map/ppermute | solution.py:420
where the time goes:
time: 242 us; the launch traced here: 241 us
  waiting for transfers between devices  110 us (45%)
  starting transfers between devices  77.4 us (32%)
  Pallas kernels  32.6 us (13%)
  local copies, waits for them, and re-layouts  19.6 us (8%)
    all_to_all x5, waiting for transfers between devices, exchange(): return lax.all_to_all(v, CHIPS, split_axis=0, concat_axis=0, tiled=True)  55.6 us
    ppermute x14, waiting for transfers between devices, send(): return lax.ppermute(v, axis, [(i, (i + k) % n) for i in range(n)])  46 us
    all_to_all x5, starting transfers between devices, exchange(): return lax.all_to_all(v, CHIPS, split_axis=0, concat_axis=0, tiled=True)  41.3 us
    ppermute x14, starting transfers between devices, send(): return lax.ppermute(v, axis, [(i, (i + k) % n) for i in range(n)])  27.3 us
    unnamed x44, local copies, waits for them, and re-layouts  18 us
    ppermute x6, starting transfers between devices, swap(): return lax.ppermute(v, 'c', [(0, 1), (1, 0)])  8.84 us
    ppermute x6, waiting for transfers between devices, swap(): return lax.ppermute(v, 'c', [(0, 1), (1, 0)])  8.68 us
    pallas_call x1, Pallas kernels, weight_grad(): pl.pallas_call(weight_kernel, in_specs=[SMEM] + [VMEM] * 3, out_specs=[VM...  4.88 us
  transfers between devices with their start and end apart: 25, of which 15 were waited for; matrix products, arithmetic and copies ran while one was open for 0% of the time, Pallas kernels for 11%

commit v1 on v0

--- a/solution.py
+++ b/solution.py
@@ -8,10 +8,12 @@
 F32 = jnp.float32
 BF16 = jnp.bfloat16
 CHIPS = ("zh", "y")
+DEVICES = ("zh", "y", "c")
 SIZES = {"zl": 2, "x": 4, "zh": 4, "y": 4, "c": 2}
 
-LA, LJ, NCHIP, A, B, D = 4, 8, 16, 128, 256, 768
-PARTS = jax.ShapeDtypeStruct((NCHIP, 2, LA * LJ, D), BF16)
+LA, LJ, NDEV, NCHIP, A, B, D = 4, 8, 32, 16, 128, 256, 768
+PARTS = jax.ShapeDtypeStruct((NDEV, LA * LJ, D), BF16)
+FIRST = jax.ShapeDtypeStruct((NDEV, 2, 2, 2 * LJ, D), BF16)
 WR, WCH = 576, 48
 TWO = jax.ShapeDtypeStruct((NCHIP, 384 + WCH, 128), BF16)
 VMEM = pl.BlockSpec(memory_space=pltpu.VMEM)
@@ -30,26 +32,49 @@
     return lax.dot_general(a, b, (((ca,), (cb,)), ((), ())), preferred_element_type=F32)
 
 
-def grad_two_kernel(t_ref, g_ref, o_ref):
-    for i in range(4):
-        rows = pl.ds(i * 16, 16)
-        v = t_ref[:, rows, :].astype(F32) * g_ref[:, rows, :].astype(F32)
-        v = v.reshape(LA, 2, LJ, D)
-        for core in range(2):
-            o_ref[i, core] = v[:, core].reshape(LA * LJ, D).astype(BF16)
-
-
-def grad_two_parts(tokens, grad_out):
-    rows = pl.BlockSpec((LA, 64, D), lambda i: (0, i, 0))
-    return pl.pallas_call(
-        grad_two_kernel,
-        grid=(4,),
-        in_specs=[rows, rows],
-        out_specs=pl.BlockSpec((4, 2, LA * LJ, D), lambda i: (i, 0, 0, 0)),
-        out_shape=PARTS,
+def first_kernel(t_ref, g_ref, r_ref, o_ref, x_ref):
+    for a in range(2):
+        t = t_ref[a]
+        x_ref[0, a] = t.astype(F32) * g_ref[a].astype(F32)
+        x_ref[1, a] = dot(r_ref[a], t, 1, 0)
+
+    @pl.loop(0, NDEV)
+    def _(i):
+        rows = pl.ds(pl.multiple_of(i * LJ, LJ), LJ)
+        for kind in range(2):
+            both = jnp.concatenate([x_ref[kind, a, rows, :] for a in range(2)], axis=0)
+            o_ref[i, 0, kind] = both.astype(BF16)
+
+
+def first_parts(tokens, grad_out, right_blocks):
+    rows = pl.BlockSpec((2, B, D), lambda p: (p, 0, 0))
+    return pl.pallas_call(
+        first_kernel,
+        grid=(2,),
+        in_specs=[rows, rows, pl.BlockSpec((2, B, B), lambda p: (p, 0, 0))],
+        out_specs=pl.BlockSpec((NDEV, 1, 2, 2 * LJ, D), lambda p: (0, p, 0, 0, 0)),
+        out_shape=FIRST,
+        scratch_shapes=[pltpu.VMEM((2, 2, B, D), F32)],
         compiler_params=params(60),
-        name="grad_two",
-    )(tokens, grad_out)
+        name="first_parts",
+    )(tokens, grad_out, right_blocks)
+
+
+def project_kernel(t_ref, w_ref, p_ref):
+    for a in range(LA):
+        p_ref[a] = dot(t_ref[a], w_ref[...], 1, 0).astype(BF16)
+
+
+def project(tokens, in_weight):
+    return pl.pallas_call(
+        project_kernel,
+        in_specs=[VMEM] * 2,
+        out_specs=VMEM,
+        out_shape=jax.ShapeDtypeStruct((LA, B, D), BF16),
+        compiler_params=params(14),
+        cost_estimate=cost(),
+        name="project",
+    )(tokens, in_weight)
 
 
 COLUMNS = pltpu.VMEM((6, A * LJ, 128), F32)
@@ -64,101 +89,74 @@
     return jnp.concatenate([x_ref[k, rows, :] for k in range(6)], axis=1)
 
 
-def to_parts(x_ref, o_ref):
-    @pl.loop(0, NCHIP)
-    def _(i):
-        for core in range(2):
-            o_ref[i, core] = get_rows(x_ref, pl.ds(i * 64 + core * 32, 32)).astype(BF16)
-
-
-def front_kernel(t_ref, r_ref, w_ref, o_ref, p_ref, x_ref):
-    for a in range(LA):
-        t = t_ref[a]
-        one = dot(r_ref[a], t, 1, 0)
-        x_ref[:, pl.ds(a * LJ, LJ), :] = one.reshape(32, LJ, D)
-        p_ref[a] = dot(t, w_ref[...], 1, 0).astype(BF16)
-
-    @pl.loop(0, NCHIP)
-    def _(i):
-        o_ref[i] = x_ref[pl.ds(i * 2, 2)].astype(BF16)
-
-
-def front(tokens, right_blocks, in_weight):
-    return pl.pallas_call(
-        front_kernel,
-        in_specs=[VMEM] * 3,
-        out_specs=[VMEM] * 2,
-        out_shape=[PARTS, jax.ShapeDtypeStruct((LA, B, D), BF16)],
-        scratch_shapes=[pltpu.VMEM((32, LA * LJ, D), F32)],
-        compiler_params=params(18),
-        cost_estimate=cost(),
-        name="front",
-    )(tokens, right_blocks, in_weight)
-
-
-def load_columns(core, own_ref, other_ref, x_ref):
-    @pl.loop(0, NCHIP)
-    def _(i):
-        put_rows(x_ref, pl.ds(i * 64 + core * 32, 32), own_ref[i, core].astype(F32))
-        put_rows(x_ref, pl.ds(i * 64 + (1 - core) * 32, 32), other_ref[i, core].astype(F32))
-
-
-def one_kernel(core_ref, own_ref, other_ref, l_ref, o_ref, gj_ref, oj_ref, x_ref):
-    load_columns(core_ref[0], own_ref, other_ref, x_ref)
+def load_columns(kind, parts_ref, x_ref):
+    @pl.loop(0, NDEV)
+    def _(i):
+        for p in range(2):
+            put_rows(x_ref, pl.ds(i * 32 + p * 16, 16), parts_ref[i, p, kind].astype(F32))
+
+
+def one_kernel(parts_ref, l_ref, o_ref, x_ref):
+    load_columns(0, parts_ref, x_ref)
     for j in range(LJ):
         at = pl.ds(j, A, stride=LJ)
         g = get_rows(x_ref, at).astype(BF16)
-        one = dot(l_ref[j], g, 0, 0)
-        gj_ref[j] = g
-        oj_ref[j] = one.astype(BF16)
-        put_rows(x_ref, at, one)
-    to_parts(x_ref, o_ref)
-
-
-def grad_one_columns(core, own, other, left_blocks):
-    by_j = jax.ShapeDtypeStruct((LJ, A, D), BF16)
+        put_rows(x_ref, at, dot(l_ref[j], g, 0, 0))
+
+    @pl.loop(0, NDEV)
+    def _(i):
+        o_ref[i] = get_rows(x_ref, pl.ds(i * 32, 32)).astype(BF16)
+
+
+def grad_one_columns(parts, left_blocks):
     return pl.pallas_call(
         one_kernel,
-        in_specs=[SMEM] + [VMEM] * 3,
-        out_specs=[VMEM] * 3,
-        out_shape=[PARTS, by_j, by_j],
+        in_specs=[VMEM] * 2,
+        out_specs=VMEM,
+        out_shape=PARTS,
         scratch_shapes=[COLUMNS],
         compiler_params=params(18),
         cost_estimate=cost(),
         name="grad_one_columns",
-    )(core, own, other, left_blocks)
-
-
-def weight_kernel(core_ref, own_ref, other_ref, oj_ref, t_ref, mine_ref, theirs_ref, x_ref):
+    )(parts, left_blocks)
+
+
+def weight_kernel(core_ref, parts_ref, l_ref, t_ref, gj_ref, mine_ref, theirs_ref, x_ref, oj_ref):
     core = core_ref[0]
-    load_columns(core, own_ref, other_ref, x_ref)
+    load_columns(0, parts_ref, x_ref)
+    for j in range(LJ):
+        g = get_rows(x_ref, pl.ds(j, A, stride=LJ)).astype(BF16)
+        gj_ref[j] = g
+        oj_ref[pl.ds(j * A, A), :] = dot(l_ref[j], g, 0, 0).astype(BF16)
+    load_columns(1, parts_ref, x_ref)
     for j in range(LJ):
         t_ref[pl.ds(j * A, A), :] = get_rows(x_ref, pl.ds(j, A, stride=LJ)).astype(BF16)
     for half, out in ((1 - core, theirs_ref), (core, mine_ref)):
         t = t_ref[:, pl.ds(pl.multiple_of(half * 384, 128), 384)]
-        part = dot(t, oj_ref[...].reshape(A * LJ, D), 0, 0)
+        part = dot(t, oj_ref[...], 0, 0)
         for q in range(4):
             for k in range(6):
                 piece = part[q * 96:(q + 1) * 96, k * 128:(k + 1) * 128]
                 out[q, pl.ds(k * 96, 96), :] = piece.astype(out.dtype)
 
 
-def weight_grad(core, own, other, by_j_one):
+def weight_grad(core, parts, left_blocks):
     half = (4, WR, 128)
     return pl.pallas_call(
         weight_kernel,
-        in_specs=[SMEM] + [VMEM] * 3,
-        out_specs=[VMEM] * 3,
+        in_specs=[SMEM] + [VMEM] * 2,
+        out_specs=[VMEM] * 4,
         out_shape=[
             jax.ShapeDtypeStruct((A * LJ, D), BF16),
+            jax.ShapeDtypeStruct((LJ, A, D), BF16),
             jax.ShapeDtypeStruct(half, F32),
             jax.ShapeDtypeStruct(half, BF16),
         ],
-        scratch_shapes=[COLUMNS],
-        compiler_params=params(18),
+        scratch_shapes=[COLUMNS, pltpu.VMEM((A * LJ, D), BF16)],
+        compiler_params=params(20),
         cost_estimate=cost(),
         name="weight_grad",
-    )(core, own, other, by_j_one)
+    )(core, parts, left_blocks)
 
 
 def two_kernel(t_ref, w_ref, l_ref, gj_ref, o_ref, lp_ref, x_ref, s_ref):
@@ -249,7 +247,9 @@
     total = p_ref[0].astype(F32)
     for i in range(1, NCHIP):
         total = total + p_ref[i].astype(F32)
-    o_ref[...] = total
+    total = total.astype(BF16)
+    for i in range(2 * NCHIP):
+        o_ref[i] = total
 
 
 def weight_sum(two_parts):
@@ -257,8 +257,8 @@
         weight_sum_kernel,
         grid=(1,),
         in_specs=[pl.BlockSpec((NCHIP, WCH, 128), lambda i: (0, 384 // WCH, 0))],
-        out_specs=pl.BlockSpec((WCH, 128), lambda i: (0, 0)),
-        out_shape=jax.ShapeDtypeStruct((WCH, 128), F32),
+        out_specs=pl.BlockSpec((2 * NCHIP, WCH, 128), lambda i: (0, 0, 0)),
+        out_shape=jax.ShapeDtypeStruct((2 * NCHIP, WCH, 128), BF16),
         compiler_params=params(6),
         cost_estimate=cost(),
         name="weight_sum",
@@ -307,33 +307,12 @@
     )(at, own, other)
 
 
-def join_kernel(core_ref, own_ref, other_ref, o_ref):
-    core = core_ref[0]
-
-    @pl.loop(0, NCHIP)
-    def _(i):
-        o_ref[i, core] = own_ref[i, core]
-        o_ref[i, 1 - core] = other_ref[i, core]
-
-
-def join_cores(core, own, other):
-    return pl.pallas_call(
-        join_kernel,
-        in_specs=[SMEM] + [VMEM] * 2,
-        out_specs=VMEM,
-        out_shape=PARTS,
-        compiler_params=params(10),
-        cost_estimate=cost(),
-        name="join_cores",
-    )(core, own, other)
-
-
 def right_kernel(x_index_ref, parts_ref, p_ref, l_ref, g_ref, own_ref, a_ref, b_ref, c_ref, x_ref):
     x = x_index_ref[0]
 
-    @pl.loop(0, NCHIP)
-    def _(i):
-        x_ref[pl.ds(i * 2, 2)] = parts_ref[i].astype(F32)
+    @pl.loop(0, NDEV)
+    def _(i):
+        x_ref[i] = parts_ref[i].astype(F32)
 
     for k, out in enumerate((own_ref, a_ref, b_ref, c_ref)):
         a = lax.rem(x + k, 4)
@@ -412,8 +391,8 @@
     )(two_parts, tokens, grad_out, back_proj)
 
 
-def exchange(v):
-    return lax.all_to_all(v, CHIPS, split_axis=0, concat_axis=0, tiled=True)
+def exchange(v, axes):
+    return lax.all_to_all(v, axes, split_axis=0, concat_axis=0, tiled=True)
 
 
 def swap(v):
@@ -429,10 +408,6 @@
     return [send(v, axis, k + 1) for k, v in enumerate(pieces)]
 
 
-def gather_from(v, axis):
-    return jnp.stack([v] + along(axis, [v] * (SIZES[axis] - 1)))
-
-
 def place_of(*axes):
     return jnp.stack([lax.axis_index(axis).astype(jnp.int32) for axis in axes])
 
@@ -441,40 +416,37 @@
     tokens, grad_out = tokens[0], grad_out[0]
     core, x_index = place_of("c"), place_of("x")
 
-    grad_parts = exchange(grad_two_parts(tokens, grad_out))
-
-    token_split, projected = front(tokens, right_blocks, in_weight)
-    token_split, projected, grad_parts = lax.optimization_barrier((token_split, projected, grad_parts))
-    token_parts = exchange(token_split)
-
-    one_out, grad_j, one_j = grad_one_columns(core, grad_parts, swap(grad_parts), left_blocks)
-    one_split = join_cores(core, one_out, swap(one_out))
-    one_split, grad_j, one_j, token_parts = lax.optimization_barrier((one_split, grad_j, one_j, token_parts))
-    one_parts = exchange(one_split)
-
-    by_j_token, weight_mine, weight_theirs = weight_grad(core, token_parts, swap(token_parts), one_j)
+    first = exchange(first_parts(tokens, grad_out, right_blocks), DEVICES)
+    projected = project(tokens, in_weight)
+    first, projected = lax.optimization_barrier((first, projected))
+
+    one_split = grad_one_columns(first, left_blocks)
+    one_parts = exchange(one_split, DEVICES)
+
+    by_j_token, grad_j, weight_mine, weight_theirs = weight_grad(core, first, left_blocks)
     two_out, left_part = two_columns(by_j_token, in_weight, left_blocks, grad_j)
     total, *away = spread(x_index, weight_mine, swap(weight_theirs))
     two_split = join_two(core, two_out, swap(two_out), total, along("x", away))
     two_split, left_part, one_parts = lax.optimization_barrier((two_split, left_part, one_parts))
-    two_parts = exchange(two_split)
+    two_parts = exchange(two_split, CHIPS)
 
     grad_one, blocks, *away = block_grads(x_index, one_parts, projected, left_part)
     got = along("x", away)
     blocks = (blocks + got[0].astype(F32)) + (got[1].astype(F32) + got[2].astype(F32))
     back_proj = back_projected(grad_one, right_blocks, in_weight)
-    blocks = (blocks + send(blocks, "zl", 1)).astype(BF16)
+    blocks = blocks.astype(BF16)
+    blocks = (blocks.astype(F32) + send(blocks, "zl", 1).astype(F32)).astype(BF16)
     blocks, back_proj, two_parts = lax.optimization_barrier((blocks, back_proj, two_parts))
 
-    weight = weight_sum(two_parts)
-    weight = (weight + send(weight, "zl", 1)).astype(BF16)
-    weight = exchange(jnp.broadcast_to(weight[None], (NCHIP, WCH, 128)))[:WR // WCH].reshape(WR, 128)
+    weight = exchange(weight_sum(two_parts), ("zl",) + CHIPS)
     grad_left, grad_right = place_blocks(x_index, [blocks] + along("x", [blocks] * 3))
+    weight, two_parts, grad_left, grad_right = lax.optimization_barrier((weight, two_parts, grad_left, grad_right))
+    weight = weight.reshape(2, NCHIP, WCH, 128).astype(F32)
+    weight = (weight[0] + weight[1])[:WR // WCH].reshape(WR, 128).astype(BF16)
+    got_weight = along("x", [weight] * 3)
     mixed, grad_tokens = end(two_parts, tokens, grad_out, back_proj)
-    weight, grad_left, grad_right, mixed, grad_tokens = lax.optimization_barrier(
-        (weight, grad_left, grad_right, mixed, grad_tokens)
-    )
-    weight = gather_from(weight, "x")
+    *got_weight, mixed, grad_tokens = lax.optimization_barrier((*got_weight, mixed, grad_tokens))
+    weight = jnp.stack([weight, *got_weight])
     grad_weight = place_weight(place_of("x", "c"), weight, swap(weight))
     return mixed[None], grad_tokens[None], grad_left, grad_right, grad_weight
 

time: 242 us -> 228 us (0.942)
  local copies, waits for them, and re-layouts: 19.6 us -> 11.6 us
  starting transfers between devices: 77.4 us -> 71.9 us
  Pallas kernels: 32.6 us -> 28.8 us
    all_to_all x5 -> x4, waiting for transfers between devices: 55.6 us -> 71.5 us  [exchange(): return lax.all_to_all(v, axes, split_axis=0, concat_axis=0, tiled=True)]
    ppermute x14 -> x13, waiting for transfers between devices: 46 us -> 35.2 us  [send(): return lax.ppermute(v, axis, [(i, (i + k) % n) for i in range(n)])]
    all_to_all x5 -> x4, starting transfers between devices: 41.3 us -> 34.6 us  [exchange(): return lax.all_to_all(v, axes, split_axis=0, concat_axis=0, tiled=True)]
    unnamed x44 -> x34, local copies, waits for them, and re-layouts: 18 us -> 11.6 us
    ppermute x14 -> x13, starting transfers between devices: 27.3 us -> 32.6 us  [send(): return lax.ppermute(v, axis, [(i, (i + k) % n) for i in range(n)])]
    ppermute x6 -> x3, starting transfers between devices: 8.84 us -> 4.7 us  [swap(): return lax.ppermute(v, 'c', [(0, 1), (1, 0)])]
    pallas_call x5 -> x4, Pallas kernels: 14.9 us -> 11.5 us  [the longest x1 4.24 us: weight_grad(): pl.pallas_call(weight_kernel, in_specs=[SMEM] + [VMEM] * 2, out_specs=[VM...]
    ppermute x6 -> x3, waiting for transfers between devices: 8.68 us -> 5.64 us  [swap(): return lax.ppermute(v, 'c', [(0, 1), (1, 0)])]
  transfers between devices with their start and end apart: 25 -> 20, of which waited for: 15 -> 11; matrix products, arithmetic and copies ran while one was open for 0% -> 0% of each run, Pallas kernels for 11% -> 9%
where the time goes in v1:
time: 228 us; the launch traced here: 227 us
  waiting for transfers between devices  112 us (49%)
  starting transfers between devices  71.9 us (32%)
  Pallas kernels  28.8 us (13%)
  local copies, waits for them, and re-layouts  11.6 us (5%)
    all_to_all x4, waiting for transfers between devices, exchange(): return lax.all_to_all(v, axes, split_axis=0, concat_axis=0, tiled=True)  71.5 us
    ppermute x13, waiting for transfers between devices, send(): return lax.ppermute(v, axis, [(i, (i + k) % n) for i in range(n)])  35.2 us
    all_to_all x4, starting transfers between devices, exchange(): return lax.all_to_all(v, axes, split_axis=0, concat_axis=0, tiled=True)  34.6 us
    ppermute x13, starting transfers between devices, send(): return lax.ppermute(v, axis, [(i, (i + k) % n) for i in range(n)])  32.6 us
    unnamed x34, local copies, waits for them, and re-layouts  11.6 us
    ppermute x3, waiting for transfers between devices, swap(): return lax.ppermute(v, 'c', [(0, 1), (1, 0)])  5.64 us
    ppermute x3, starting transfers between devices, swap(): return lax.ppermute(v, 'c', [(0, 1), (1, 0)])  4.7 us
  transfers between devices with their start and end apart: 20, of which 11 were waited for; matrix products, arithmetic and copies ran while one was open for 0% of the time, Pallas kernels for 9%

profile of v1, /device:TPU:1, one launch (start us, length us, event | category | flops | bytes accessed | tf_op | source)
XLA Modules:
  0.0 227.1 jit_solution(8597530992464458199)
XLA Ops:
  0.6 4.0 %first_parts.1 = bf16[32,2,2,16,768]{4,3,2,1,0:T(8,128)(2,1)} custom-call(bf16[4,256,768]{2,1,0:T(8,128)(2,1)} %bitcast.13, bf16[4,256,768]{2,1,0:T(8,128)(2,1)} %bitcast.16, bf16[4,256,256]{2,1,0:T(8,128)(2,1)} %r_ref.3), custom_call_target="tpu_custom_call" | custom-call | tf_op jit(solution)/shard_map/first_parts/pallas_call | solution.py:51
  4.7 12.8 %all-to-all-start = ((bf16[32,2,2,16,768]{4,3,2,1,0:T(8,128)(2,1)}), bf16[32,2,2,16,768]{4,3,2,1,0:T(8,128)(2,1)S(1)}, u32[]{:S(2)}, u32[]{:S(2)}) async-start(bf16[32,2,2,16,768]{4,3,2,1,0:T(8,128)(2,1)} %first_parts.1), calls=%async_computation | async-start | bytes 6291456 | tf_op jit(solution)/shard_map/all_to_all | solution.py:395
  17.4 1.4 copy-done
  18.8 1.3 copy-done.4
  20.1 1.4 project.1.p_ref
  21.5 1.1 copy-done.8
  22.7 67.3 %all-to-all-done.parts_ref = bf16[32,2,2,16,768]{4,3,2,1,0:T(8,128)(2,1)S(1)} async-done(((bf16[32,2,2,16,768]{4,3,2,1,0:T(8,128)(2,1)}), bf16[32,2,2,16,768]{4,3,2,1,0:T(8,128)(2,1)S(1)}, u32[]{:S(2)}, u32[]{:S(2)}) %all-to-all-start) | async-done | bytes 3145760 | tf_op jit(solution)/shard_map/all_to_all | solution.py:395
  90.0 1.9 grad_one_columns.1
  91.9 1.1 copy-done.7
  93.0 6.0 %all-to-all-start.1 = ((bf16[32,32,768]{2,1,0:T(8,128)(2,1)}), bf16[32,32,768]{2,1,0:T(8,128)(2,1)}, u32[]{:S(2)}, u32[]{:S(2)}) async-start(bf16[32,32,768]{2,1,0:T(8,128)(2,1)} %copy-done.7), calls=%async_computation.1 | async-start | bytes 3145728 | tf_op jit(solution)/shard_map/all_to_all | solution.py:395
  99.1 4.2 %weight_grad.1 = (bf16[1024,768]{1,0:T(8,128)(2,1)S(1)}, bf16[8,128,768]{2,1,0:T(8,128)(2,1)S(1)}, f32[4,576,128]{2,1,0:T(8,128)S(1)}, bf16[4,576,128]{2,1,0:T(8,128)(2,1)}) custom-call(s32[1]{0:T(128)} %bitcast.1.core_ref, bf16[32,2,2,16,768]{4,3,2,1,0:T(8,128)(2,1)S(1)} %all-to-all-done.parts_ref, bf16[8,128,128]{2,1,0:T(8,128)(2,1)S(1)} %copy-done.11), custom_call_target="tpu_custom_call" | custom-call | flops 1000 | bytes 1000 | tf_op jit(solution)/shard_map/weight_grad/pallas_call | solution.py:145
  103.3 3.2 %two_columns.1 = (bf16[16,2,192,128]{3,2,1,0:T(8,128)(2,1)S(1)}, f32[8,128,128]{2,1,0:T(8,128)S(1)}) custom-call(bf16[1024,768]{1,0:T(8,128)(2,1)S(1)} %get-tuple-element.42.t_ref, bf16[768,768]{1,0:T(8,128)(2,1)S(1)} %copy-done.5, bf16[8,128,128]{2,1,0:T(8,128)(2,1)S(1)} %copy-done.11, bf16[8,128,768]{2,1,0:T(8,128)(2,1)S(1)} %get-tuple-element.43.gj_ref), custom_call_target="tpu_custom_call" | custom-call | flops 1000 | bytes 1000 | tf_op jit(solution)/shard_map/two_columns/pallas_call | solution.py:181
  106.5 0.8 copy-done.15
  107.8 4.1 %collective-permute-done.1.got_ref = bf16[4,576,128]{2,1,0:T(8,128)(2,1)} collective-permute-done((bf16[4,576,128]{2,1,0:T(8,128)(2,1)}, bf16[4,576,128]{2,1,0:T(8,128)(2,1)}, u32[]{:S(2)}, u32[]{:S(2)}) %collective-permute-start.1) | collective-permute-done | bytes 589856 | tf_op jit(solution)/shard_map/ppermute | solution.py:399
  111.9 1.3 copy-done.14
  113.2 1.2 spread.1
  114.4 1.3 collective-permute-start.2
  115.6 2.5 %collective-permute-start.3 = (bf16[576,128]{1,0:T(8,128)(2,1)S(1)}, bf16[576,128]{1,0:T(8,128)(2,1)S(1)}, u32[]{:S(2)}, u32[]{:S(2)}) collective-permute-start(bf16[576,128]{1,0:T(8,128)(2,1)S(1)} %get-tuple-element.49), channel_id=1, source_target_pairs={{0,64},{32,96},{64,0},{96,32},{1,65},{33,97},{65,1},{97,33},{2,66}... | collective-permute-start | bytes 442376 | tf_op jit(solution)/shard_map/ppermute | solution.py:404
  118.1 1.2 collective-permute-start.4
  119.3 1.6 collective-permute-done.2.a_ref
  120.9 4.1 %collective-permute-done.3.b_ref = bf16[576,128]{1,0:T(8,128)(2,1)S(1)} collective-permute-done((bf16[576,128]{1,0:T(8,128)(2,1)S(1)}, bf16[576,128]{1,0:T(8,128)(2,1)S(1)}, u32[]{:S(2)}, u32[]{:S(2)}) %collective-permute-start.3) | collective-permute-done | bytes 147488 | tf_op jit(solution)/shard_map/ppermute | solution.py:404
  125.0 1.5 join_two.1
  126.5 4.2 %all-to-all-done.1.parts_ref = bf16[32,32,768]{2,1,0:T(8,128)(2,1)} async-done(((bf16[32,32,768]{2,1,0:T(8,128)(2,1)}), bf16[32,32,768]{2,1,0:T(8,128)(2,1)}, u32[]{:S(2)}, u32[]{:S(2)}) %all-to-all-start.1) | async-done | bytes 1572896 | tf_op jit(solution)/shard_map/all_to_all | solution.py:395
  130.7 7.0 %all-to-all-start.2 = ((bf16[16,432,128]{2,1,0:T(8,128)(2,1)}), bf16[16,432,128]{2,1,0:T(8,128)(2,1)S(1)}, u32[]{:S(2)}, u32[]{:S(2)}) async-start(bf16[16,432,128]{2,1,0:T(8,128)(2,1)} %join_two.1), calls=%async_computation.2 | async-start | bytes 3538944 | tf_op jit(solution)/shard_map/all_to_all | solution.py:395
  137.8 1.0 copy-done.16
  138.8 2.5 %block_grads.1 = (bf16[4,256,768]{2,1,0:T(8,128)(2,1)S(1)}, f32[768,128]{1,0:T(8,128)S(1)}, bf16[768,128]{1,0:T(8,128)(2,1)S(1)}, bf16[768,128]{1,0:T(8,128)(2,1)S(1)}, bf16[768,128]{1,0:T(8,128)(2,1)S(1)}) custom-call(s32[1]{0:T(128)} %bitcast.x_index_ref, bf16[32,32,768]{2,1,0:T(8,128)(2,1)} %all-to-all-done.1.parts_ref, ...), custom_call_target="tpu_custom_call" | custom-call | flops 1000 | bytes 1000 | tf_op jit(solution)/shard_map/block_grads/pallas_call | solution.py:329
  141.3 7.1 %collective-permute-start.5 = (bf16[768,128]{1,0:T(8,128)(2,1)S(1)}, bf16[768,128]{1,0:T(8,128)(2,1)S(1)}, u32[]{:S(2)}, u32[]{:S(2)}) collective-permute-start(bf16[768,128]{1,0:T(8,128)(2,1)S(1)} %get-tuple-element.56), channel_id=1, source_target_pairs={{0,32},{32,64},{64,96},{96,0},{1,33},{33,65},{65,97},{97,1},{2,34}... | collective-permute-start | bytes 589832 | tf_op jit(solution)/shard_map/ppermute | solution.py:404
  148.5 2.5 %collective-permute-start.7 = (bf16[768,128]{1,0:T(8,128)(2,1)S(1)}, bf16[768,128]{1,0:T(8,128)(2,1)S(1)}, u32[]{:S(2)}, u32[]{:S(2)}) collective-permute-start(bf16[768,128]{1,0:T(8,128)(2,1)S(1)} %get-tuple-element.58), channel_id=1, source_target_pairs={{0,96},{32,0},{64,32},{96,64},{1,97},{33,1},{65,33},{97,65},{2,98}... | collective-permute-start | bytes 589832 | tf_op jit(solution)/shard_map/ppermute | solution.py:404
  151.0 0.8 collective-permute-done.5
  151.7 4.2 %collective-permute-done.6 = bf16[768,128]{1,0:T(8,128)(2,1)S(1)} collective-permute-done((bf16[768,128]{1,0:T(8,128)(2,1)S(1)}, bf16[768,128]{1,0:T(8,128)(2,1)S(1)}, u32[]{:S(2)}, u32[]{:S(2)}) %collective-permute-start.6) | collective-permute-done | bytes 196640 | tf_op jit(solution)/shard_map/ppermute | solution.py:404
  156.1 4.9 %collective-permute-start.8 = (bf16[768,128]{1,0:T(8,128)(2,1)S(1)}, bf16[768,128]{1,0:T(8,128)(2,1)S(1)}, u32[]{:S(2)}, u32[]{:S(2)}) collective-permute-start(bf16[768,128]{1,0:T(8,128)(2,1)S(1)} %add_convert_fusion.1), channel_id=1, source_target_pairs={{0,128},{128,0},{1,129},{129,1},{2,130},{130,2},{3,131},{131,3},{4... | collective-permute-start | bytes 589832 | tf_op jit(solution)/shard_map/ppermute | solution.py:404
  161.0 2.6 %back_projected.1.b_ref = f32[4,256,768]{2,1,0:T(8,128)S(1)} custom-call(bf16[4,256,768]{2,1,0:T(8,128)(2,1)S(1)} %get-tuple-element.59.g_ref, bf16[4,256,256]{2,1,0:T(8,128)(2,1)S(1)} %copy-done.12, bf16[768,768]{1,0:T(8,128)(2,1)S(1)} %copy-done.6), custom_call_target="tpu_custom_call" | custom-call | flops 1000 | bytes 1000 | tf_op jit(solution)/shard_map/back_projected/pallas_call | solution.py:348
  163.6 1.6 copy-done.2
  165.2 18.4 %collective-permute-done.8 = bf16[768,128]{1,0:T(8,128)(2,1)S(1)} collective-permute-done((bf16[768,128]{1,0:T(8,128)(2,1)S(1)}, bf16[768,128]{1,0:T(8,128)(2,1)S(1)}, u32[]{:S(2)}, u32[]{:S(2)}) %collective-permute-start.8) | collective-permute-done | bytes 196640 | tf_op jit(solution)/shard_map/ppermute | solution.py:404
  183.7 0.8 weight_sum.1
  184.5 8.8 %all-to-all-start.3 = ((bf16[32,48,128]{2,1,0:T(8,128)(2,1)}), bf16[32,48,128]{2,1,0:T(8,128)(2,1)}, u32[]{:S(2)}, u32[]{:S(2)}) async-start(bf16[32,48,128]{2,1,0:T(8,128)(2,1)} %weight_sum.1), calls=%async_computation.3 | async-start | bytes 786432 | tf_op jit(solution)/shard_map/all_to_all | solution.py:395
  193.4 3.2 %collective-permute-start.10 = (bf16[768,128]{1,0:T(8,128)(2,1)S(1)}, bf16[768,128]{1,0:T(8,128)(2,1)S(1)}, u32[]{:S(2)}, u32[]{:S(2)}) collective-permute-start(bf16[768,128]{1,0:T(8,128)(2,1)S(1)} %add_convert_fusion.own_ref), channel_id=1, source_target_pairs={{0,64},{32,96},{64,0},{96,32},{1,65},{33,97},{65,1},{97,33},{2,66}... | collective-permute-start | bytes 589832 | tf_op jit(solution)/shard_map/ppermute | solution.py:404
  196.5 4.0 %collective-permute-start.11 = (bf16[768,128]{1,0:T(8,128)(2,1)S(1)}, bf16[768,128]{1,0:T(8,128)(2,1)S(1)}, u32[]{:S(2)}, u32[]{:S(2)}) collective-permute-start(bf16[768,128]{1,0:T(8,128)(2,1)S(1)} %add_convert_fusion.own_ref), channel_id=1, source_target_pairs={{0,96},{32,0},{64,32},{96,64},{1,97},{33,1},{65,33},{97,65},{2,98}... | collective-permute-start | bytes 589832 | tf_op jit(solution)/shard_map/ppermute | solution.py:404
  200.5 5.6 %collective-permute-done.11.c_ref = bf16[768,128]{1,0:T(8,128)(2,1)S(1)} collective-permute-done((bf16[768,128]{1,0:T(8,128)(2,1)S(1)}, bf16[768,128]{1,0:T(8,128)(2,1)S(1)}, u32[]{:S(2)}, u32[]{:S(2)}) %collective-permute-start.11) | collective-permute-done | bytes 196640 | tf_op jit(solution)/shard_map/ppermute | solution.py:404
  206.7 1.0 place_blocks.1
  207.6 1.2 convert_element_type.50
  208.9 3.4 %collective-permute-start.12 = (bf16[576,128]{1,0:T(8,128)(2,1)S(1)}, bf16[576,128]{1,0:T(8,128)(2,1)S(1)}, u32[]{:S(2)}, u32[]{:S(2)}) collective-permute-start(bf16[576,128]{1,0:T(8,128)(2,1)S(1)} %bitcast.18), channel_id=1, source_target_pairs={{0,32},{32,64},{64,96},{96,0},{1,33},{33,65},{65,97},{97,1},{2,34}... | collective-permute-start | bytes 442376 | tf_op jit(solution)/shard_map/ppermute | solution.py:404
  212.7 2.1 collective-permute-start.14
  214.8 1.9 copy-done.3
  216.7 2.7 %end.1 = (bf16[4,256,768]{2,1,0:T(8,128)(2,1)}, bf16[4,256,768]{2,1,0:T(8,128)(2,1)}) custom-call(bf16[16,432,128]{2,1,0:T(8,128)(2,1)S(1)} %all-to-all-done.2.p_ref.parts_ref, bf16[4,256,768]{2,1,0:T(8,128)(2,1)S(1)} %bitcast.15, bf16[4,256,768]{2,1,0:T(8,128)(2,1)S(1)} %bitcast.17, f32[4,256,768]{2,1,0:T(8,128)S(1)} %copy-done.3), custom_call_target="tpu_custom_call" | custom-call | tf_op jit(solution)/shard_map/end/pallas_call | solution.py:383
  219.5 4.2 %collective-permute-start.15 = (bf16[4,576,128]{2,1,0:T(8,128)(2,1)S(1)}, bf16[4,576,128]{2,1,0:T(8,128)(2,1)S(1)}, u32[]{:S(2)}, u32[]{:S(2)}) collective-permute-start(bf16[4,576,128]{2,1,0:T(8,128)(2,1)S(1)} %pad_maximum_fusion.own_ref), channel_id=1, source_target_pairs={{0,1},{1,0},{2,3},{3,2},{4,5},{5,4},{6,7},{7,6},{8,9},{9,8},{10,11... | collective-permute-start | bytes 1769480 | tf_op jit(solution)/shard_map/ppermute | solution.py:399
  223.8 1.6 collective-permute-done.15.other_ref
  225.3 1.8 place_weight.1
  (46 shorter events, 1.9 us)
Async XLA Ops:
  4.7 85.3 %all-to-all-start = ((bf16[32,2,2,16,768]{4,3,2,1,0:T(8,128)(2,1)}), bf16[32,2,2,16,768]{4,3,2,1,0:T(8,128)(2,1)S(1)}, u32[]{:S(2)}, u32[]{:S(2)}) async-start(bf16[32,2,2,16,768]{4,3,2,1,0:T(8,128)(2,1)} %first_parts.1), calls=%async_computation | async-start | bytes 6291456 | tf_op jit(solution)/shard_map/all_to_all | solution.py:395
  17.4 1.4 copy-start
  18.8 1.3 copy-start.4
  20.1 69.9 %copy-start.11 = (bf16[8,128,128]{2,1,0:T(8,128)(2,1)S(1)}, bf16[8,128,128]{2,1,0:T(8,128)(2,1)}, u32[]{:S(2)}) copy-start(bf16[8,128,128]{2,1,0:T(8,128)(2,1)} %l_ref.5) | copy-start | bytes 786436
  21.5 1.1 copy-start.8
  91.9 1.1 copy-start.7
  93.0 37.7 %all-to-all-start.1 = ((bf16[32,32,768]{2,1,0:T(8,128)(2,1)}), bf16[32,32,768]{2,1,0:T(8,128)(2,1)}, u32[]{:S(2)}, u32[]{:S(2)}) async-start(bf16[32,32,768]{2,1,0:T(8,128)(2,1)} %copy-done.7), calls=%async_computation.1 | async-start | bytes 3145728 | tf_op jit(solution)/shard_map/all_to_all | solution.py:395
  99.0 4.3 %copy-start.5 = (bf16[768,768]{1,0:T(8,128)(2,1)S(1)}, bf16[768,768]{1,0:T(8,128)(2,1)}, u32[]{:S(2)}) copy-start(bf16[768,768]{1,0:T(8,128)(2,1)} %w_ref.5) | copy-start | bytes 3538948
  103.3 3.2 %copy-start.13 = (f32[4,576,128]{2,1,0:T(8,128)}, f32[4,576,128]{2,1,0:T(8,128)S(1)}, u32[]{:S(2)}) copy-start(f32[4,576,128]{2,1,0:T(8,128)S(1)} %get-tuple-element.45.mine_ref) | copy-start | bytes 3538948
  106.5 0.8 copy-start.15
  107.3 17.7 %collective-permute-start = (bf16[16,2,192,128]{3,2,1,0:T(8,128)(2,1)S(1)}, bf16[16,2,192,128]{3,2,1,0:T(8,128)(2,1)S(1)}, u32[]{:S(2)}, u32[]{:S(2)}) collective-permute-start(bf16[16,2,192,128]{3,2,1,0:T(8,128)(2,1)S(1)} %get-tuple-element.44.own_ref), channel_id=1, source_target_pairs={{0,1},{1,0},{2,3},{3,2},{4,5},{5,4},{6,7},{7,6},{8,9},{9,8},{10,11... | collective-permute-start | bytes 4718600 | tf_op jit(solution)/shard_map/ppermute | solution.py:399
  107.6 4.3 %collective-permute-start.1 = (bf16[4,576,128]{2,1,0:T(8,128)(2,1)}, bf16[4,576,128]{2,1,0:T(8,128)(2,1)}, u32[]{:S(2)}, u32[]{:S(2)}) collective-permute-start(bf16[4,576,128]{2,1,0:T(8,128)(2,1)} %get-tuple-element.46), channel_id=1, source_target_pairs={{0,1},{1,0},{2,3},{3,2},{4,5},{5,4},{6,7},{7,6},{8,9},{9,8},{10,11... | collective-permute-start | bytes 1769480 | tf_op jit(solution)/shard_map/ppermute | solution.py:399
  111.9 1.3 copy-start.14
  114.4 6.5 %collective-permute-start.2 = (bf16[576,128]{1,0:T(8,128)(2,1)S(1)}, bf16[576,128]{1,0:T(8,128)(2,1)S(1)}, u32[]{:S(2)}, u32[]{:S(2)}) collective-permute-start(bf16[576,128]{1,0:T(8,128)(2,1)S(1)} %get-tuple-element.48), channel_id=1, source_target_pairs={{0,32},{32,64},{64,96},{96,0},{1,33},{33,65},{65,97},{97,1},{2,34}... | collective-permute-start | bytes 442376 | tf_op jit(solution)/shard_map/ppermute | solution.py:404
  115.6 9.4 %collective-permute-start.3 = (bf16[576,128]{1,0:T(8,128)(2,1)S(1)}, bf16[576,128]{1,0:T(8,128)(2,1)S(1)}, u32[]{:S(2)}, u32[]{:S(2)}) collective-permute-start(bf16[576,128]{1,0:T(8,128)(2,1)S(1)} %get-tuple-element.49), channel_id=1, source_target_pairs={{0,64},{32,96},{64,0},{96,32},{1,65},{33,97},{65,1},{97,33},{2,66}... | collective-permute-start | bytes 442376 | tf_op jit(solution)/shard_map/ppermute | solution.py:404
  118.1 6.9 %collective-permute-start.4 = (bf16[576,128]{1,0:T(8,128)(2,1)S(1)}, bf16[576,128]{1,0:T(8,128)(2,1)S(1)}, u32[]{:S(2)}, u32[]{:S(2)}) collective-permute-start(bf16[576,128]{1,0:T(8,128)(2,1)S(1)} %get-tuple-element.50), channel_id=1, source_target_pairs={{0,96},{32,0},{64,32},{96,64},{1,97},{33,1},{65,33},{97,65},{2,98}... | collective-permute-start | bytes 442376 | tf_op jit(solution)/shard_map/ppermute | solution.py:404
  130.7 7.1 %copy-start.9 = (bf16[4,256,768]{2,1,0:T(8,128)(2,1)S(1)}, bf16[4,256,768]{2,1,0:T(8,128)(2,1)}, u32[]{:S(2)}) copy-start(bf16[4,256,768]{2,1,0:T(8,128)(2,1)} %copy-done.8) | copy-start | bytes 4718596
  130.7 53.0 %all-to-all-start.2 = ((bf16[16,432,128]{2,1,0:T(8,128)(2,1)}), bf16[16,432,128]{2,1,0:T(8,128)(2,1)S(1)}, u32[]{:S(2)}, u32[]{:S(2)}) async-start(bf16[16,432,128]{2,1,0:T(8,128)(2,1)} %join_two.1), calls=%async_computation.2 | async-start | bytes 3538944 | tf_op jit(solution)/shard_map/all_to_all | solution.py:395
  137.8 1.0 copy-start.16
  138.8 22.2 %copy-start.6 = (bf16[768,768]{1,0:T(8,128)(2,1)S(1)}, bf16[768,768]{1,0:T(8,128)(2,1)}, u32[]{:S(2)}) copy-start(bf16[768,768]{1,0:T(8,128)(2,1)} %w_ref.5) | copy-start | bytes 3538948
  138.8 22.2 %copy-start.12 = (bf16[4,256,256]{2,1,0:T(8,128)(2,1)S(1)}, bf16[4,256,256]{2,1,0:T(8,128)(2,1)}, u32[]{:S(2)}) copy-start(bf16[4,256,256]{2,1,0:T(8,128)(2,1)} %r_ref.3) | copy-start | bytes 1572868
  141.3 10.4 %collective-permute-start.5 = (bf16[768,128]{1,0:T(8,128)(2,1)S(1)}, bf16[768,128]{1,0:T(8,128)(2,1)S(1)}, u32[]{:S(2)}, u32[]{:S(2)}) collective-permute-start(bf16[768,128]{1,0:T(8,128)(2,1)S(1)} %get-tuple-element.56), channel_id=1, source_target_pairs={{0,32},{32,64},{64,96},{96,0},{1,33},{33,65},{65,97},{97,1},{2,34}... | collective-permute-start | bytes 589832 | tf_op jit(solution)/shard_map/ppermute | solution.py:404
  148.5 7.5 %collective-permute-start.6 = (bf16[768,128]{1,0:T(8,128)(2,1)S(1)}, bf16[768,128]{1,0:T(8,128)(2,1)S(1)}, u32[]{:S(2)}, u32[]{:S(2)}) collective-permute-start(bf16[768,128]{1,0:T(8,128)(2,1)S(1)} %get-tuple-element.57), channel_id=1, source_target_pairs={{0,64},{32,96},{64,0},{96,32},{1,65},{33,97},{65,1},{97,33},{2,66}... | collective-permute-start | bytes 589832 | tf_op jit(solution)/shard_map/ppermute | solution.py:404
  148.5 7.5 %collective-permute-start.7 = (bf16[768,128]{1,0:T(8,128)(2,1)S(1)}, bf16[768,128]{1,0:T(8,128)(2,1)S(1)}, u32[]{:S(2)}, u32[]{:S(2)}) collective-permute-start(bf16[768,128]{1,0:T(8,128)(2,1)S(1)} %get-tuple-element.58), channel_id=1, source_target_pairs={{0,96},{32,0},{64,32},{96,64},{1,97},{33,1},{65,33},{97,65},{2,98}... | collective-permute-start | bytes 589832 | tf_op jit(solution)/shard_map/ppermute | solution.py:404
  156.1 27.6 %collective-permute-start.8 = (bf16[768,128]{1,0:T(8,128)(2,1)S(1)}, bf16[768,128]{1,0:T(8,128)(2,1)S(1)}, u32[]{:S(2)}, u32[]{:S(2)}) collective-permute-start(bf16[768,128]{1,0:T(8,128)(2,1)S(1)} %add_convert_fusion.1), channel_id=1, source_target_pairs={{0,128},{128,0},{1,129},{129,1},{2,130},{130,2},{3,131},{131,3},{4... | collective-permute-start | bytes 589832 | tf_op jit(solution)/shard_map/ppermute | solution.py:404
  163.6 1.6 copy-start.2
  184.5 23.1 %all-to-all-start.3 = ((bf16[32,48,128]{2,1,0:T(8,128)(2,1)}), bf16[32,48,128]{2,1,0:T(8,128)(2,1)}, u32[]{:S(2)}, u32[]{:S(2)}) async-start(bf16[32,48,128]{2,1,0:T(8,128)(2,1)} %weight_sum.1), calls=%async_computation.3 | async-start | bytes 786432 | tf_op jit(solution)/shard_map/all_to_all | solution.py:395
  193.3 21.5 %copy-start.1 = (bf16[1,4,256,768]{3,2,1,0:T(8,128)(2,1)S(1)}, bf16[1,4,256,768]{3,2,1,0:T(8,128)(2,1)}, u32[]{:S(2)}) copy-start(bf16[1,4,256,768]{3,2,1,0:T(8,128)(2,1)} %param.5) | copy-start | bytes 4718596
  193.4 7.2 %collective-permute-start.10 = (bf16[768,128]{1,0:T(8,128)(2,1)S(1)}, bf16[768,128]{1,0:T(8,128)(2,1)S(1)}, u32[]{:S(2)}, u32[]{:S(2)}) collective-permute-start(bf16[768,128]{1,0:T(8,128)(2,1)S(1)} %add_convert_fusion.own_ref), channel_id=1, source_target_pairs={{0,64},{32,96},{64,0},{96,32},{1,65},{33,97},{65,1},{97,33},{2,66}... | collective-permute-start | bytes 589832 | tf_op jit(solution)/shard_map/ppermute | solution.py:404
  196.5 9.6 %collective-permute-start.11 = (bf16[768,128]{1,0:T(8,128)(2,1)S(1)}, bf16[768,128]{1,0:T(8,128)(2,1)S(1)}, u32[]{:S(2)}, u32[]{:S(2)}) collective-permute-start(bf16[768,128]{1,0:T(8,128)(2,1)S(1)} %add_convert_fusion.own_ref), channel_id=1, source_target_pairs={{0,96},{32,0},{64,32},{96,64},{1,97},{33,1},{65,33},{97,65},{2,98}... | collective-permute-start | bytes 589832 | tf_op jit(solution)/shard_map/ppermute | solution.py:404
  200.5 6.1 %collective-permute-start.9 = (bf16[768,128]{1,0:T(8,128)(2,1)S(1)}, bf16[768,128]{1,0:T(8,128)(2,1)S(1)}, u32[]{:S(2)}, u32[]{:S(2)}) collective-permute-start(bf16[768,128]{1,0:T(8,128)(2,1)S(1)} %add_convert_fusion.own_ref), channel_id=1, source_target_pairs={{0,32},{32,64},{64,96},{96,0},{1,33},{33,65},{65,97},{97,1},{2,34}... | collective-permute-start | bytes 589832 | tf_op jit(solution)/shard_map/ppermute | solution.py:404
  207.6 7.2 %copy-start.10 = (bf16[1,4,256,768]{3,2,1,0:T(8,128)(2,1)S(1)}, bf16[1,4,256,768]{3,2,1,0:T(8,128)(2,1)}, u32[]{:S(2)}) copy-start(bf16[1,4,256,768]{3,2,1,0:T(8,128)(2,1)} %param.6) | copy-start | bytes 4718596
  208.9 10.5 %collective-permute-start.12 = (bf16[576,128]{1,0:T(8,128)(2,1)S(1)}, bf16[576,128]{1,0:T(8,128)(2,1)S(1)}, u32[]{:S(2)}, u32[]{:S(2)}) collective-permute-start(bf16[576,128]{1,0:T(8,128)(2,1)S(1)} %bitcast.18), channel_id=1, source_target_pairs={{0,32},{32,64},{64,96},{96,0},{1,33},{33,65},{65,97},{97,1},{2,34}... | collective-permute-start | bytes 442376 | tf_op jit(solution)/shard_map/ppermute | solution.py:404
  212.3 7.1 %collective-permute-start.13 = (bf16[576,128]{1,0:T(8,128)(2,1)S(1)}, bf16[576,128]{1,0:T(8,128)(2,1)S(1)}, u32[]{:S(2)}, u32[]{:S(2)}) collective-permute-start(bf16[576,128]{1,0:T(8,128)(2,1)S(1)} %bitcast.19), channel_id=1, source_target_pairs={{0,64},{32,96},{64,0},{96,32},{1,65},{33,97},{65,1},{97,33},{2,66}... | collective-permute-start | bytes 442376 | tf_op jit(solution)/shard_map/ppermute | solution.py:404
  212.7 6.7 %collective-permute-start.14 = (bf16[576,128]{1,0:T(8,128)(2,1)S(1)}, bf16[576,128]{1,0:T(8,128)(2,1)S(1)}, u32[]{:S(2)}, u32[]{:S(2)}) collective-permute-start(bf16[576,128]{1,0:T(8,128)(2,1)S(1)} %bitcast.20), channel_id=1, source_target_pairs={{0,96},{32,0},{64,32},{96,64},{1,97},{33,1},{65,33},{97,65},{2,98}... | collective-permute-start | bytes 442376 | tf_op jit(solution)/shard_map/ppermute | solution.py:404
  214.8 1.9 copy-start.3
  219.5 5.8 %collective-permute-start.15 = (bf16[4,576,128]{2,1,0:T(8,128)(2,1)S(1)}, bf16[4,576,128]{2,1,0:T(8,128)(2,1)S(1)}, u32[]{:S(2)}, u32[]{:S(2)}) collective-permute-start(bf16[4,576,128]{2,1,0:T(8,128)(2,1)S(1)} %pad_maximum_fusion.own_ref), channel_id=1, source_target_pairs={{0,1},{1,0},{2,3},{3,2},{4,5},{5,4},{6,7},{7,6},{8,9},{9,8},{10,11... | collective-permute-start | bytes 1769480 | tf_op jit(solution)/shard_map/ppermute | solution.py:399

commit v2 on v1

--- a/solution.py
+++ b/solution.py
@@ -34,16 +34,17 @@
 
 def first_kernel(t_ref, g_ref, r_ref, o_ref, x_ref):
     for a in range(2):
-        t = t_ref[a]
-        x_ref[0, a] = t.astype(F32) * g_ref[a].astype(F32)
-        x_ref[1, a] = dot(r_ref[a], t, 1, 0)
-
-    @pl.loop(0, NDEV)
-    def _(i):
-        rows = pl.ds(pl.multiple_of(i * LJ, LJ), LJ)
-        for kind in range(2):
-            both = jnp.concatenate([x_ref[kind, a, rows, :] for a in range(2)], axis=0)
-            o_ref[i, 0, kind] = both.astype(BF16)
+        x_ref[a] = dot(r_ref[a], t_ref[a], 1, 0)
+
+    @pl.loop(0, NDEV // 2, unroll=4)
+    def _(i):
+        rows = pl.ds(pl.multiple_of(i * 2 * LJ, 2 * LJ), 2 * LJ)
+        two = [t_ref[a, rows, :].astype(F32) * g_ref[a, rows, :].astype(F32) for a in range(2)]
+        one = [x_ref[a, rows, :] for a in range(2)]
+        for kind, v in enumerate((two, one)):
+            for h in range(2):
+                both = jnp.concatenate([v[a][h * LJ:(h + 1) * LJ] for a in range(2)], axis=0)
+                o_ref[i * 2 + h, 0, kind] = both.astype(BF16)
 
 
 def first_parts(tokens, grad_out, right_blocks):
@@ -54,7 +55,7 @@
         in_specs=[rows, rows, pl.BlockSpec((2, B, B), lambda p: (p, 0, 0))],
         out_specs=pl.BlockSpec((NDEV, 1, 2, 2 * LJ, D), lambda p: (0, p, 0, 0, 0)),
         out_shape=FIRST,
-        scratch_shapes=[pltpu.VMEM((2, 2, B, D), F32)],
+        scratch_shapes=[pltpu.VMEM((2, B, D), F32)],
         compiler_params=params(60),
         name="first_parts",
     )(tokens, grad_out, right_blocks)
@@ -90,7 +91,7 @@
 
 
 def load_columns(kind, parts_ref, x_ref):
-    @pl.loop(0, NDEV)
+    @pl.loop(0, NDEV, unroll=4)
     def _(i):
         for p in range(2):
             put_rows(x_ref, pl.ds(i * 32 + p * 16, 16), parts_ref[i, p, kind].astype(F32))
@@ -103,7 +104,7 @@
         g = get_rows(x_ref, at).astype(BF16)
         put_rows(x_ref, at, dot(l_ref[j], g, 0, 0))
 
-    @pl.loop(0, NDEV)
+    @pl.loop(0, NDEV, unroll=4)
     def _(i):
         o_ref[i] = get_rows(x_ref, pl.ds(i * 32, 32)).astype(BF16)
 

time: 228 us -> 226 us (level)
  starting transfers between devices: 71.9 us -> 67 us
  waiting for transfers between devices: 112 us -> 116 us
    ppermute x13, starting transfers between devices: 32.6 us -> 28.8 us  [send(): return lax.ppermute(v, axis, [(i, (i + k) % n) for i in range(n)])]
  transfers between devices with their start and end apart: 20 -> 20, of which waited for: 11 -> 13; matrix products, arithmetic and copies ran while one was open for 0% -> 0% of each run, Pallas kernels for 9% -> 9%
where the time goes in v2:
time: 226 us; the launch traced here: 225 us
  waiting for transfers between devices  116 us (51%)
  starting transfers between devices  67 us (30%)
  Pallas kernels  28.3 us (13%)
  local copies, waits for them, and re-layouts  11.6 us (5%)
    all_to_all x4, waiting for transfers between devices, exchange(): return lax.all_to_all(v, axes, split_axis=0, concat_axis=0, tiled=True)  73.4 us
    ppermute x13, waiting for transfers between devices, send(): return lax.ppermute(v, axis, [(i, (i + k) % n) for i in range(n)])  36.8 us
    all_to_all x4, starting transfers between devices, exchange(): return lax.all_to_all(v, axes, split_axis=0, concat_axis=0, tiled=True)  34.1 us
    ppermute x13, starting transfers between devices, send(): return lax.ppermute(v, axis, [(i, (i + k) % n) for i in range(n)])  28.8 us
    unnamed x34, local copies, waits for them, and re-layouts  11.6 us
    ppermute x3, waiting for transfers between devices, swap(): return lax.ppermute(v, 'c', [(0, 1), (1, 0)])  5.64 us
  transfers between devices with their start and end apart: 20, of which 13 were waited for; matrix products, arithmetic and copies ran while one was open for 0% of the time, Pallas kernels for 9%

profile of v2, /device:TPU:1, one launch (start us, length us, event | category | flops | bytes accessed | tf_op | source)
XLA Modules:
  0.0 225.1 jit_solution(1023653087984796772)
XLA Ops:
  0.6 3.8 %first_parts.1 = bf16[32,2,2,16,768]{4,3,2,1,0:T(8,128)(2,1)} custom-call(bf16[4,256,768]{2,1,0:T(8,128)(2,1)} %bitcast.13, bf16[4,256,768]{2,1,0:T(8,128)(2,1)} %bitcast.16, bf16[4,256,256]{2,1,0:T(8,128)(2,1)} %r_ref.3), custom_call_target="tpu_custom_call" | custom-call | tf_op jit(solution)/shard_map/first_parts/pallas_call | solution.py:52
  4.4 12.8 %all-to-all-start = ((bf16[32,2,2,16,768]{4,3,2,1,0:T(8,128)(2,1)}), bf16[32,2,2,16,768]{4,3,2,1,0:T(8,128)(2,1)S(1)}, u32[]{:S(2)}, u32[]{:S(2)}) async-start(bf16[32,2,2,16,768]{4,3,2,1,0:T(8,128)(2,1)} %first_parts.1), calls=%async_computation | async-start | bytes 6291456 | tf_op jit(solution)/shard_map/all_to_all | solution.py:396
  17.2 1.4 copy-done
  18.6 1.3 copy-done.4
  19.9 1.4 project.1.p_ref
  21.3 1.1 copy-done.8
  22.4 67.2 %all-to-all-done.parts_ref = bf16[32,2,2,16,768]{4,3,2,1,0:T(8,128)(2,1)S(1)} async-done(((bf16[32,2,2,16,768]{4,3,2,1,0:T(8,128)(2,1)}), bf16[32,2,2,16,768]{4,3,2,1,0:T(8,128)(2,1)S(1)}, u32[]{:S(2)}, u32[]{:S(2)}) %all-to-all-start) | async-done | bytes 3145760 | tf_op jit(solution)/shard_map/all_to_all | solution.py:396
  89.7 1.7 grad_one_columns.1
  91.4 1.1 copy-done.7
  92.5 6.2 %all-to-all-start.1 = ((bf16[32,32,768]{2,1,0:T(8,128)(2,1)}), bf16[32,32,768]{2,1,0:T(8,128)(2,1)}, u32[]{:S(2)}, u32[]{:S(2)}) async-start(bf16[32,32,768]{2,1,0:T(8,128)(2,1)} %copy-done.7), calls=%async_computation.1 | async-start | bytes 3145728 | tf_op jit(solution)/shard_map/all_to_all | solution.py:396
  98.7 4.1 %weight_grad.1 = (bf16[1024,768]{1,0:T(8,128)(2,1)S(1)}, bf16[8,128,768]{2,1,0:T(8,128)(2,1)S(1)}, f32[4,576,128]{2,1,0:T(8,128)S(1)}, bf16[4,576,128]{2,1,0:T(8,128)(2,1)}) custom-call(s32[1]{0:T(128)} %bitcast.1.core_ref, bf16[32,2,2,16,768]{4,3,2,1,0:T(8,128)(2,1)S(1)} %all-to-all-done.parts_ref, bf16[8,128,128]{2,1,0:T(8,128)(2,1)S(1)} %copy-done.11), custom_call_target="tpu_custom_call" | custom-call | flops 1000 | bytes 1000 | tf_op jit(solution)/shard_map/weight_grad/pallas_call | solution.py:146
  102.8 3.2 %two_columns.1 = (bf16[16,2,192,128]{3,2,1,0:T(8,128)(2,1)S(1)}, f32[8,128,128]{2,1,0:T(8,128)S(1)}) custom-call(bf16[1024,768]{1,0:T(8,128)(2,1)S(1)} %get-tuple-element.42.t_ref, bf16[768,768]{1,0:T(8,128)(2,1)S(1)} %copy-done.5, bf16[8,128,128]{2,1,0:T(8,128)(2,1)S(1)} %copy-done.11, bf16[8,128,768]{2,1,0:T(8,128)(2,1)S(1)} %get-tuple-element.43.gj_ref), custom_call_target="tpu_custom_call" | custom-call | flops 1000 | bytes 1000 | tf_op jit(solution)/shard_map/two_columns/pallas_call | solution.py:182
  107.4 4.1 %collective-permute-done.1.got_ref = bf16[4,576,128]{2,1,0:T(8,128)(2,1)} collective-permute-done((bf16[4,576,128]{2,1,0:T(8,128)(2,1)}, bf16[4,576,128]{2,1,0:T(8,128)(2,1)}, u32[]{:S(2)}, u32[]{:S(2)}) %collective-permute-start.1) | collective-permute-done | bytes 589856 | tf_op jit(solution)/shard_map/ppermute | solution.py:400
  111.5 1.3 copy-done.14
  112.7 1.2 spread.1
  113.9 1.3 collective-permute-start.2
  115.2 2.3 %collective-permute-start.3 = (bf16[576,128]{1,0:T(8,128)(2,1)S(1)}, bf16[576,128]{1,0:T(8,128)(2,1)S(1)}, u32[]{:S(2)}, u32[]{:S(2)}) collective-permute-start(bf16[576,128]{1,0:T(8,128)(2,1)S(1)} %get-tuple-element.49), channel_id=1, source_target_pairs={{0,64},{32,96},{64,0},{96,32},{1,65},{33,97},{65,1},{97,33},{2,66}... | collective-permute-start | bytes 442376 | tf_op jit(solution)/shard_map/ppermute | solution.py:405
  117.5 1.3 collective-permute-start.4
  118.8 1.7 collective-permute-done.2.a_ref
  120.4 4.0 %collective-permute-done.3.b_ref = bf16[576,128]{1,0:T(8,128)(2,1)S(1)} collective-permute-done((bf16[576,128]{1,0:T(8,128)(2,1)S(1)}, bf16[576,128]{1,0:T(8,128)(2,1)S(1)}, u32[]{:S(2)}, u32[]{:S(2)}) %collective-permute-start.3) | collective-permute-done | bytes 147488 | tf_op jit(solution)/shard_map/ppermute | solution.py:405
  124.4 1.5 join_two.1
  125.9 5.1 %all-to-all-done.1.parts_ref = bf16[32,32,768]{2,1,0:T(8,128)(2,1)} async-done(((bf16[32,32,768]{2,1,0:T(8,128)(2,1)}), bf16[32,32,768]{2,1,0:T(8,128)(2,1)}, u32[]{:S(2)}, u32[]{:S(2)}) %all-to-all-start.1) | async-done | bytes 1572896 | tf_op jit(solution)/shard_map/all_to_all | solution.py:396
  131.1 7.0 %all-to-all-start.2 = ((bf16[16,432,128]{2,1,0:T(8,128)(2,1)}), bf16[16,432,128]{2,1,0:T(8,128)(2,1)S(1)}, u32[]{:S(2)}, u32[]{:S(2)}) async-start(bf16[16,432,128]{2,1,0:T(8,128)(2,1)} %join_two.1), calls=%async_computation.2 | async-start | bytes 3538944 | tf_op jit(solution)/shard_map/all_to_all | solution.py:396
  138.1 1.0 copy-done.16
  139.2 2.5 %block_grads.1 = (bf16[4,256,768]{2,1,0:T(8,128)(2,1)S(1)}, f32[768,128]{1,0:T(8,128)S(1)}, bf16[768,128]{1,0:T(8,128)(2,1)S(1)}, bf16[768,128]{1,0:T(8,128)(2,1)S(1)}, bf16[768,128]{1,0:T(8,128)(2,1)S(1)}) custom-call(s32[1]{0:T(128)} %bitcast.x_index_ref, bf16[32,32,768]{2,1,0:T(8,128)(2,1)} %all-to-all-done.1.parts_ref, ...), custom_call_target="tpu_custom_call" | custom-call | flops 1000 | bytes 1000 | tf_op jit(solution)/shard_map/block_grads/pallas_call | solution.py:330
  141.7 1.4 collective-permute-start.5
  143.1 2.2 collective-permute-start.6
  145.3 1.4 collective-permute-start.7
  147.7 3.1 %collective-permute-done.6 = bf16[768,128]{1,0:T(8,128)(2,1)S(1)} collective-permute-done((bf16[768,128]{1,0:T(8,128)(2,1)S(1)}, bf16[768,128]{1,0:T(8,128)(2,1)S(1)}, u32[]{:S(2)}, u32[]{:S(2)}) %collective-permute-start.6) | collective-permute-done | bytes 196640 | tf_op jit(solution)/shard_map/ppermute | solution.py:405
  150.9 9.7 %collective-permute-start.8 = (bf16[768,128]{1,0:T(8,128)(2,1)S(1)}, bf16[768,128]{1,0:T(8,128)(2,1)S(1)}, u32[]{:S(2)}, u32[]{:S(2)}) collective-permute-start(bf16[768,128]{1,0:T(8,128)(2,1)S(1)} %add_convert_fusion.1), channel_id=1, source_target_pairs={{0,128},{128,0},{1,129},{129,1},{2,130},{130,2},{3,131},{131,3},{4... | collective-permute-start | bytes 589832 | tf_op jit(solution)/shard_map/ppermute | solution.py:405
  160.6 2.6 %back_projected.1.b_ref = f32[4,256,768]{2,1,0:T(8,128)S(1)} custom-call(bf16[4,256,768]{2,1,0:T(8,128)(2,1)S(1)} %get-tuple-element.59.g_ref, bf16[4,256,256]{2,1,0:T(8,128)(2,1)S(1)} %copy-done.12, bf16[768,768]{1,0:T(8,128)(2,1)S(1)} %copy-done.6), custom_call_target="tpu_custom_call" | custom-call | flops 1000 | bytes 1000 | tf_op jit(solution)/shard_map/back_projected/pallas_call | solution.py:349
  163.2 1.6 copy-done.2
  164.9 19.3 %collective-permute-done.8 = bf16[768,128]{1,0:T(8,128)(2,1)S(1)} collective-permute-done((bf16[768,128]{1,0:T(8,128)(2,1)S(1)}, bf16[768,128]{1,0:T(8,128)(2,1)S(1)}, u32[]{:S(2)}, u32[]{:S(2)}) %collective-permute-start.8) | collective-permute-done | bytes 196640 | tf_op jit(solution)/shard_map/ppermute | solution.py:405
  185.1 8.2 %all-to-all-start.3 = ((bf16[32,48,128]{2,1,0:T(8,128)(2,1)}), bf16[32,48,128]{2,1,0:T(8,128)(2,1)}, u32[]{:S(2)}, u32[]{:S(2)}) async-start(bf16[32,48,128]{2,1,0:T(8,128)(2,1)} %weight_sum.1), calls=%async_computation.3 | async-start | bytes 786432 | tf_op jit(solution)/shard_map/all_to_all | solution.py:396
  193.3 2.8 %collective-permute-start.10 = (bf16[768,128]{1,0:T(8,128)(2,1)S(1)}, bf16[768,128]{1,0:T(8,128)(2,1)S(1)}, u32[]{:S(2)}, u32[]{:S(2)}) collective-permute-start(bf16[768,128]{1,0:T(8,128)(2,1)S(1)} %add_convert_fusion.own_ref), channel_id=1, source_target_pairs={{0,64},{32,96},{64,0},{96,32},{1,65},{33,97},{65,1},{97,33},{2,66}... | collective-permute-start | bytes 589832 | tf_op jit(solution)/shard_map/ppermute | solution.py:405
  197.6 2.8 %collective-permute-done.10.b_ref = bf16[768,128]{1,0:T(8,128)(2,1)S(1)} collective-permute-done((bf16[768,128]{1,0:T(8,128)(2,1)S(1)}, bf16[768,128]{1,0:T(8,128)(2,1)S(1)}, u32[]{:S(2)}, u32[]{:S(2)}) %collective-permute-start.10) | collective-permute-done | bytes 196640 | tf_op jit(solution)/shard_map/ppermute | solution.py:405
  200.3 3.8 %collective-permute-done.11.c_ref = bf16[768,128]{1,0:T(8,128)(2,1)S(1)} collective-permute-done((bf16[768,128]{1,0:T(8,128)(2,1)S(1)}, bf16[768,128]{1,0:T(8,128)(2,1)S(1)}, u32[]{:S(2)}, u32[]{:S(2)}) %collective-permute-start.11) | collective-permute-done | bytes 196640 | tf_op jit(solution)/shard_map/ppermute | solution.py:405
  204.2 1.1 collective-permute-done.9.a_ref
  206.3 1.0 all-to-all-done.3
  207.3 1.2 convert_element_type.50
  208.6 1.3 collective-permute-start.12
  209.8 1.6 collective-permute-start.13
  211.5 2.0 collective-permute-start.14
  213.5 1.9 copy-done.3
  215.4 2.7 %end.1 = (bf16[4,256,768]{2,1,0:T(8,128)(2,1)}, bf16[4,256,768]{2,1,0:T(8,128)(2,1)}) custom-call(bf16[16,432,128]{2,1,0:T(8,128)(2,1)S(1)} %all-to-all-done.2.p_ref.parts_ref, bf16[4,256,768]{2,1,0:T(8,128)(2,1)S(1)} %bitcast.15, bf16[4,256,768]{2,1,0:T(8,128)(2,1)S(1)} %bitcast.17, f32[4,256,768]{2,1,0:T(8,128)S(1)} %copy-done.3), custom_call_target="tpu_custom_call" | custom-call | tf_op jit(solution)/shard_map/end/pallas_call | solution.py:384
  218.2 3.6 %collective-permute-start.15 = (bf16[4,576,128]{2,1,0:T(8,128)(2,1)S(1)}, bf16[4,576,128]{2,1,0:T(8,128)(2,1)S(1)}, u32[]{:S(2)}, u32[]{:S(2)}) collective-permute-start(bf16[4,576,128]{2,1,0:T(8,128)(2,1)S(1)} %pad_maximum_fusion.own_ref), channel_id=1, source_target_pairs={{0,1},{1,0},{2,3},{3,2},{4,5},{5,4},{6,7},{7,6},{8,9},{9,8},{10,11... | collective-permute-start | bytes 1769480 | tf_op jit(solution)/shard_map/ppermute | solution.py:400
  221.8 1.6 collective-permute-done.15.other_ref
  223.4 1.8 place_weight.1
  (46 shorter events, 6.0 us)
Async XLA Ops:
  4.4 85.2 %all-to-all-start = ((bf16[32,2,2,16,768]{4,3,2,1,0:T(8,128)(2,1)}), bf16[32,2,2,16,768]{4,3,2,1,0:T(8,128)(2,1)S(1)}, u32[]{:S(2)}, u32[]{:S(2)}) async-start(bf16[32,2,2,16,768]{4,3,2,1,0:T(8,128)(2,1)} %first_parts.1), calls=%async_computation | async-start | bytes 6291456 | tf_op jit(solution)/shard_map/all_to_all | solution.py:396
  17.2 1.4 copy-start
  18.6 1.3 copy-start.4
  19.9 69.8 %copy-start.11 = (bf16[8,128,128]{2,1,0:T(8,128)(2,1)S(1)}, bf16[8,128,128]{2,1,0:T(8,128)(2,1)}, u32[]{:S(2)}) copy-start(bf16[8,128,128]{2,1,0:T(8,128)(2,1)} %l_ref.5) | copy-start | bytes 786436
  21.3 1.1 copy-start.8
  91.4 1.1 copy-start.7
  92.5 38.6 %all-to-all-start.1 = ((bf16[32,32,768]{2,1,0:T(8,128)(2,1)}), bf16[32,32,768]{2,1,0:T(8,128)(2,1)}, u32[]{:S(2)}, u32[]{:S(2)}) async-start(bf16[32,32,768]{2,1,0:T(8,128)(2,1)} %copy-done.7), calls=%async_computation.1 | async-start | bytes 3145728 | tf_op jit(solution)/shard_map/all_to_all | solution.py:396
  98.7 4.1 %copy-start.5 = (bf16[768,768]{1,0:T(8,128)(2,1)S(1)}, bf16[768,768]{1,0:T(8,128)(2,1)}, u32[]{:S(2)}) copy-start(bf16[768,768]{1,0:T(8,128)(2,1)} %w_ref.5) | copy-start | bytes 3538948
  102.8 3.2 %copy-start.13 = (f32[4,576,128]{2,1,0:T(8,128)}, f32[4,576,128]{2,1,0:T(8,128)S(1)}, u32[]{:S(2)}) copy-start(f32[4,576,128]{2,1,0:T(8,128)S(1)} %get-tuple-element.45.mine_ref) | copy-start | bytes 3538948
  106.1 0.8 copy-start.15
  106.9 17.6 %collective-permute-start = (bf16[16,2,192,128]{3,2,1,0:T(8,128)(2,1)S(1)}, bf16[16,2,192,128]{3,2,1,0:T(8,128)(2,1)S(1)}, u32[]{:S(2)}, u32[]{:S(2)}) collective-permute-start(bf16[16,2,192,128]{3,2,1,0:T(8,128)(2,1)S(1)} %get-tuple-element.44.own_ref), channel_id=1, source_target_pairs={{0,1},{1,0},{2,3},{3,2},{4,5},{5,4},{6,7},{7,6},{8,9},{9,8},{10,11... | collective-permute-start | bytes 4718600 | tf_op jit(solution)/shard_map/ppermute | solution.py:400
  107.1 4.3 %collective-permute-start.1 = (bf16[4,576,128]{2,1,0:T(8,128)(2,1)}, bf16[4,576,128]{2,1,0:T(8,128)(2,1)}, u32[]{:S(2)}, u32[]{:S(2)}) collective-permute-start(bf16[4,576,128]{2,1,0:T(8,128)(2,1)} %get-tuple-element.46), channel_id=1, source_target_pairs={{0,1},{1,0},{2,3},{3,2},{4,5},{5,4},{6,7},{7,6},{8,9},{9,8},{10,11... | collective-permute-start | bytes 1769480 | tf_op jit(solution)/shard_map/ppermute | solution.py:400
  111.5 1.3 copy-start.14
  113.9 6.6 %collective-permute-start.2 = (bf16[576,128]{1,0:T(8,128)(2,1)S(1)}, bf16[576,128]{1,0:T(8,128)(2,1)S(1)}, u32[]{:S(2)}, u32[]{:S(2)}) collective-permute-start(bf16[576,128]{1,0:T(8,128)(2,1)S(1)} %get-tuple-element.48), channel_id=1, source_target_pairs={{0,32},{32,64},{64,96},{96,0},{1,33},{33,65},{65,97},{97,1},{2,34}... | collective-permute-start | bytes 442376 | tf_op jit(solution)/shard_map/ppermute | solution.py:405
  115.2 9.3 %collective-permute-start.3 = (bf16[576,128]{1,0:T(8,128)(2,1)S(1)}, bf16[576,128]{1,0:T(8,128)(2,1)S(1)}, u32[]{:S(2)}, u32[]{:S(2)}) collective-permute-start(bf16[576,128]{1,0:T(8,128)(2,1)S(1)} %get-tuple-element.49), channel_id=1, source_target_pairs={{0,64},{32,96},{64,0},{96,32},{1,65},{33,97},{65,1},{97,33},{2,66}... | collective-permute-start | bytes 442376 | tf_op jit(solution)/shard_map/ppermute | solution.py:405
  117.5 7.0 %collective-permute-start.4 = (bf16[576,128]{1,0:T(8,128)(2,1)S(1)}, bf16[576,128]{1,0:T(8,128)(2,1)S(1)}, u32[]{:S(2)}, u32[]{:S(2)}) collective-permute-start(bf16[576,128]{1,0:T(8,128)(2,1)S(1)} %get-tuple-element.50), channel_id=1, source_target_pairs={{0,96},{32,0},{64,32},{96,64},{1,97},{33,1},{65,33},{97,65},{2,98}... | collective-permute-start | bytes 442376 | tf_op jit(solution)/shard_map/ppermute | solution.py:405
  131.1 7.0 %copy-start.9 = (bf16[4,256,768]{2,1,0:T(8,128)(2,1)S(1)}, bf16[4,256,768]{2,1,0:T(8,128)(2,1)}, u32[]{:S(2)}) copy-start(bf16[4,256,768]{2,1,0:T(8,128)(2,1)} %copy-done.8) | copy-start | bytes 4718596
  131.1 53.2 %all-to-all-start.2 = ((bf16[16,432,128]{2,1,0:T(8,128)(2,1)}), bf16[16,432,128]{2,1,0:T(8,128)(2,1)S(1)}, u32[]{:S(2)}, u32[]{:S(2)}) async-start(bf16[16,432,128]{2,1,0:T(8,128)(2,1)} %join_two.1), calls=%async_computation.2 | async-start | bytes 3538944 | tf_op jit(solution)/shard_map/all_to_all | solution.py:396
  138.1 1.0 copy-start.16
  139.1 21.4 %copy-start.6 = (bf16[768,768]{1,0:T(8,128)(2,1)S(1)}, bf16[768,768]{1,0:T(8,128)(2,1)}, u32[]{:S(2)}) copy-start(bf16[768,768]{1,0:T(8,128)(2,1)} %w_ref.5) | copy-start | bytes 3538948
  139.1 21.5 %copy-start.12 = (bf16[4,256,256]{2,1,0:T(8,128)(2,1)S(1)}, bf16[4,256,256]{2,1,0:T(8,128)(2,1)}, u32[]{:S(2)}) copy-start(bf16[4,256,256]{2,1,0:T(8,128)(2,1)} %r_ref.3) | copy-start | bytes 1572868
  141.7 6.0 %collective-permute-start.5 = (bf16[768,128]{1,0:T(8,128)(2,1)S(1)}, bf16[768,128]{1,0:T(8,128)(2,1)S(1)}, u32[]{:S(2)}, u32[]{:S(2)}) collective-permute-start(bf16[768,128]{1,0:T(8,128)(2,1)S(1)} %get-tuple-element.56), channel_id=1, source_target_pairs={{0,32},{32,64},{64,96},{96,0},{1,33},{33,65},{65,97},{97,1},{2,34}... | collective-permute-start | bytes 589832 | tf_op jit(solution)/shard_map/ppermute | solution.py:405
  143.1 7.7 %collective-permute-start.6 = (bf16[768,128]{1,0:T(8,128)(2,1)S(1)}, bf16[768,128]{1,0:T(8,128)(2,1)S(1)}, u32[]{:S(2)}, u32[]{:S(2)}) collective-permute-start(bf16[768,128]{1,0:T(8,128)(2,1)S(1)} %get-tuple-element.57), channel_id=1, source_target_pairs={{0,64},{32,96},{64,0},{96,32},{1,65},{33,97},{65,1},{97,33},{2,66}... | collective-permute-start | bytes 589832 | tf_op jit(solution)/shard_map/ppermute | solution.py:405
  145.3 5.5 %collective-permute-start.7 = (bf16[768,128]{1,0:T(8,128)(2,1)S(1)}, bf16[768,128]{1,0:T(8,128)(2,1)S(1)}, u32[]{:S(2)}, u32[]{:S(2)}) collective-permute-start(bf16[768,128]{1,0:T(8,128)(2,1)S(1)} %get-tuple-element.58), channel_id=1, source_target_pairs={{0,96},{32,0},{64,32},{96,64},{1,97},{33,1},{65,33},{97,65},{2,98}... | collective-permute-start | bytes 589832 | tf_op jit(solution)/shard_map/ppermute | solution.py:405
  150.9 33.3 %collective-permute-start.8 = (bf16[768,128]{1,0:T(8,128)(2,1)S(1)}, bf16[768,128]{1,0:T(8,128)(2,1)S(1)}, u32[]{:S(2)}, u32[]{:S(2)}) collective-permute-start(bf16[768,128]{1,0:T(8,128)(2,1)S(1)} %add_convert_fusion.1), channel_id=1, source_target_pairs={{0,128},{128,0},{1,129},{129,1},{2,130},{130,2},{3,131},{131,3},{4... | collective-permute-start | bytes 589832 | tf_op jit(solution)/shard_map/ppermute | solution.py:405
  163.2 1.6 copy-start.2
  185.1 22.2 %all-to-all-start.3 = ((bf16[32,48,128]{2,1,0:T(8,128)(2,1)}), bf16[32,48,128]{2,1,0:T(8,128)(2,1)}, u32[]{:S(2)}, u32[]{:S(2)}) async-start(bf16[32,48,128]{2,1,0:T(8,128)(2,1)} %weight_sum.1), calls=%async_computation.3 | async-start | bytes 786432 | tf_op jit(solution)/shard_map/all_to_all | solution.py:396
  193.3 20.2 %copy-start.1 = (bf16[1,4,256,768]{3,2,1,0:T(8,128)(2,1)S(1)}, bf16[1,4,256,768]{3,2,1,0:T(8,128)(2,1)}, u32[]{:S(2)}) copy-start(bf16[1,4,256,768]{3,2,1,0:T(8,128)(2,1)} %param.5) | copy-start | bytes 4718596
  193.3 7.1 %collective-permute-start.10 = (bf16[768,128]{1,0:T(8,128)(2,1)S(1)}, bf16[768,128]{1,0:T(8,128)(2,1)S(1)}, u32[]{:S(2)}, u32[]{:S(2)}) collective-permute-start(bf16[768,128]{1,0:T(8,128)(2,1)S(1)} %add_convert_fusion.own_ref), channel_id=1, source_target_pairs={{0,64},{32,96},{64,0},{96,32},{1,65},{33,97},{65,1},{97,33},{2,66}... | collective-permute-start | bytes 589832 | tf_op jit(solution)/shard_map/ppermute | solution.py:405
  196.1 8.1 %collective-permute-start.11 = (bf16[768,128]{1,0:T(8,128)(2,1)S(1)}, bf16[768,128]{1,0:T(8,128)(2,1)S(1)}, u32[]{:S(2)}, u32[]{:S(2)}) collective-permute-start(bf16[768,128]{1,0:T(8,128)(2,1)S(1)} %add_convert_fusion.own_ref), channel_id=1, source_target_pairs={{0,96},{32,0},{64,32},{96,64},{1,97},{33,1},{65,33},{97,65},{2,98}... | collective-permute-start | bytes 589832 | tf_op jit(solution)/shard_map/ppermute | solution.py:405
  197.0 8.4 %collective-permute-start.9 = (bf16[768,128]{1,0:T(8,128)(2,1)S(1)}, bf16[768,128]{1,0:T(8,128)(2,1)S(1)}, u32[]{:S(2)}, u32[]{:S(2)}) collective-permute-start(bf16[768,128]{1,0:T(8,128)(2,1)S(1)} %add_convert_fusion.own_ref), channel_id=1, source_target_pairs={{0,32},{32,64},{64,96},{96,0},{1,33},{33,65},{65,97},{97,1},{2,34}... | collective-permute-start | bytes 589832 | tf_op jit(solution)/shard_map/ppermute | solution.py:405
  207.3 6.1 %copy-start.10 = (bf16[1,4,256,768]{3,2,1,0:T(8,128)(2,1)S(1)}, bf16[1,4,256,768]{3,2,1,0:T(8,128)(2,1)}, u32[]{:S(2)}) copy-start(bf16[1,4,256,768]{3,2,1,0:T(8,128)(2,1)} %param.6) | copy-start | bytes 4718596
  208.6 9.5 %collective-permute-start.12 = (bf16[576,128]{1,0:T(8,128)(2,1)S(1)}, bf16[576,128]{1,0:T(8,128)(2,1)S(1)}, u32[]{:S(2)}, u32[]{:S(2)}) collective-permute-start(bf16[576,128]{1,0:T(8,128)(2,1)S(1)} %bitcast.18), channel_id=1, source_target_pairs={{0,32},{32,64},{64,96},{96,0},{1,33},{33,65},{65,97},{97,1},{2,34}... | collective-permute-start | bytes 442376 | tf_op jit(solution)/shard_map/ppermute | solution.py:405
  209.8 8.2 %collective-permute-start.13 = (bf16[576,128]{1,0:T(8,128)(2,1)S(1)}, bf16[576,128]{1,0:T(8,128)(2,1)S(1)}, u32[]{:S(2)}, u32[]{:S(2)}) collective-permute-start(bf16[576,128]{1,0:T(8,128)(2,1)S(1)} %bitcast.19), channel_id=1, source_target_pairs={{0,64},{32,96},{64,0},{96,32},{1,65},{33,97},{65,1},{97,33},{2,66}... | collective-permute-start | bytes 442376 | tf_op jit(solution)/shard_map/ppermute | solution.py:405
  211.5 6.6 %collective-permute-start.14 = (bf16[576,128]{1,0:T(8,128)(2,1)S(1)}, bf16[576,128]{1,0:T(8,128)(2,1)S(1)}, u32[]{:S(2)}, u32[]{:S(2)}) collective-permute-start(bf16[576,128]{1,0:T(8,128)(2,1)S(1)} %bitcast.20), channel_id=1, source_target_pairs={{0,96},{32,0},{64,32},{96,64},{1,97},{33,1},{65,33},{97,65},{2,98}... | collective-permute-start | bytes 442376 | tf_op jit(solution)/shard_map/ppermute | solution.py:405
  213.5 1.9 copy-start.3
  218.2 5.2 %collective-permute-start.15 = (bf16[4,576,128]{2,1,0:T(8,128)(2,1)S(1)}, bf16[4,576,128]{2,1,0:T(8,128)(2,1)S(1)}, u32[]{:S(2)}, u32[]{:S(2)}) collective-permute-start(bf16[4,576,128]{2,1,0:T(8,128)(2,1)S(1)} %pad_maximum_fusion.own_ref), channel_id=1, source_target_pairs={{0,1},{1,0},{2,3},{3,2},{4,5},{5,4},{6,7},{7,6},{8,9},{9,8},{10,11... | collective-permute-start | bytes 1769480 | tf_op jit(solution)/shard_map/ppermute | solution.py:400

commit v3 on v2

--- a/solution.py
+++ b/solution.py
@@ -286,26 +286,30 @@
     )(x_index, *pieces)
 
 
-def place_kernel(at_ref, own_ref, other_ref, o_ref):
-    x, core = at_ref[0], at_ref[1]
-    for half, ref in ((core, own_ref), (1 - core, other_ref)):
-        for kx in range(4):
-            q = lax.rem(x + 4 - kx, 4)
-            rows = pl.ds(pl.multiple_of(half * 384 + q * 96, 96), 96)
-            for k in range(6):
-                o_ref[rows, pl.ds(k * 128, 128)] = ref[kx, pl.ds(k * 96, 96), :]
-
-
-def place_weight(at, own, other):
+def place_kernel(x_index_ref, half_ref, *refs):
+    pieces, o_ref = refs[:4], refs[-1]
+    for kx, ref in enumerate(pieces):
+        rows = pl.ds(pl.multiple_of(lax.rem(x_index_ref[0] + 4 - kx, 4) * 96, 96), 96)
+        for k in range(6):
+            o_ref[rows, pl.ds(k * 128, 128)] = ref[pl.ds(k * 96, 96), :]
+
+
+def place_half(x_index, half, pieces, whole=None):
+    rest = [] if whole is None else [whole]
     return pl.pallas_call(
         place_kernel,
-        in_specs=[SMEM] + [VMEM] * 2,
-        out_specs=VMEM,
+        grid_spec=pltpu.PrefetchScalarGridSpec(
+            num_scalar_prefetch=2,
+            grid=(1,),
+            in_specs=[pl.BlockSpec((WR, 128), lambda i, x, h: (0, 0))] * 4 + [pl.BlockSpec(memory_space=pl.ANY)] * len(rest),
+            out_specs=pl.BlockSpec((384, D), lambda i, x, h: (h[0], 0)),
+        ),
         out_shape=jax.ShapeDtypeStruct((D, D), BF16),
+        input_output_aliases={} if whole is None else {6: 0},
         compiler_params=params(6),
         cost_estimate=cost(),
-        name="place_weight",
-    )(at, own, other)
+        name="place_half",
+    )(x_index, half, *pieces, *rest)
 
 
 def right_kernel(x_index_ref, parts_ref, p_ref, l_ref, g_ref, own_ref, a_ref, b_ref, c_ref, x_ref):
@@ -447,8 +451,11 @@
     got_weight = along("x", [weight] * 3)
     mixed, grad_tokens = end(two_parts, tokens, grad_out, back_proj)
     *got_weight, mixed, grad_tokens = lax.optimization_barrier((*got_weight, mixed, grad_tokens))
-    weight = jnp.stack([weight, *got_weight])
-    grad_weight = place_weight(place_of("x", "c"), weight, swap(weight))
+    pieces = [weight, *got_weight]
+    others = [swap(v) for v in pieces]
+    grad_weight = place_half(x_index, core, pieces)
+    *others, grad_weight = lax.optimization_barrier((*others, grad_weight))
+    grad_weight = place_half(x_index, 1 - core, others, grad_weight)
     return mixed[None], grad_tokens[None], grad_left, grad_right, grad_weight
 
 

time: 226 us -> 225 us (level)
    ppermute x3 -> x6, waiting for transfers between devices: 5.64 us -> 4.44 us  [swap(): return lax.ppermute(v, 'c', [(0, 1), (1, 0)])]
    ppermute x3 -> x6, starting transfers between devices: 4.06 us -> 4.95 us  [swap(): return lax.ppermute(v, 'c', [(0, 1), (1, 0)])]
  transfers between devices with their start and end apart: 20 -> 23, of which waited for: 13 -> 13; matrix products, arithmetic and copies ran while one was open for 0% -> 0% of each run, Pallas kernels for 9% -> 9%
where the time goes in v3:
time: 225 us; the launch traced here: 224 us
  waiting for transfers between devices  114 us (51%)
  starting transfers between devices  68 us (30%)
  Pallas kernels  28.3 us (13%)
  local copies, waits for them, and re-layouts  11.6 us (5%)
    all_to_all x4, waiting for transfers between devices, exchange(): return lax.all_to_all(v, axes, split_axis=0, concat_axis=0, tiled=True)  73 us
    ppermute x13, waiting for transfers between devices, send(): return lax.ppermute(v, axis, [(i, (i + k) % n) for i in range(n)])  36.9 us
    all_to_all x4, starting transfers between devices, exchange(): return lax.all_to_all(v, axes, split_axis=0, concat_axis=0, tiled=True)  34.1 us
    ppermute x13, starting transfers between devices, send(): return lax.ppermute(v, axis, [(i, (i + k) % n) for i in range(n)])  28.9 us
    unnamed x34, local copies, waits for them, and re-layouts  11.6 us
    ppermute x6, starting transfers between devices, swap(): return lax.ppermute(v, 'c', [(0, 1), (1, 0)])  4.95 us
  transfers between devices with their start and end apart: 23, of which 13 were waited for; matrix products, arithmetic and copies ran while one was open for 0% of the time, Pallas kernels for 9%

profile of v3, /device:TPU:1, one launch (start us, length us, event | category | flops | bytes accessed | tf_op | source)
XLA Modules:
  0.0 224.3 jit_solution(6059103583960601133)
XLA Ops:
  0.6 3.8 %first_parts.1 = bf16[32,2,2,16,768]{4,3,2,1,0:T(8,128)(2,1)} custom-call(bf16[4,256,768]{2,1,0:T(8,128)(2,1)} %bitcast.9, bf16[4,256,768]{2,1,0:T(8,128)(2,1)} %bitcast.12, bf16[4,256,256]{2,1,0:T(8,128)(2,1)} %r_ref.3), custom_call_target="tpu_custom_call" | custom-call | tf_op jit(solution)/shard_map/first_parts/pallas_call | solution.py:52
  4.4 12.8 %all-to-all-start = ((bf16[32,2,2,16,768]{4,3,2,1,0:T(8,128)(2,1)}), bf16[32,2,2,16,768]{4,3,2,1,0:T(8,128)(2,1)S(1)}, u32[]{:S(2)}, u32[]{:S(2)}) async-start(bf16[32,2,2,16,768]{4,3,2,1,0:T(8,128)(2,1)} %first_parts.1), calls=%async_computation | async-start | bytes 6291456 | tf_op jit(solution)/shard_map/all_to_all | solution.py:400
  17.2 1.4 copy-done
  18.6 1.3 copy-done.4
  19.9 1.4 project.1.p_ref
  21.3 1.1 copy-done.8
  22.4 67.2 %all-to-all-done.parts_ref = bf16[32,2,2,16,768]{4,3,2,1,0:T(8,128)(2,1)S(1)} async-done(((bf16[32,2,2,16,768]{4,3,2,1,0:T(8,128)(2,1)}), bf16[32,2,2,16,768]{4,3,2,1,0:T(8,128)(2,1)S(1)}, u32[]{:S(2)}, u32[]{:S(2)}) %all-to-all-start) | async-done | bytes 3145760 | tf_op jit(solution)/shard_map/all_to_all | solution.py:400
  89.7 1.7 grad_one_columns.1
  91.4 1.1 copy-done.7
  92.5 6.2 %all-to-all-start.1 = ((bf16[32,32,768]{2,1,0:T(8,128)(2,1)}), bf16[32,32,768]{2,1,0:T(8,128)(2,1)}, u32[]{:S(2)}, u32[]{:S(2)}) async-start(bf16[32,32,768]{2,1,0:T(8,128)(2,1)} %copy-done.7), calls=%async_computation.1 | async-start | bytes 3145728 | tf_op jit(solution)/shard_map/all_to_all | solution.py:400
  98.7 4.1 %weight_grad.1 = (bf16[1024,768]{1,0:T(8,128)(2,1)S(1)}, bf16[8,128,768]{2,1,0:T(8,128)(2,1)S(1)}, f32[4,576,128]{2,1,0:T(8,128)S(1)}, bf16[4,576,128]{2,1,0:T(8,128)(2,1)}) custom-call(s32[1]{0:T(128)} %bitcast.1.core_ref.half_ref, bf16[32,2,2,16,768]{4,3,2,1,0:T(8,128)(2,1)S(1)} %all-to-all-done.parts_ref, bf16[8,128,128]{2,1,0:T(8,128)(2,1)S(1)} %copy-done.11), custom_call_target="tpu_custom_call" | custom-call | flops 1000 | bytes 1000 | tf_op jit(solution)/shard_map/weight_grad/pallas_call | solution.py:146
  102.8 3.2 %two_columns.1 = (bf16[16,2,192,128]{3,2,1,0:T(8,128)(2,1)S(1)}, f32[8,128,128]{2,1,0:T(8,128)S(1)}) custom-call(bf16[1024,768]{1,0:T(8,128)(2,1)S(1)} %get-tuple-element.47.t_ref, bf16[768,768]{1,0:T(8,128)(2,1)S(1)} %copy-done.5, bf16[8,128,128]{2,1,0:T(8,128)(2,1)S(1)} %copy-done.11, bf16[8,128,768]{2,1,0:T(8,128)(2,1)S(1)} %get-tuple-element.48.gj_ref), custom_call_target="tpu_custom_call" | custom-call | flops 1000 | bytes 1000 | tf_op jit(solution)/shard_map/two_columns/pallas_call | solution.py:182
  107.3 4.1 %collective-permute-done.1.got_ref = bf16[4,576,128]{2,1,0:T(8,128)(2,1)} collective-permute-done((bf16[4,576,128]{2,1,0:T(8,128)(2,1)}, bf16[4,576,128]{2,1,0:T(8,128)(2,1)}, u32[]{:S(2)}, u32[]{:S(2)}) %collective-permute-start.1) | collective-permute-done | bytes 589856 | tf_op jit(solution)/shard_map/ppermute | solution.py:404
  111.4 1.3 copy-done.14
  112.7 1.2 spread.1
  113.8 1.3 collective-permute-start.2
  115.1 2.3 %collective-permute-start.3 = (bf16[576,128]{1,0:T(8,128)(2,1)S(1)}, bf16[576,128]{1,0:T(8,128)(2,1)S(1)}, u32[]{:S(2)}, u32[]{:S(2)}) collective-permute-start(bf16[576,128]{1,0:T(8,128)(2,1)S(1)} %get-tuple-element.54), channel_id=1, source_target_pairs={{0,64},{32,96},{64,0},{96,32},{1,65},{33,97},{65,1},{97,33},{2,66}... | collective-permute-start | bytes 442376 | tf_op jit(solution)/shard_map/ppermute | solution.py:409
  117.4 1.3 collective-permute-start.4
  118.7 1.6 collective-permute-done.2.a_ref
  120.4 4.0 %collective-permute-done.3.b_ref = bf16[576,128]{1,0:T(8,128)(2,1)S(1)} collective-permute-done((bf16[576,128]{1,0:T(8,128)(2,1)S(1)}, bf16[576,128]{1,0:T(8,128)(2,1)S(1)}, u32[]{:S(2)}, u32[]{:S(2)}) %collective-permute-start.3) | collective-permute-done | bytes 147488 | tf_op jit(solution)/shard_map/ppermute | solution.py:409
  124.4 1.5 join_two.1
  125.9 5.1 %all-to-all-done.1.parts_ref = bf16[32,32,768]{2,1,0:T(8,128)(2,1)} async-done(((bf16[32,32,768]{2,1,0:T(8,128)(2,1)}), bf16[32,32,768]{2,1,0:T(8,128)(2,1)}, u32[]{:S(2)}, u32[]{:S(2)}) %all-to-all-start.1) | async-done | bytes 1572896 | tf_op jit(solution)/shard_map/all_to_all | solution.py:400
  131.0 7.0 %all-to-all-start.2 = ((bf16[16,432,128]{2,1,0:T(8,128)(2,1)}), bf16[16,432,128]{2,1,0:T(8,128)(2,1)S(1)}, u32[]{:S(2)}, u32[]{:S(2)}) async-start(bf16[16,432,128]{2,1,0:T(8,128)(2,1)} %join_two.1), calls=%async_computation.2 | async-start | bytes 3538944 | tf_op jit(solution)/shard_map/all_to_all | solution.py:400
  138.0 1.0 copy-done.16
  139.0 2.5 %block_grads.1 = (bf16[4,256,768]{2,1,0:T(8,128)(2,1)S(1)}, f32[768,128]{1,0:T(8,128)S(1)}, bf16[768,128]{1,0:T(8,128)(2,1)S(1)}, bf16[768,128]{1,0:T(8,128)(2,1)S(1)}, bf16[768,128]{1,0:T(8,128)(2,1)S(1)}) custom-call(s32[1]{0:T(128)} %bitcast.x_index_ref, bf16[32,32,768]{2,1,0:T(8,128)(2,1)} %all-to-all-done.1.parts_ref, ...), custom_call_target="tpu_custom_call" | custom-call | flops 1000 | bytes 1000 | tf_op jit(solution)/shard_map/block_grads/pallas_call | solution.py:334
  141.5 1.5 collective-permute-start.5
  143.1 2.2 collective-permute-start.6
  145.3 1.3 collective-permute-start.7
  147.5 3.2 %collective-permute-done.6 = bf16[768,128]{1,0:T(8,128)(2,1)S(1)} collective-permute-done((bf16[768,128]{1,0:T(8,128)(2,1)S(1)}, bf16[768,128]{1,0:T(8,128)(2,1)S(1)}, u32[]{:S(2)}, u32[]{:S(2)}) %collective-permute-start.6) | collective-permute-done | bytes 196640 | tf_op jit(solution)/shard_map/ppermute | solution.py:409
  150.9 9.7 %collective-permute-start.8 = (bf16[768,128]{1,0:T(8,128)(2,1)S(1)}, bf16[768,128]{1,0:T(8,128)(2,1)S(1)}, u32[]{:S(2)}, u32[]{:S(2)}) collective-permute-start(bf16[768,128]{1,0:T(8,128)(2,1)S(1)} %add_convert_fusion.1), channel_id=1, source_target_pairs={{0,128},{128,0},{1,129},{129,1},{2,130},{130,2},{3,131},{131,3},{4... | collective-permute-start | bytes 589832 | tf_op jit(solution)/shard_map/ppermute | solution.py:409
  160.6 2.6 %back_projected.1.b_ref = f32[4,256,768]{2,1,0:T(8,128)S(1)} custom-call(bf16[4,256,768]{2,1,0:T(8,128)(2,1)S(1)} %get-tuple-element.64.g_ref, bf16[4,256,256]{2,1,0:T(8,128)(2,1)S(1)} %copy-done.12, bf16[768,768]{1,0:T(8,128)(2,1)S(1)} %copy-done.6), custom_call_target="tpu_custom_call" | custom-call | flops 1000 | bytes 1000 | tf_op jit(solution)/shard_map/back_projected/pallas_call | solution.py:353
  163.2 1.6 copy-done.2
  164.9 19.2 %collective-permute-done.8 = bf16[768,128]{1,0:T(8,128)(2,1)S(1)} collective-permute-done((bf16[768,128]{1,0:T(8,128)(2,1)S(1)}, bf16[768,128]{1,0:T(8,128)(2,1)S(1)}, u32[]{:S(2)}, u32[]{:S(2)}) %collective-permute-start.8) | collective-permute-done | bytes 196640 | tf_op jit(solution)/shard_map/ppermute | solution.py:409
  184.9 8.2 %all-to-all-start.3 = ((bf16[32,48,128]{2,1,0:T(8,128)(2,1)}), bf16[32,48,128]{2,1,0:T(8,128)(2,1)}, u32[]{:S(2)}, u32[]{:S(2)}) async-start(bf16[32,48,128]{2,1,0:T(8,128)(2,1)} %weight_sum.1), calls=%async_computation.3 | async-start | bytes 786432 | tf_op jit(solution)/shard_map/all_to_all | solution.py:400
  193.1 2.8 %collective-permute-start.10 = (bf16[768,128]{1,0:T(8,128)(2,1)S(1)}, bf16[768,128]{1,0:T(8,128)(2,1)S(1)}, u32[]{:S(2)}, u32[]{:S(2)}) collective-permute-start(bf16[768,128]{1,0:T(8,128)(2,1)S(1)} %add_convert_fusion.own_ref), channel_id=1, source_target_pairs={{0,64},{32,96},{64,0},{96,32},{1,65},{33,97},{65,1},{97,33},{2,66}... | collective-permute-start | bytes 589832 | tf_op jit(solution)/shard_map/ppermute | solution.py:409
  195.9 1.0 collective-permute-start.11
  197.4 2.5 %collective-permute-done.10.b_ref = bf16[768,128]{1,0:T(8,128)(2,1)S(1)} collective-permute-done((bf16[768,128]{1,0:T(8,128)(2,1)S(1)}, bf16[768,128]{1,0:T(8,128)(2,1)S(1)}, u32[]{:S(2)}, u32[]{:S(2)}) %collective-permute-start.10) | collective-permute-done | bytes 196640 | tf_op jit(solution)/shard_map/ppermute | solution.py:409
  199.9 4.3 %collective-permute-done.11.c_ref = bf16[768,128]{1,0:T(8,128)(2,1)S(1)} collective-permute-done((bf16[768,128]{1,0:T(8,128)(2,1)S(1)}, bf16[768,128]{1,0:T(8,128)(2,1)S(1)}, u32[]{:S(2)}, u32[]{:S(2)}) %collective-permute-start.11) | collective-permute-done | bytes 196640 | tf_op jit(solution)/shard_map/ppermute | solution.py:409
  204.2 1.1 collective-permute-done.9.a_ref
  205.3 1.0 place_blocks.1
  206.9 1.2 convert_element_type.35
  208.2 1.7 collective-permute-start.12
  209.8 1.3 collective-permute-start.13
  211.2 1.9 collective-permute-start.14
  213.1 3.7 %collective-permute-start.15 = (bf16[576,128]{1,0:T(8,128)(2,1)S(1)}, bf16[576,128]{1,0:T(8,128)(2,1)S(1)}, u32[]{:S(2)}, u32[]{:S(2)}) collective-permute-start(bf16[576,128]{1,0:T(8,128)(2,1)S(1)} %bitcast.17), channel_id=1, source_target_pairs={{0,1},{1,0},{2,3},{3,2},{4,5},{5,4},{6,7},{7,6},{8,9},{9,8},{10,11... | collective-permute-start | bytes 442376 | tf_op jit(solution)/shard_map/ppermute | solution.py:404
  216.8 1.9 copy-done.3
  218.7 2.7 %end.1 = (bf16[4,256,768]{2,1,0:T(8,128)(2,1)}, bf16[4,256,768]{2,1,0:T(8,128)(2,1)}) custom-call(bf16[16,432,128]{2,1,0:T(8,128)(2,1)S(1)} %all-to-all-done.2.p_ref.parts_ref, bf16[4,256,768]{2,1,0:T(8,128)(2,1)S(1)} %bitcast.11, bf16[4,256,768]{2,1,0:T(8,128)(2,1)S(1)} %bitcast.13, f32[4,256,768]{2,1,0:T(8,128)S(1)} %copy-done.3), custom_call_target="tpu_custom_call" | custom-call | tf_op jit(solution)/shard_map/end/pallas_call | solution.py:388
  223.4 0.9 place_half.3
  (51 shorter events, 6.3 us)
Async XLA Ops:
  4.4 85.2 %all-to-all-start = ((bf16[32,2,2,16,768]{4,3,2,1,0:T(8,128)(2,1)}), bf16[32,2,2,16,768]{4,3,2,1,0:T(8,128)(2,1)S(1)}, u32[]{:S(2)}, u32[]{:S(2)}) async-start(bf16[32,2,2,16,768]{4,3,2,1,0:T(8,128)(2,1)} %first_parts.1), calls=%async_computation | async-start | bytes 6291456 | tf_op jit(solution)/shard_map/all_to_all | solution.py:400
  17.2 1.4 copy-start
  18.6 1.3 copy-start.4
  19.9 69.8 %copy-start.11 = (bf16[8,128,128]{2,1,0:T(8,128)(2,1)S(1)}, bf16[8,128,128]{2,1,0:T(8,128)(2,1)}, u32[]{:S(2)}) copy-start(bf16[8,128,128]{2,1,0:T(8,128)(2,1)} %l_ref.5) | copy-start | bytes 786436
  21.3 1.1 copy-start.8
  91.4 1.1 copy-start.7
  92.5 38.4 %all-to-all-start.1 = ((bf16[32,32,768]{2,1,0:T(8,128)(2,1)}), bf16[32,32,768]{2,1,0:T(8,128)(2,1)}, u32[]{:S(2)}, u32[]{:S(2)}) async-start(bf16[32,32,768]{2,1,0:T(8,128)(2,1)} %copy-done.7), calls=%async_computation.1 | async-start | bytes 3145728 | tf_op jit(solution)/shard_map/all_to_all | solution.py:400
  98.7 4.1 %copy-start.5 = (bf16[768,768]{1,0:T(8,128)(2,1)S(1)}, bf16[768,768]{1,0:T(8,128)(2,1)}, u32[]{:S(2)}) copy-start(bf16[768,768]{1,0:T(8,128)(2,1)} %w_ref.5) | copy-start | bytes 3538948
  102.8 3.2 %copy-start.13 = (f32[4,576,128]{2,1,0:T(8,128)}, f32[4,576,128]{2,1,0:T(8,128)S(1)}, u32[]{:S(2)}) copy-start(f32[4,576,128]{2,1,0:T(8,128)S(1)} %get-tuple-element.50.mine_ref) | copy-start | bytes 3538948
  106.0 0.8 copy-start.15
  106.8 17.6 %collective-permute-start = (bf16[16,2,192,128]{3,2,1,0:T(8,128)(2,1)S(1)}, bf16[16,2,192,128]{3,2,1,0:T(8,128)(2,1)S(1)}, u32[]{:S(2)}, u32[]{:S(2)}) collective-permute-start(bf16[16,2,192,128]{3,2,1,0:T(8,128)(2,1)S(1)} %get-tuple-element.49.own_ref), channel_id=1, source_target_pairs={{0,1},{1,0},{2,3},{3,2},{4,5},{5,4},{6,7},{7,6},{8,9},{9,8},{10,11... | collective-permute-start | bytes 4718600 | tf_op jit(solution)/shard_map/ppermute | solution.py:404
  107.1 4.3 %collective-permute-start.1 = (bf16[4,576,128]{2,1,0:T(8,128)(2,1)}, bf16[4,576,128]{2,1,0:T(8,128)(2,1)}, u32[]{:S(2)}, u32[]{:S(2)}) collective-permute-start(bf16[4,576,128]{2,1,0:T(8,128)(2,1)} %get-tuple-element.51), channel_id=1, source_target_pairs={{0,1},{1,0},{2,3},{3,2},{4,5},{5,4},{6,7},{7,6},{8,9},{9,8},{10,11... | collective-permute-start | bytes 1769480 | tf_op jit(solution)/shard_map/ppermute | solution.py:404
  111.4 1.3 copy-start.14
  113.8 6.5 %collective-permute-start.2 = (bf16[576,128]{1,0:T(8,128)(2,1)S(1)}, bf16[576,128]{1,0:T(8,128)(2,1)S(1)}, u32[]{:S(2)}, u32[]{:S(2)}) collective-permute-start(bf16[576,128]{1,0:T(8,128)(2,1)S(1)} %get-tuple-element.53), channel_id=1, source_target_pairs={{0,32},{32,64},{64,96},{96,0},{1,33},{33,65},{65,97},{97,1},{2,34}... | collective-permute-start | bytes 442376 | tf_op jit(solution)/shard_map/ppermute | solution.py:409
  115.1 9.2 %collective-permute-start.3 = (bf16[576,128]{1,0:T(8,128)(2,1)S(1)}, bf16[576,128]{1,0:T(8,128)(2,1)S(1)}, u32[]{:S(2)}, u32[]{:S(2)}) collective-permute-start(bf16[576,128]{1,0:T(8,128)(2,1)S(1)} %get-tuple-element.54), channel_id=1, source_target_pairs={{0,64},{32,96},{64,0},{96,32},{1,65},{33,97},{65,1},{97,33},{2,66}... | collective-permute-start | bytes 442376 | tf_op jit(solution)/shard_map/ppermute | solution.py:409
  117.4 6.9 %collective-permute-start.4 = (bf16[576,128]{1,0:T(8,128)(2,1)S(1)}, bf16[576,128]{1,0:T(8,128)(2,1)S(1)}, u32[]{:S(2)}, u32[]{:S(2)}) collective-permute-start(bf16[576,128]{1,0:T(8,128)(2,1)S(1)} %get-tuple-element.55), channel_id=1, source_target_pairs={{0,96},{32,0},{64,32},{96,64},{1,97},{33,1},{65,33},{97,65},{2,98}... | collective-permute-start | bytes 442376 | tf_op jit(solution)/shard_map/ppermute | solution.py:409
  131.0 7.0 %copy-start.9 = (bf16[4,256,768]{2,1,0:T(8,128)(2,1)S(1)}, bf16[4,256,768]{2,1,0:T(8,128)(2,1)}, u32[]{:S(2)}) copy-start(bf16[4,256,768]{2,1,0:T(8,128)(2,1)} %copy-done.8) | copy-start | bytes 4718596
  131.0 53.2 %all-to-all-start.2 = ((bf16[16,432,128]{2,1,0:T(8,128)(2,1)}), bf16[16,432,128]{2,1,0:T(8,128)(2,1)S(1)}, u32[]{:S(2)}, u32[]{:S(2)}) async-start(bf16[16,432,128]{2,1,0:T(8,128)(2,1)} %join_two.1), calls=%async_computation.2 | async-start | bytes 3538944 | tf_op jit(solution)/shard_map/all_to_all | solution.py:400
  138.0 1.0 copy-start.16
  139.0 21.6 %copy-start.6 = (bf16[768,768]{1,0:T(8,128)(2,1)S(1)}, bf16[768,768]{1,0:T(8,128)(2,1)}, u32[]{:S(2)}) copy-start(bf16[768,768]{1,0:T(8,128)(2,1)} %w_ref.5) | copy-start | bytes 3538948
  139.0 21.6 %copy-start.12 = (bf16[4,256,256]{2,1,0:T(8,128)(2,1)S(1)}, bf16[4,256,256]{2,1,0:T(8,128)(2,1)}, u32[]{:S(2)}) copy-start(bf16[4,256,256]{2,1,0:T(8,128)(2,1)} %r_ref.3) | copy-start | bytes 1572868
  141.5 6.0 %collective-permute-start.5 = (bf16[768,128]{1,0:T(8,128)(2,1)S(1)}, bf16[768,128]{1,0:T(8,128)(2,1)S(1)}, u32[]{:S(2)}, u32[]{:S(2)}) collective-permute-start(bf16[768,128]{1,0:T(8,128)(2,1)S(1)} %get-tuple-element.61), channel_id=1, source_target_pairs={{0,32},{32,64},{64,96},{96,0},{1,33},{33,65},{65,97},{97,1},{2,34}... | collective-permute-start | bytes 589832 | tf_op jit(solution)/shard_map/ppermute | solution.py:409
  143.1 7.7 %collective-permute-start.6 = (bf16[768,128]{1,0:T(8,128)(2,1)S(1)}, bf16[768,128]{1,0:T(8,128)(2,1)S(1)}, u32[]{:S(2)}, u32[]{:S(2)}) collective-permute-start(bf16[768,128]{1,0:T(8,128)(2,1)S(1)} %get-tuple-element.62), channel_id=1, source_target_pairs={{0,64},{32,96},{64,0},{96,32},{1,65},{33,97},{65,1},{97,33},{2,66}... | collective-permute-start | bytes 589832 | tf_op jit(solution)/shard_map/ppermute | solution.py:409
  145.3 5.5 %collective-permute-start.7 = (bf16[768,128]{1,0:T(8,128)(2,1)S(1)}, bf16[768,128]{1,0:T(8,128)(2,1)S(1)}, u32[]{:S(2)}, u32[]{:S(2)}) collective-permute-start(bf16[768,128]{1,0:T(8,128)(2,1)S(1)} %get-tuple-element.63), channel_id=1, source_target_pairs={{0,96},{32,0},{64,32},{96,64},{1,97},{33,1},{65,33},{97,65},{2,98}... | collective-permute-start | bytes 589832 | tf_op jit(solution)/shard_map/ppermute | solution.py:409
  150.9 33.2 %collective-permute-start.8 = (bf16[768,128]{1,0:T(8,128)(2,1)S(1)}, bf16[768,128]{1,0:T(8,128)(2,1)S(1)}, u32[]{:S(2)}, u32[]{:S(2)}) collective-permute-start(bf16[768,128]{1,0:T(8,128)(2,1)S(1)} %add_convert_fusion.1), channel_id=1, source_target_pairs={{0,128},{128,0},{1,129},{129,1},{2,130},{130,2},{3,131},{131,3},{4... | collective-permute-start | bytes 589832 | tf_op jit(solution)/shard_map/ppermute | solution.py:409
  163.2 1.6 copy-start.2
  184.9 22.0 %all-to-all-start.3 = ((bf16[32,48,128]{2,1,0:T(8,128)(2,1)}), bf16[32,48,128]{2,1,0:T(8,128)(2,1)}, u32[]{:S(2)}, u32[]{:S(2)}) async-start(bf16[32,48,128]{2,1,0:T(8,128)(2,1)} %weight_sum.1), calls=%async_computation.3 | async-start | bytes 786432 | tf_op jit(solution)/shard_map/all_to_all | solution.py:400
  193.1 23.7 %copy-start.1 = (bf16[1,4,256,768]{3,2,1,0:T(8,128)(2,1)S(1)}, bf16[1,4,256,768]{3,2,1,0:T(8,128)(2,1)}, u32[]{:S(2)}) copy-start(bf16[1,4,256,768]{3,2,1,0:T(8,128)(2,1)} %param.5) | copy-start | bytes 4718596
  193.1 6.8 %collective-permute-start.10 = (bf16[768,128]{1,0:T(8,128)(2,1)S(1)}, bf16[768,128]{1,0:T(8,128)(2,1)S(1)}, u32[]{:S(2)}, u32[]{:S(2)}) collective-permute-start(bf16[768,128]{1,0:T(8,128)(2,1)S(1)} %add_convert_fusion.own_ref), channel_id=1, source_target_pairs={{0,64},{32,96},{64,0},{96,32},{1,65},{33,97},{65,1},{97,33},{2,66}... | collective-permute-start | bytes 589832 | tf_op jit(solution)/shard_map/ppermute | solution.py:409
  195.9 8.2 %collective-permute-start.11 = (bf16[768,128]{1,0:T(8,128)(2,1)S(1)}, bf16[768,128]{1,0:T(8,128)(2,1)S(1)}, u32[]{:S(2)}, u32[]{:S(2)}) collective-permute-start(bf16[768,128]{1,0:T(8,128)(2,1)S(1)} %add_convert_fusion.own_ref), channel_id=1, source_target_pairs={{0,96},{32,0},{64,32},{96,64},{1,97},{33,1},{65,33},{97,65},{2,98}... | collective-permute-start | bytes 589832 | tf_op jit(solution)/shard_map/ppermute | solution.py:409
  197.0 8.4 %collective-permute-start.9 = (bf16[768,128]{1,0:T(8,128)(2,1)S(1)}, bf16[768,128]{1,0:T(8,128)(2,1)S(1)}, u32[]{:S(2)}, u32[]{:S(2)}) collective-permute-start(bf16[768,128]{1,0:T(8,128)(2,1)S(1)} %add_convert_fusion.own_ref), channel_id=1, source_target_pairs={{0,32},{32,64},{64,96},{96,0},{1,33},{33,65},{65,97},{97,1},{2,34}... | collective-permute-start | bytes 589832 | tf_op jit(solution)/shard_map/ppermute | solution.py:409
  206.9 9.9 %copy-start.10 = (bf16[1,4,256,768]{3,2,1,0:T(8,128)(2,1)S(1)}, bf16[1,4,256,768]{3,2,1,0:T(8,128)(2,1)}, u32[]{:S(2)}) copy-start(bf16[1,4,256,768]{3,2,1,0:T(8,128)(2,1)} %param.6) | copy-start | bytes 4718596
  208.2 13.3 %collective-permute-start.12 = (bf16[576,128]{1,0:T(8,128)(2,1)S(1)}, bf16[576,128]{1,0:T(8,128)(2,1)S(1)}, u32[]{:S(2)}, u32[]{:S(2)}) collective-permute-start(bf16[576,128]{1,0:T(8,128)(2,1)S(1)} %bitcast.14), channel_id=1, source_target_pairs={{0,32},{32,64},{64,96},{96,0},{1,33},{33,65},{65,97},{97,1},{2,34}... | collective-permute-start | bytes 442376 | tf_op jit(solution)/shard_map/ppermute | solution.py:409
  209.8 11.6 %collective-permute-start.13 = (bf16[576,128]{1,0:T(8,128)(2,1)S(1)}, bf16[576,128]{1,0:T(8,128)(2,1)S(1)}, u32[]{:S(2)}, u32[]{:S(2)}) collective-permute-start(bf16[576,128]{1,0:T(8,128)(2,1)S(1)} %bitcast.15), channel_id=1, source_target_pairs={{0,64},{32,96},{64,0},{96,32},{1,65},{33,97},{65,1},{97,33},{2,66}... | collective-permute-start | bytes 442376 | tf_op jit(solution)/shard_map/ppermute | solution.py:409
  211.2 10.3 %collective-permute-start.14 = (bf16[576,128]{1,0:T(8,128)(2,1)S(1)}, bf16[576,128]{1,0:T(8,128)(2,1)S(1)}, u32[]{:S(2)}, u32[]{:S(2)}) collective-permute-start(bf16[576,128]{1,0:T(8,128)(2,1)S(1)} %bitcast.16), channel_id=1, source_target_pairs={{0,96},{32,0},{64,32},{96,64},{1,97},{33,1},{65,33},{97,65},{2,98}... | collective-permute-start | bytes 442376 | tf_op jit(solution)/shard_map/ppermute | solution.py:409
  213.1 10.0 %collective-permute-start.15 = (bf16[576,128]{1,0:T(8,128)(2,1)S(1)}, bf16[576,128]{1,0:T(8,128)(2,1)S(1)}, u32[]{:S(2)}, u32[]{:S(2)}) collective-permute-start(bf16[576,128]{1,0:T(8,128)(2,1)S(1)} %bitcast.17), channel_id=1, source_target_pairs={{0,1},{1,0},{2,3},{3,2},{4,5},{5,4},{6,7},{7,6},{8,9},{9,8},{10,11... | collective-permute-start | bytes 442376 | tf_op jit(solution)/shard_map/ppermute | solution.py:404
  216.8 1.9 copy-start.3
  221.5 1.6 collective-permute-start.16
  221.6 1.6 collective-permute-start.17
  222.1 1.4 collective-permute-start.18

commit v4 on v3

--- a/solution.py
+++ b/solution.py
@@ -443,11 +443,11 @@
     blocks = (blocks.astype(F32) + send(blocks, "zl", 1).astype(F32)).astype(BF16)
     blocks, back_proj, two_parts = lax.optimization_barrier((blocks, back_proj, two_parts))
 
-    weight = exchange(weight_sum(two_parts), ("zl",) + CHIPS)
+    weight = exchange(weight_sum(two_parts), ("zh", "zl", "y"))
     grad_left, grad_right = place_blocks(x_index, [blocks] + along("x", [blocks] * 3))
     weight, two_parts, grad_left, grad_right = lax.optimization_barrier((weight, two_parts, grad_left, grad_right))
-    weight = weight.reshape(2, NCHIP, WCH, 128).astype(F32)
-    weight = (weight[0] + weight[1])[:WR // WCH].reshape(WR, 128).astype(BF16)
+    weight = weight.reshape(4, 2, 4, WCH, 128).astype(F32)
+    weight = (weight[:, 0] + weight[:, 1]).reshape(NCHIP * WCH, 128)[:WR].astype(BF16)
     got_weight = along("x", [weight] * 3)
     mixed, grad_tokens = end(two_parts, tokens, grad_out, back_proj)
     *got_weight, mixed, grad_tokens = lax.optimization_barrier((*got_weight, mixed, grad_tokens))

time: 225 us -> 225 us (level)
  waiting for transfers between devices: 114 us -> 124 us
  starting transfers between devices: 68 us -> 58.7 us
    ppermute x13, starting transfers between devices: 28.9 us -> 13.8 us  [send(): return lax.ppermute(v, axis, [(i, (i + k) % n) for i in range(n)])]
    ppermute x13, waiting for transfers between devices: 36.9 us -> 47.8 us  [send(): return lax.ppermute(v, axis, [(i, (i + k) % n) for i in range(n)])]
    all_to_all x4, starting transfers between devices: 34.1 us -> 39.4 us  [exchange(): return lax.all_to_all(v, axes, split_axis=0, concat_axis=0, tiled=True)]
    unnamed x34 -> x35, local copies, waits for them, and re-layouts: 11.6 us -> 11.6 us
  transfers between devices with their start and end apart: 23 -> 23, of which waited for: 13 -> 11; matrix products, arithmetic and copies ran while one was open for 0% -> 0% of each run, Pallas kernels for 9% -> 9%
where the time goes in v4:
time: 225 us; the launch traced here: 224 us
  waiting for transfers between devices  124 us (55%)
  starting transfers between devices  58.7 us (26%)
  Pallas kernels  28.3 us (13%)
  local copies, waits for them, and re-layouts  11.6 us (5%)
    all_to_all x4, waiting for transfers between devices, exchange(): return lax.all_to_all(v, axes, split_axis=0, concat_axis=0, tiled=True)  72.4 us
    ppermute x13, waiting for transfers between devices, send(): return lax.ppermute(v, axis, [(i, (i + k) % n) for i in range(n)])  47.8 us
    all_to_all x4, starting transfers between devices, exchange(): return lax.all_to_all(v, axes, split_axis=0, concat_axis=0, tiled=True)  39.4 us
    ppermute x13, starting transfers between devices, send(): return lax.ppermute(v, axis, [(i, (i + k) % n) for i in range(n)])  13.8 us
    unnamed x35, local copies, waits for them, and re-layouts  11.6 us
    ppermute x6, starting transfers between devices, swap(): return lax.ppermute(v, 'c', [(0, 1), (1, 0)])  5.53 us
  transfers between devices with their start and end apart: 23, of which 11 were waited for; matrix products, arithmetic and copies ran while one was open for 0% of the time, Pallas kernels for 9%

profile of v4, /device:TPU:1, one launch (start us, length us, event | category | flops | bytes accessed | tf_op | source)
XLA Modules:
  0.0 224.1 jit_solution(6591828438850943485)
XLA Ops:
  0.6 3.8 %first_parts.1 = bf16[32,2,2,16,768]{4,3,2,1,0:T(8,128)(2,1)} custom-call(bf16[4,256,768]{2,1,0:T(8,128)(2,1)} %bitcast.13, bf16[4,256,768]{2,1,0:T(8,128)(2,1)} %bitcast.16, bf16[4,256,256]{2,1,0:T(8,128)(2,1)} %r_ref.3), custom_call_target="tpu_custom_call" | custom-call | tf_op jit(solution)/shard_map/first_parts/pallas_call | solution.py:52
  4.4 12.8 %all-to-all-start = ((bf16[32,2,2,16,768]{4,3,2,1,0:T(8,128)(2,1)}), bf16[32,2,2,16,768]{4,3,2,1,0:T(8,128)(2,1)S(1)}, u32[]{:S(2)}, u32[]{:S(2)}) async-start(bf16[32,2,2,16,768]{4,3,2,1,0:T(8,128)(2,1)} %first_parts.1), calls=%async_computation | async-start | bytes 6291456 | tf_op jit(solution)/shard_map/all_to_all | solution.py:400
  17.2 1.4 copy-done
  18.6 1.3 copy-done.4
  19.9 1.4 project.1.p_ref
  21.3 1.1 copy-done.8
  22.4 67.2 %all-to-all-done.parts_ref = bf16[32,2,2,16,768]{4,3,2,1,0:T(8,128)(2,1)S(1)} async-done(((bf16[32,2,2,16,768]{4,3,2,1,0:T(8,128)(2,1)}), bf16[32,2,2,16,768]{4,3,2,1,0:T(8,128)(2,1)S(1)}, u32[]{:S(2)}, u32[]{:S(2)}) %all-to-all-start) | async-done | bytes 3145760 | tf_op jit(solution)/shard_map/all_to_all | solution.py:400
  89.7 1.7 grad_one_columns.1
  91.4 1.1 copy-done.7
  92.5 6.2 %all-to-all-start.1 = ((bf16[32,32,768]{2,1,0:T(8,128)(2,1)}), bf16[32,32,768]{2,1,0:T(8,128)(2,1)}, u32[]{:S(2)}, u32[]{:S(2)}) async-start(bf16[32,32,768]{2,1,0:T(8,128)(2,1)} %copy-done.7), calls=%async_computation.1 | async-start | bytes 3145728 | tf_op jit(solution)/shard_map/all_to_all | solution.py:400
  98.7 4.0 %weight_grad.1 = (bf16[1024,768]{1,0:T(8,128)(2,1)S(1)}, bf16[8,128,768]{2,1,0:T(8,128)(2,1)S(1)}, f32[4,576,128]{2,1,0:T(8,128)S(1)}, bf16[4,576,128]{2,1,0:T(8,128)(2,1)}) custom-call(s32[1]{0:T(128)} %bitcast.1.core_ref.half_ref, bf16[32,2,2,16,768]{4,3,2,1,0:T(8,128)(2,1)S(1)} %all-to-all-done.parts_ref, bf16[8,128,128]{2,1,0:T(8,128)(2,1)S(1)} %copy-done.11), custom_call_target="tpu_custom_call" | custom-call | flops 1000 | bytes 1000 | tf_op jit(solution)/shard_map/weight_grad/pallas_call | solution.py:146
  102.8 3.2 %two_columns.1 = (bf16[16,2,192,128]{3,2,1,0:T(8,128)(2,1)S(1)}, f32[8,128,128]{2,1,0:T(8,128)S(1)}) custom-call(bf16[1024,768]{1,0:T(8,128)(2,1)S(1)} %get-tuple-element.47.t_ref, bf16[768,768]{1,0:T(8,128)(2,1)S(1)} %copy-done.5, bf16[8,128,128]{2,1,0:T(8,128)(2,1)S(1)} %copy-done.11, bf16[8,128,768]{2,1,0:T(8,128)(2,1)S(1)} %get-tuple-element.48.gj_ref), custom_call_target="tpu_custom_call" | custom-call | flops 1000 | bytes 1000 | tf_op jit(solution)/shard_map/two_columns/pallas_call | solution.py:182
  106.0 0.8 copy-done.15
  107.3 4.1 %collective-permute-done.1.got_ref = bf16[4,576,128]{2,1,0:T(8,128)(2,1)} collective-permute-done((bf16[4,576,128]{2,1,0:T(8,128)(2,1)}, bf16[4,576,128]{2,1,0:T(8,128)(2,1)}, u32[]{:S(2)}, u32[]{:S(2)}) %collective-permute-start.1) | collective-permute-done | bytes 589856 | tf_op jit(solution)/shard_map/ppermute | solution.py:404
  111.4 1.3 copy-done.14
  112.7 1.2 spread.1
  113.8 1.3 collective-permute-start.2
  115.1 2.3 %collective-permute-start.3 = (bf16[576,128]{1,0:T(8,128)(2,1)S(1)}, bf16[576,128]{1,0:T(8,128)(2,1)S(1)}, u32[]{:S(2)}, u32[]{:S(2)}) collective-permute-start(bf16[576,128]{1,0:T(8,128)(2,1)S(1)} %get-tuple-element.54), channel_id=1, source_target_pairs={{0,64},{32,96},{64,0},{96,32},{1,65},{33,97},{65,1},{97,33},{2,66}... | collective-permute-start | bytes 442376 | tf_op jit(solution)/shard_map/ppermute | solution.py:409
  117.4 1.3 collective-permute-start.4
  118.7 1.6 collective-permute-done.2.a_ref
  120.4 4.0 %collective-permute-done.3.b_ref = bf16[576,128]{1,0:T(8,128)(2,1)S(1)} collective-permute-done((bf16[576,128]{1,0:T(8,128)(2,1)S(1)}, bf16[576,128]{1,0:T(8,128)(2,1)S(1)}, u32[]{:S(2)}, u32[]{:S(2)}) %collective-permute-start.3) | collective-permute-done | bytes 147488 | tf_op jit(solution)/shard_map/ppermute | solution.py:409
  124.4 1.5 join_two.1
  125.9 5.2 %all-to-all-done.1.parts_ref = bf16[32,32,768]{2,1,0:T(8,128)(2,1)} async-done(((bf16[32,32,768]{2,1,0:T(8,128)(2,1)}), bf16[32,32,768]{2,1,0:T(8,128)(2,1)}, u32[]{:S(2)}, u32[]{:S(2)}) %all-to-all-start.1) | async-done | bytes 1572896 | tf_op jit(solution)/shard_map/all_to_all | solution.py:400
  131.0 12.2 %all-to-all-start.2 = ((bf16[16,432,128]{2,1,0:T(8,128)(2,1)}), bf16[16,432,128]{2,1,0:T(8,128)(2,1)S(1)}, u32[]{:S(2)}, u32[]{:S(2)}) async-start(bf16[16,432,128]{2,1,0:T(8,128)(2,1)} %join_two.1), calls=%async_computation.2 | async-start | bytes 3538944 | tf_op jit(solution)/shard_map/all_to_all | solution.py:400
  143.2 1.0 copy-done.16
  144.3 2.5 %block_grads.1 = (bf16[4,256,768]{2,1,0:T(8,128)(2,1)S(1)}, f32[768,128]{1,0:T(8,128)S(1)}, bf16[768,128]{1,0:T(8,128)(2,1)S(1)}, bf16[768,128]{1,0:T(8,128)(2,1)S(1)}, bf16[768,128]{1,0:T(8,128)(2,1)S(1)}) custom-call(s32[1]{0:T(128)} %bitcast.x_index_ref, bf16[32,32,768]{2,1,0:T(8,128)(2,1)} %all-to-all-done.1.parts_ref, ...), custom_call_target="tpu_custom_call" | custom-call | flops 1000 | bytes 1000 | tf_op jit(solution)/shard_map/block_grads/pallas_call | solution.py:334
  147.2 2.6 %collective-permute-start.7 = (bf16[768,128]{1,0:T(8,128)(2,1)S(1)}, bf16[768,128]{1,0:T(8,128)(2,1)S(1)}, u32[]{:S(2)}, u32[]{:S(2)}) collective-permute-start(bf16[768,128]{1,0:T(8,128)(2,1)S(1)} %get-tuple-element.63), channel_id=1, source_target_pairs={{0,96},{32,0},{64,32},{96,64},{1,97},{33,1},{65,33},{97,65},{2,98}... | collective-permute-start | bytes 589832 | tf_op jit(solution)/shard_map/ppermute | solution.py:409
  149.7 9.1 %collective-permute-done.5 = bf16[768,128]{1,0:T(8,128)(2,1)S(1)} collective-permute-done((bf16[768,128]{1,0:T(8,128)(2,1)S(1)}, bf16[768,128]{1,0:T(8,128)(2,1)S(1)}, u32[]{:S(2)}, u32[]{:S(2)}) %collective-permute-start.5) | collective-permute-done | bytes 196640 | tf_op jit(solution)/shard_map/ppermute | solution.py:409
  159.0 1.6 collective-permute-start.8
  160.6 2.6 %back_projected.1.b_ref = f32[4,256,768]{2,1,0:T(8,128)S(1)} custom-call(bf16[4,256,768]{2,1,0:T(8,128)(2,1)S(1)} %get-tuple-element.64.g_ref, bf16[4,256,256]{2,1,0:T(8,128)(2,1)S(1)} %copy-done.12, bf16[768,768]{1,0:T(8,128)(2,1)S(1)} %copy-done.6), custom_call_target="tpu_custom_call" | custom-call | flops 1000 | bytes 1000 | tf_op jit(solution)/shard_map/back_projected/pallas_call | solution.py:353
  163.2 1.6 copy-done.2
  164.8 22.3 %collective-permute-done.8 = bf16[768,128]{1,0:T(8,128)(2,1)S(1)} collective-permute-done((bf16[768,128]{1,0:T(8,128)(2,1)S(1)}, bf16[768,128]{1,0:T(8,128)(2,1)S(1)}, u32[]{:S(2)}, u32[]{:S(2)}) %collective-permute-start.8) | collective-permute-done | bytes 196640 | tf_op jit(solution)/shard_map/ppermute | solution.py:409
  187.3 0.8 weight_sum.1
  188.1 8.2 %all-to-all-start.3 = ((bf16[32,48,128]{2,1,0:T(8,128)(2,1)}), bf16[32,48,128]{2,1,0:T(8,128)(2,1)S(1)}, u32[]{:S(2)}, u32[]{:S(2)}) async-start(bf16[32,48,128]{2,1,0:T(8,128)(2,1)} %weight_sum.1), calls=%async_computation.3 | async-start | bytes 786432 | tf_op jit(solution)/shard_map/all_to_all | solution.py:400
  196.8 1.1 collective-permute-start.9
  197.9 4.8 %collective-permute-done.10.b_ref = bf16[768,128]{1,0:T(8,128)(2,1)S(1)} collective-permute-done((bf16[768,128]{1,0:T(8,128)(2,1)S(1)}, bf16[768,128]{1,0:T(8,128)(2,1)S(1)}, u32[]{:S(2)}, u32[]{:S(2)}) %collective-permute-start.10) | collective-permute-done | bytes 196640 | tf_op jit(solution)/shard_map/ppermute | solution.py:409
  202.7 1.3 collective-permute-done.11.c_ref
  204.0 4.5 %collective-permute-done.9.a_ref = bf16[768,128]{1,0:T(8,128)(2,1)S(1)} collective-permute-done((bf16[768,128]{1,0:T(8,128)(2,1)S(1)}, bf16[768,128]{1,0:T(8,128)(2,1)S(1)}, u32[]{:S(2)}, u32[]{:S(2)}) %collective-permute-start.9) | collective-permute-done | bytes 196640 | tf_op jit(solution)/shard_map/ppermute | solution.py:409
  208.6 1.0 place_blocks.1
  209.8 0.4 collective-permute-start.13
  210.3 2.2 collective-permute-start.14
  212.5 3.5 %collective-permute-start.15 = (bf16[576,128]{1,0:T(8,128)(2,1)S(1)}, bf16[576,128]{1,0:T(8,128)(2,1)S(1)}, u32[]{:S(2)}, u32[]{:S(2)}) collective-permute-start(bf16[576,128]{1,0:T(8,128)(2,1)S(1)} %bitcast.21), channel_id=1, source_target_pairs={{0,1},{1,0},{2,3},{3,2},{4,5},{5,4},{6,7},{7,6},{8,9},{9,8},{10,11... | collective-permute-start | bytes 442376 | tf_op jit(solution)/shard_map/ppermute | solution.py:404
  216.1 1.9 copy-done.3
  217.9 2.7 %end.1 = (bf16[4,256,768]{2,1,0:T(8,128)(2,1)}, bf16[4,256,768]{2,1,0:T(8,128)(2,1)}) custom-call(bf16[16,432,128]{2,1,0:T(8,128)(2,1)S(1)} %all-to-all-done.2.p_ref.parts_ref, bf16[4,256,768]{2,1,0:T(8,128)(2,1)S(1)} %bitcast.15, bf16[4,256,768]{2,1,0:T(8,128)(2,1)S(1)} %bitcast.17, f32[4,256,768]{2,1,0:T(8,128)S(1)} %copy-done.3), custom_call_target="tpu_custom_call" | custom-call | tf_op jit(solution)/shard_map/end/pallas_call | solution.py:388
  220.7 1.0 collective-permute-start.16
  221.6 0.5 collective-permute-start.18
  222.2 0.9 place_half.2.refs_4_
  223.2 0.9 place_half.3
  (51 shorter events, 2.0 us)
Async XLA Ops:
  4.4 85.2 %all-to-all-start = ((bf16[32,2,2,16,768]{4,3,2,1,0:T(8,128)(2,1)}), bf16[32,2,2,16,768]{4,3,2,1,0:T(8,128)(2,1)S(1)}, u32[]{:S(2)}, u32[]{:S(2)}) async-start(bf16[32,2,2,16,768]{4,3,2,1,0:T(8,128)(2,1)} %first_parts.1), calls=%async_computation | async-start | bytes 6291456 | tf_op jit(solution)/shard_map/all_to_all | solution.py:400
  17.2 1.4 copy-start
  18.6 1.3 copy-start.4
  19.9 69.8 %copy-start.11 = (bf16[8,128,128]{2,1,0:T(8,128)(2,1)S(1)}, bf16[8,128,128]{2,1,0:T(8,128)(2,1)}, u32[]{:S(2)}) copy-start(bf16[8,128,128]{2,1,0:T(8,128)(2,1)} %l_ref.5) | copy-start | bytes 786436
  21.3 1.1 copy-start.8
  91.4 1.1 copy-start.7
  92.5 38.5 %all-to-all-start.1 = ((bf16[32,32,768]{2,1,0:T(8,128)(2,1)}), bf16[32,32,768]{2,1,0:T(8,128)(2,1)}, u32[]{:S(2)}, u32[]{:S(2)}) async-start(bf16[32,32,768]{2,1,0:T(8,128)(2,1)} %copy-done.7), calls=%async_computation.1 | async-start | bytes 3145728 | tf_op jit(solution)/shard_map/all_to_all | solution.py:400
  98.7 4.1 %copy-start.5 = (bf16[768,768]{1,0:T(8,128)(2,1)S(1)}, bf16[768,768]{1,0:T(8,128)(2,1)}, u32[]{:S(2)}) copy-start(bf16[768,768]{1,0:T(8,128)(2,1)} %w_ref.5) | copy-start | bytes 3538948
  102.8 3.2 %copy-start.13 = (f32[4,576,128]{2,1,0:T(8,128)}, f32[4,576,128]{2,1,0:T(8,128)S(1)}, u32[]{:S(2)}) copy-start(f32[4,576,128]{2,1,0:T(8,128)S(1)} %get-tuple-element.50.mine_ref) | copy-start | bytes 3538948
  106.0 0.8 copy-start.15
  106.8 17.6 %collective-permute-start = (bf16[16,2,192,128]{3,2,1,0:T(8,128)(2,1)S(1)}, bf16[16,2,192,128]{3,2,1,0:T(8,128)(2,1)S(1)}, u32[]{:S(2)}, u32[]{:S(2)}) collective-permute-start(bf16[16,2,192,128]{3,2,1,0:T(8,128)(2,1)S(1)} %get-tuple-element.49.own_ref), channel_id=1, source_target_pairs={{0,1},{1,0},{2,3},{3,2},{4,5},{5,4},{6,7},{7,6},{8,9},{9,8},{10,11... | collective-permute-start | bytes 4718600 | tf_op jit(solution)/shard_map/ppermute | solution.py:404
  107.1 4.3 %collective-permute-start.1 = (bf16[4,576,128]{2,1,0:T(8,128)(2,1)}, bf16[4,576,128]{2,1,0:T(8,128)(2,1)}, u32[]{:S(2)}, u32[]{:S(2)}) collective-permute-start(bf16[4,576,128]{2,1,0:T(8,128)(2,1)} %get-tuple-element.51), channel_id=1, source_target_pairs={{0,1},{1,0},{2,3},{3,2},{4,5},{5,4},{6,7},{7,6},{8,9},{9,8},{10,11... | collective-permute-start | bytes 1769480 | tf_op jit(solution)/shard_map/ppermute | solution.py:404
  111.4 1.3 copy-start.14
  113.8 6.5 %collective-permute-start.2 = (bf16[576,128]{1,0:T(8,128)(2,1)S(1)}, bf16[576,128]{1,0:T(8,128)(2,1)S(1)}, u32[]{:S(2)}, u32[]{:S(2)}) collective-permute-start(bf16[576,128]{1,0:T(8,128)(2,1)S(1)} %get-tuple-element.53), channel_id=1, source_target_pairs={{0,32},{32,64},{64,96},{96,0},{1,33},{33,65},{65,97},{97,1},{2,34}... | collective-permute-start | bytes 442376 | tf_op jit(solution)/shard_map/ppermute | solution.py:409
  115.1 9.2 %collective-permute-start.3 = (bf16[576,128]{1,0:T(8,128)(2,1)S(1)}, bf16[576,128]{1,0:T(8,128)(2,1)S(1)}, u32[]{:S(2)}, u32[]{:S(2)}) collective-permute-start(bf16[576,128]{1,0:T(8,128)(2,1)S(1)} %get-tuple-element.54), channel_id=1, source_target_pairs={{0,64},{32,96},{64,0},{96,32},{1,65},{33,97},{65,1},{97,33},{2,66}... | collective-permute-start | bytes 442376 | tf_op jit(solution)/shard_map/ppermute | solution.py:409
  117.4 6.9 %collective-permute-start.4 = (bf16[576,128]{1,0:T(8,128)(2,1)S(1)}, bf16[576,128]{1,0:T(8,128)(2,1)S(1)}, u32[]{:S(2)}, u32[]{:S(2)}) collective-permute-start(bf16[576,128]{1,0:T(8,128)(2,1)S(1)} %get-tuple-element.55), channel_id=1, source_target_pairs={{0,96},{32,0},{64,32},{96,64},{1,97},{33,1},{65,33},{97,65},{2,98}... | collective-permute-start | bytes 442376 | tf_op jit(solution)/shard_map/ppermute | solution.py:409
  131.0 12.2 %copy-start.9 = (bf16[4,256,768]{2,1,0:T(8,128)(2,1)S(1)}, bf16[4,256,768]{2,1,0:T(8,128)(2,1)}, u32[]{:S(2)}) copy-start(bf16[4,256,768]{2,1,0:T(8,128)(2,1)} %copy-done.8) | copy-start | bytes 4718596
  131.0 56.2 %all-to-all-start.2 = ((bf16[16,432,128]{2,1,0:T(8,128)(2,1)}), bf16[16,432,128]{2,1,0:T(8,128)(2,1)S(1)}, u32[]{:S(2)}, u32[]{:S(2)}) async-start(bf16[16,432,128]{2,1,0:T(8,128)(2,1)} %join_two.1), calls=%async_computation.2 | async-start | bytes 3538944 | tf_op jit(solution)/shard_map/all_to_all | solution.py:400
  143.2 1.0 copy-start.16
  144.3 16.3 %copy-start.6 = (bf16[768,768]{1,0:T(8,128)(2,1)S(1)}, bf16[768,768]{1,0:T(8,128)(2,1)}, u32[]{:S(2)}) copy-start(bf16[768,768]{1,0:T(8,128)(2,1)} %w_ref.5) | copy-start | bytes 3538948
  144.3 16.3 %copy-start.12 = (bf16[4,256,256]{2,1,0:T(8,128)(2,1)S(1)}, bf16[4,256,256]{2,1,0:T(8,128)(2,1)}, u32[]{:S(2)}) copy-start(bf16[4,256,256]{2,1,0:T(8,128)(2,1)} %r_ref.3) | copy-start | bytes 1572868
  146.8 12.1 %collective-permute-start.5 = (bf16[768,128]{1,0:T(8,128)(2,1)S(1)}, bf16[768,128]{1,0:T(8,128)(2,1)S(1)}, u32[]{:S(2)}, u32[]{:S(2)}) collective-permute-start(bf16[768,128]{1,0:T(8,128)(2,1)S(1)} %get-tuple-element.61), channel_id=1, source_target_pairs={{0,32},{32,64},{64,96},{96,0},{1,33},{33,65},{65,97},{97,1},{2,34}... | collective-permute-start | bytes 589832 | tf_op jit(solution)/shard_map/ppermute | solution.py:409
  147.1 11.8 %collective-permute-start.6 = (bf16[768,128]{1,0:T(8,128)(2,1)S(1)}, bf16[768,128]{1,0:T(8,128)(2,1)S(1)}, u32[]{:S(2)}, u32[]{:S(2)}) collective-permute-start(bf16[768,128]{1,0:T(8,128)(2,1)S(1)} %get-tuple-element.62), channel_id=1, source_target_pairs={{0,64},{32,96},{64,0},{96,32},{1,65},{33,97},{65,1},{97,33},{2,66}... | collective-permute-start | bytes 589832 | tf_op jit(solution)/shard_map/ppermute | solution.py:409
  147.2 11.7 %collective-permute-start.7 = (bf16[768,128]{1,0:T(8,128)(2,1)S(1)}, bf16[768,128]{1,0:T(8,128)(2,1)S(1)}, u32[]{:S(2)}, u32[]{:S(2)}) collective-permute-start(bf16[768,128]{1,0:T(8,128)(2,1)S(1)} %get-tuple-element.63), channel_id=1, source_target_pairs={{0,96},{32,0},{64,32},{96,64},{1,97},{33,1},{65,33},{97,65},{2,98}... | collective-permute-start | bytes 589832 | tf_op jit(solution)/shard_map/ppermute | solution.py:409
  159.0 28.2 %collective-permute-start.8 = (bf16[768,128]{1,0:T(8,128)(2,1)S(1)}, bf16[768,128]{1,0:T(8,128)(2,1)S(1)}, u32[]{:S(2)}, u32[]{:S(2)}) collective-permute-start(bf16[768,128]{1,0:T(8,128)(2,1)S(1)} %add_convert_fusion.1), channel_id=1, source_target_pairs={{0,128},{128,0},{1,129},{129,1},{2,130},{130,2},{3,131},{131,3},{4... | collective-permute-start | bytes 589832 | tf_op jit(solution)/shard_map/ppermute | solution.py:409
  163.2 1.6 copy-start.2
  188.1 21.5 %all-to-all-start.3 = ((bf16[32,48,128]{2,1,0:T(8,128)(2,1)}), bf16[32,48,128]{2,1,0:T(8,128)(2,1)S(1)}, u32[]{:S(2)}, u32[]{:S(2)}) async-start(bf16[32,48,128]{2,1,0:T(8,128)(2,1)} %weight_sum.1), calls=%async_computation.3 | async-start | bytes 786432 | tf_op jit(solution)/shard_map/all_to_all | solution.py:400
  196.3 6.4 %collective-permute-start.10 = (bf16[768,128]{1,0:T(8,128)(2,1)S(1)}, bf16[768,128]{1,0:T(8,128)(2,1)S(1)}, u32[]{:S(2)}, u32[]{:S(2)}) collective-permute-start(bf16[768,128]{1,0:T(8,128)(2,1)S(1)} %add_convert_fusion.own_ref), channel_id=1, source_target_pairs={{0,64},{32,96},{64,0},{96,32},{1,65},{33,97},{65,1},{97,33},{2,66}... | collective-permute-start | bytes 589832 | tf_op jit(solution)/shard_map/ppermute | solution.py:409
  196.4 7.7 %collective-permute-start.11 = (bf16[768,128]{1,0:T(8,128)(2,1)S(1)}, bf16[768,128]{1,0:T(8,128)(2,1)S(1)}, u32[]{:S(2)}, u32[]{:S(2)}) collective-permute-start(bf16[768,128]{1,0:T(8,128)(2,1)S(1)} %add_convert_fusion.own_ref), channel_id=1, source_target_pairs={{0,96},{32,0},{64,32},{96,64},{1,97},{33,1},{65,33},{97,65},{2,98}... | collective-permute-start | bytes 589832 | tf_op jit(solution)/shard_map/ppermute | solution.py:409
  196.8 11.8 %collective-permute-start.9 = (bf16[768,128]{1,0:T(8,128)(2,1)S(1)}, bf16[768,128]{1,0:T(8,128)(2,1)S(1)}, u32[]{:S(2)}, u32[]{:S(2)}) collective-permute-start(bf16[768,128]{1,0:T(8,128)(2,1)S(1)} %add_convert_fusion.own_ref), channel_id=1, source_target_pairs={{0,32},{32,64},{64,96},{96,0},{1,33},{33,65},{65,97},{97,1},{2,34}... | collective-permute-start | bytes 589832 | tf_op jit(solution)/shard_map/ppermute | solution.py:409
  209.6 6.5 %copy-start.1 = (bf16[1,4,256,768]{3,2,1,0:T(8,128)(2,1)S(1)}, bf16[1,4,256,768]{3,2,1,0:T(8,128)(2,1)}, u32[]{:S(2)}) copy-start(bf16[1,4,256,768]{3,2,1,0:T(8,128)(2,1)} %param.5) | copy-start | bytes 4718596
  209.6 6.5 %copy-start.10 = (bf16[1,4,256,768]{3,2,1,0:T(8,128)(2,1)S(1)}, bf16[1,4,256,768]{3,2,1,0:T(8,128)(2,1)}, u32[]{:S(2)}) copy-start(bf16[1,4,256,768]{3,2,1,0:T(8,128)(2,1)} %param.6) | copy-start | bytes 4718596
  209.7 10.9 %collective-permute-start.12 = (bf16[576,128]{1,0:T(8,128)(2,1)S(1)}, bf16[576,128]{1,0:T(8,128)(2,1)S(1)}, u32[]{:S(2)}, u32[]{:S(2)}) collective-permute-start(bf16[576,128]{1,0:T(8,128)(2,1)S(1)} %bitcast.18), channel_id=1, source_target_pairs={{0,32},{32,64},{64,96},{96,0},{1,33},{33,65},{65,97},{97,1},{2,34}... | collective-permute-start | bytes 442376 | tf_op jit(solution)/shard_map/ppermute | solution.py:409
  209.8 10.8 %collective-permute-start.13 = (bf16[576,128]{1,0:T(8,128)(2,1)S(1)}, bf16[576,128]{1,0:T(8,128)(2,1)S(1)}, u32[]{:S(2)}, u32[]{:S(2)}) collective-permute-start(bf16[576,128]{1,0:T(8,128)(2,1)S(1)} %bitcast.19), channel_id=1, source_target_pairs={{0,64},{32,96},{64,0},{96,32},{1,65},{33,97},{65,1},{97,33},{2,66}... | collective-permute-start | bytes 442376 | tf_op jit(solution)/shard_map/ppermute | solution.py:409
  210.3 10.4 %collective-permute-start.14 = (bf16[576,128]{1,0:T(8,128)(2,1)S(1)}, bf16[576,128]{1,0:T(8,128)(2,1)S(1)}, u32[]{:S(2)}, u32[]{:S(2)}) collective-permute-start(bf16[576,128]{1,0:T(8,128)(2,1)S(1)} %bitcast.20), channel_id=1, source_target_pairs={{0,96},{32,0},{64,32},{96,64},{1,97},{33,1},{65,33},{97,65},{2,98}... | collective-permute-start | bytes 442376 | tf_op jit(solution)/shard_map/ppermute | solution.py:409
  212.5 10.6 %collective-permute-start.15 = (bf16[576,128]{1,0:T(8,128)(2,1)S(1)}, bf16[576,128]{1,0:T(8,128)(2,1)S(1)}, u32[]{:S(2)}, u32[]{:S(2)}) collective-permute-start(bf16[576,128]{1,0:T(8,128)(2,1)S(1)} %bitcast.21), channel_id=1, source_target_pairs={{0,1},{1,0},{2,3},{3,2},{4,5},{5,4},{6,7},{7,6},{8,9},{9,8},{10,11... | collective-permute-start | bytes 442376 | tf_op jit(solution)/shard_map/ppermute | solution.py:404
  216.1 1.9 copy-start.3
  220.7 2.4 %collective-permute-start.16 = (bf16[576,128]{1,0:T(8,128)(2,1)S(1)}, bf16[576,128]{1,0:T(8,128)(2,1)S(1)}, u32[]{:S(2)}, u32[]{:S(2)}) collective-permute-start(bf16[576,128]{1,0:T(8,128)(2,1)S(1)} %collective-permute-done.12.refs_1_), channel_id=1, source_target_pairs={{0,1},{1,0},{2,3},{3,2},{4,5},{5,4},{6,7},{7,6},{8,9},{9,8},{10,11... | collective-permute-start | bytes 442376 | tf_op jit(solution)/shard_map/ppermute | solution.py:404
  221.6 1.4 collective-permute-start.17
  221.6 1.6 collective-permute-start.18

commit v5 on v4

--- a/solution.py
+++ b/solution.py
@@ -36,7 +36,7 @@
     for a in range(2):
         x_ref[a] = dot(r_ref[a], t_ref[a], 1, 0)
 
-    @pl.loop(0, NDEV // 2, unroll=4)
+    @pl.loop(0, NDEV // 2, unroll=8)
     def _(i):
         rows = pl.ds(pl.multiple_of(i * 2 * LJ, 2 * LJ), 2 * LJ)
         two = [t_ref[a, rows, :].astype(F32) * g_ref[a, rows, :].astype(F32) for a in range(2)]
@@ -91,7 +91,7 @@
 
 
 def load_columns(kind, parts_ref, x_ref):
-    @pl.loop(0, NDEV, unroll=4)
+    @pl.loop(0, NDEV, unroll=8)
     def _(i):
         for p in range(2):
             put_rows(x_ref, pl.ds(i * 32 + p * 16, 16), parts_ref[i, p, kind].astype(F32))
@@ -104,7 +104,7 @@
         g = get_rows(x_ref, at).astype(BF16)
         put_rows(x_ref, at, dot(l_ref[j], g, 0, 0))
 
-    @pl.loop(0, NDEV, unroll=4)
+    @pl.loop(0, NDEV, unroll=8)
     def _(i):
         o_ref[i] = get_rows(x_ref, pl.ds(i * 32, 32)).astype(BF16)
 

time: 225 us -> 225 us (level)
  starting transfers between devices: 58.7 us -> 65.5 us
  waiting for transfers between devices: 124 us -> 118 us
    ppermute x13, starting transfers between devices: 13.8 us -> 26.3 us  [send(): return lax.ppermute(v, axis, [(i, (i + k) % n) for i in range(n)])]
    ppermute x13, waiting for transfers between devices: 47.8 us -> 41.6 us  [send(): return lax.ppermute(v, axis, [(i, (i + k) % n) for i in range(n)])]
    all_to_all x4, starting transfers between devices: 39.4 us -> 34 us  [exchange(): return lax.all_to_all(v, axes, split_axis=0, concat_axis=0, tiled=True)]
where the time goes in v5:
time: 225 us
  waiting for transfers between devices  118 us (52%)
  starting transfers between devices  65.5 us (29%)
  Pallas kernels  28.2 us (13%)
  local copies, waits for them, and re-layouts  11.6 us (5%)
    all_to_all x4, waiting for transfers between devices, exchange(): return lax.all_to_all(v, axes, split_axis=0, concat_axis=0, tiled=True)  72.4 us
    ppermute x13, waiting for transfers between devices, send(): return lax.ppermute(v, axis, [(i, (i + k) % n) for i in range(n)])  41.6 us
    all_to_all x4, starting transfers between devices, exchange(): return lax.all_to_all(v, axes, split_axis=0, concat_axis=0, tiled=True)  34 us
    ppermute x13, starting transfers between devices, send(): return lax.ppermute(v, axis, [(i, (i + k) % n) for i in range(n)])  26.3 us
    unnamed x35, local copies, waits for them, and re-layouts  11.6 us
    ppermute x6, starting transfers between devices, swap(): return lax.ppermute(v, 'c', [(0, 1), (1, 0)])  5.14 us
  transfers between devices with their start and end apart: 23, of which 11 were waited for; matrix products, arithmetic and copies ran while one was open for 0% of the time, Pallas kernels for 9%

profile of v5, /device:TPU:1, one launch (start us, length us, event | category | flops | bytes accessed | tf_op | source)
XLA Modules:
  0.0 224.6 jit_solution(13171678391114609303)
XLA Ops:
  0.6 3.8 %first_parts.1 = bf16[32,2,2,16,768]{4,3,2,1,0:T(8,128)(2,1)} custom-call(bf16[4,256,768]{2,1,0:T(8,128)(2,1)} %bitcast.13, bf16[4,256,768]{2,1,0:T(8,128)(2,1)} %bitcast.16, bf16[4,256,256]{2,1,0:T(8,128)(2,1)} %r_ref.3), custom_call_target="tpu_custom_call" | custom-call | tf_op jit(solution)/shard_map/first_parts/pallas_call | solution.py:52
  4.4 12.8 %all-to-all-start = ((bf16[32,2,2,16,768]{4,3,2,1,0:T(8,128)(2,1)}), bf16[32,2,2,16,768]{4,3,2,1,0:T(8,128)(2,1)S(1)}, u32[]{:S(2)}, u32[]{:S(2)}) async-start(bf16[32,2,2,16,768]{4,3,2,1,0:T(8,128)(2,1)} %first_parts.1), calls=%async_computation | async-start | bytes 6291456 | tf_op jit(solution)/shard_map/all_to_all | solution.py:400
  17.2 1.4 copy-done
  18.6 1.3 copy-done.4
  19.9 1.4 project.1.p_ref
  21.3 1.1 copy-done.8
  22.4 67.3 %all-to-all-done.parts_ref = bf16[32,2,2,16,768]{4,3,2,1,0:T(8,128)(2,1)S(1)} async-done(((bf16[32,2,2,16,768]{4,3,2,1,0:T(8,128)(2,1)}), bf16[32,2,2,16,768]{4,3,2,1,0:T(8,128)(2,1)S(1)}, u32[]{:S(2)}, u32[]{:S(2)}) %all-to-all-start) | async-done | bytes 3145760 | tf_op jit(solution)/shard_map/all_to_all | solution.py:400
  89.7 1.7 grad_one_columns.1
  91.4 1.1 copy-done.7
  92.6 6.1 %all-to-all-start.1 = ((bf16[32,32,768]{2,1,0:T(8,128)(2,1)}), bf16[32,32,768]{2,1,0:T(8,128)(2,1)}, u32[]{:S(2)}, u32[]{:S(2)}) async-start(bf16[32,32,768]{2,1,0:T(8,128)(2,1)} %copy-done.7), calls=%async_computation.1 | async-start | bytes 3145728 | tf_op jit(solution)/shard_map/all_to_all | solution.py:400
  98.7 4.0 %weight_grad.1 = (bf16[1024,768]{1,0:T(8,128)(2,1)S(1)}, bf16[8,128,768]{2,1,0:T(8,128)(2,1)S(1)}, f32[4,576,128]{2,1,0:T(8,128)S(1)}, bf16[4,576,128]{2,1,0:T(8,128)(2,1)}) custom-call(s32[1]{0:T(128)} %bitcast.1.core_ref.half_ref, bf16[32,2,2,16,768]{4,3,2,1,0:T(8,128)(2,1)S(1)} %all-to-all-done.parts_ref, bf16[8,128,128]{2,1,0:T(8,128)(2,1)S(1)} %copy-done.11), custom_call_target="tpu_custom_call" | custom-call | flops 1000 | bytes 1000 | tf_op jit(solution)/shard_map/weight_grad/pallas_call | solution.py:146
  102.7 3.2 %two_columns.1 = (bf16[16,2,192,128]{3,2,1,0:T(8,128)(2,1)S(1)}, f32[8,128,128]{2,1,0:T(8,128)S(1)}) custom-call(bf16[1024,768]{1,0:T(8,128)(2,1)S(1)} %get-tuple-element.47.t_ref, bf16[768,768]{1,0:T(8,128)(2,1)S(1)} %copy-done.5, bf16[8,128,128]{2,1,0:T(8,128)(2,1)S(1)} %copy-done.11, bf16[8,128,768]{2,1,0:T(8,128)(2,1)S(1)} %get-tuple-element.48.gj_ref), custom_call_target="tpu_custom_call" | custom-call | flops 1000 | bytes 1000 | tf_op jit(solution)/shard_map/two_columns/pallas_call | solution.py:182
  106.0 0.8 copy-done.15
  107.2 4.1 %collective-permute-done.1.got_ref = bf16[4,576,128]{2,1,0:T(8,128)(2,1)} collective-permute-done((bf16[4,576,128]{2,1,0:T(8,128)(2,1)}, bf16[4,576,128]{2,1,0:T(8,128)(2,1)}, u32[]{:S(2)}, u32[]{:S(2)}) %collective-permute-start.1) | collective-permute-done | bytes 589856 | tf_op jit(solution)/shard_map/ppermute | solution.py:404
  111.3 1.3 copy-done.14
  112.6 1.2 spread.1
  113.8 1.2 collective-permute-start.2
  114.9 2.6 %collective-permute-start.3 = (bf16[576,128]{1,0:T(8,128)(2,1)S(1)}, bf16[576,128]{1,0:T(8,128)(2,1)S(1)}, u32[]{:S(2)}, u32[]{:S(2)}) collective-permute-start(bf16[576,128]{1,0:T(8,128)(2,1)S(1)} %get-tuple-element.54), channel_id=1, source_target_pairs={{0,64},{32,96},{64,0},{96,32},{1,65},{33,97},{65,1},{97,33},{2,66}... | collective-permute-start | bytes 442376 | tf_op jit(solution)/shard_map/ppermute | solution.py:409
  117.5 1.2 collective-permute-start.4
  118.7 1.6 collective-permute-done.2.a_ref
  120.3 4.1 %collective-permute-done.3.b_ref = bf16[576,128]{1,0:T(8,128)(2,1)S(1)} collective-permute-done((bf16[576,128]{1,0:T(8,128)(2,1)S(1)}, bf16[576,128]{1,0:T(8,128)(2,1)S(1)}, u32[]{:S(2)}, u32[]{:S(2)}) %collective-permute-start.3) | collective-permute-done | bytes 147488 | tf_op jit(solution)/shard_map/ppermute | solution.py:409
  124.5 1.5 join_two.1
  125.9 5.0 %all-to-all-done.1.parts_ref = bf16[32,32,768]{2,1,0:T(8,128)(2,1)} async-done(((bf16[32,32,768]{2,1,0:T(8,128)(2,1)}), bf16[32,32,768]{2,1,0:T(8,128)(2,1)}, u32[]{:S(2)}, u32[]{:S(2)}) %all-to-all-start.1) | async-done | bytes 1572896 | tf_op jit(solution)/shard_map/all_to_all | solution.py:400
  131.0 7.0 %all-to-all-start.2 = ((bf16[16,432,128]{2,1,0:T(8,128)(2,1)}), bf16[16,432,128]{2,1,0:T(8,128)(2,1)S(1)}, u32[]{:S(2)}, u32[]{:S(2)}) async-start(bf16[16,432,128]{2,1,0:T(8,128)(2,1)} %join_two.1), calls=%async_computation.2 | async-start | bytes 3538944 | tf_op jit(solution)/shard_map/all_to_all | solution.py:400
  138.0 1.0 copy-done.16
  139.0 2.5 %block_grads.1 = (bf16[4,256,768]{2,1,0:T(8,128)(2,1)S(1)}, f32[768,128]{1,0:T(8,128)S(1)}, bf16[768,128]{1,0:T(8,128)(2,1)S(1)}, bf16[768,128]{1,0:T(8,128)(2,1)S(1)}, bf16[768,128]{1,0:T(8,128)(2,1)S(1)}) custom-call(s32[1]{0:T(128)} %bitcast.x_index_ref, bf16[32,32,768]{2,1,0:T(8,128)(2,1)} %all-to-all-done.1.parts_ref, ...), custom_call_target="tpu_custom_call" | custom-call | flops 1000 | bytes 1000 | tf_op jit(solution)/shard_map/block_grads/pallas_call | solution.py:334
  141.6 1.2 collective-permute-start.5
  142.8 7.9 %collective-permute-start.6 = (bf16[768,128]{1,0:T(8,128)(2,1)S(1)}, bf16[768,128]{1,0:T(8,128)(2,1)S(1)}, u32[]{:S(2)}, u32[]{:S(2)}) collective-permute-start(bf16[768,128]{1,0:T(8,128)(2,1)S(1)} %get-tuple-element.62), channel_id=1, source_target_pairs={{0,64},{32,96},{64,0},{96,32},{1,65},{33,97},{65,1},{97,33},{2,66}... | collective-permute-start | bytes 589832 | tf_op jit(solution)/shard_map/ppermute | solution.py:409
  150.7 2.9 %collective-permute-done.5 = bf16[768,128]{1,0:T(8,128)(2,1)S(1)} collective-permute-done((bf16[768,128]{1,0:T(8,128)(2,1)S(1)}, bf16[768,128]{1,0:T(8,128)(2,1)S(1)}, u32[]{:S(2)}, u32[]{:S(2)}) %collective-permute-start.5) | collective-permute-done | bytes 196640 | tf_op jit(solution)/shard_map/ppermute | solution.py:409
  153.5 5.6 %collective-permute-done.6 = bf16[768,128]{1,0:T(8,128)(2,1)S(1)} collective-permute-done((bf16[768,128]{1,0:T(8,128)(2,1)S(1)}, bf16[768,128]{1,0:T(8,128)(2,1)S(1)}, u32[]{:S(2)}, u32[]{:S(2)}) %collective-permute-start.6) | collective-permute-done | bytes 196640 | tf_op jit(solution)/shard_map/ppermute | solution.py:409
  159.2 1.4 collective-permute-start.8
  160.6 2.6 %back_projected.1.b_ref = f32[4,256,768]{2,1,0:T(8,128)S(1)} custom-call(bf16[4,256,768]{2,1,0:T(8,128)(2,1)S(1)} %get-tuple-element.64.g_ref, bf16[4,256,256]{2,1,0:T(8,128)(2,1)S(1)} %copy-done.12, bf16[768,768]{1,0:T(8,128)(2,1)S(1)} %copy-done.6), custom_call_target="tpu_custom_call" | custom-call | flops 1000 | bytes 1000 | tf_op jit(solution)/shard_map/back_projected/pallas_call | solution.py:353
  163.3 1.6 copy-done.2
  164.9 19.2 %collective-permute-done.8 = bf16[768,128]{1,0:T(8,128)(2,1)S(1)} collective-permute-done((bf16[768,128]{1,0:T(8,128)(2,1)S(1)}, bf16[768,128]{1,0:T(8,128)(2,1)S(1)}, u32[]{:S(2)}, u32[]{:S(2)}) %collective-permute-start.8) | collective-permute-done | bytes 196640 | tf_op jit(solution)/shard_map/ppermute | solution.py:409
  184.2 0.8 weight_sum.1
  185.0 8.1 %all-to-all-start.3 = ((bf16[32,48,128]{2,1,0:T(8,128)(2,1)}), bf16[32,48,128]{2,1,0:T(8,128)(2,1)S(1)}, u32[]{:S(2)}, u32[]{:S(2)}) async-start(bf16[32,48,128]{2,1,0:T(8,128)(2,1)} %weight_sum.1), calls=%async_computation.3 | async-start | bytes 786432 | tf_op jit(solution)/shard_map/all_to_all | solution.py:400
  193.1 2.7 %collective-permute-start.10 = (bf16[768,128]{1,0:T(8,128)(2,1)S(1)}, bf16[768,128]{1,0:T(8,128)(2,1)S(1)}, u32[]{:S(2)}, u32[]{:S(2)}) collective-permute-start(bf16[768,128]{1,0:T(8,128)(2,1)S(1)} %add_convert_fusion.own_ref), channel_id=1, source_target_pairs={{0,64},{32,96},{64,0},{96,32},{1,65},{33,97},{65,1},{97,33},{2,66}... | collective-permute-start | bytes 589832 | tf_op jit(solution)/shard_map/ppermute | solution.py:409
  195.8 3.1 %collective-permute-start.11 = (bf16[768,128]{1,0:T(8,128)(2,1)S(1)}, bf16[768,128]{1,0:T(8,128)(2,1)S(1)}, u32[]{:S(2)}, u32[]{:S(2)}) collective-permute-start(bf16[768,128]{1,0:T(8,128)(2,1)S(1)} %add_convert_fusion.own_ref), channel_id=1, source_target_pairs={{0,96},{32,0},{64,32},{96,64},{1,97},{33,1},{65,33},{97,65},{2,98}... | collective-permute-start | bytes 589832 | tf_op jit(solution)/shard_map/ppermute | solution.py:409
  199.4 0.7 collective-permute-done.10.b_ref
  200.1 7.5 %collective-permute-done.11.c_ref = bf16[768,128]{1,0:T(8,128)(2,1)S(1)} collective-permute-done((bf16[768,128]{1,0:T(8,128)(2,1)S(1)}, bf16[768,128]{1,0:T(8,128)(2,1)S(1)}, u32[]{:S(2)}, u32[]{:S(2)}) %collective-permute-start.11) | collective-permute-done | bytes 196640 | tf_op jit(solution)/shard_map/ppermute | solution.py:409
  207.5 1.0 place_blocks.1
  208.7 0.7 collective-permute-start.12
  209.4 3.9 %collective-permute-start.13 = (bf16[576,128]{1,0:T(8,128)(2,1)S(1)}, bf16[576,128]{1,0:T(8,128)(2,1)S(1)}, u32[]{:S(2)}, u32[]{:S(2)}) collective-permute-start(bf16[576,128]{1,0:T(8,128)(2,1)S(1)} %bitcast.19), channel_id=1, source_target_pairs={{0,64},{32,96},{64,0},{96,32},{1,65},{33,97},{65,1},{97,33},{2,66}... | collective-permute-start | bytes 442376 | tf_op jit(solution)/shard_map/ppermute | solution.py:409
  213.4 3.6 %collective-permute-start.15 = (bf16[576,128]{1,0:T(8,128)(2,1)S(1)}, bf16[576,128]{1,0:T(8,128)(2,1)S(1)}, u32[]{:S(2)}, u32[]{:S(2)}) collective-permute-start(bf16[576,128]{1,0:T(8,128)(2,1)S(1)} %bitcast.21), channel_id=1, source_target_pairs={{0,1},{1,0},{2,3},{3,2},{4,5},{5,4},{6,7},{7,6},{8,9},{9,8},{10,11... | collective-permute-start | bytes 442376 | tf_op jit(solution)/shard_map/ppermute | solution.py:404
  217.0 1.9 copy-done.3
  218.9 2.7 %end.1 = (bf16[4,256,768]{2,1,0:T(8,128)(2,1)}, bf16[4,256,768]{2,1,0:T(8,128)(2,1)}) custom-call(bf16[16,432,128]{2,1,0:T(8,128)(2,1)S(1)} %all-to-all-done.2.p_ref.parts_ref, bf16[4,256,768]{2,1,0:T(8,128)(2,1)S(1)} %bitcast.15, bf16[4,256,768]{2,1,0:T(8,128)(2,1)S(1)} %bitcast.17, f32[4,256,768]{2,1,0:T(8,128)S(1)} %copy-done.3), custom_call_target="tpu_custom_call" | custom-call | tf_op jit(solution)/shard_map/end/pallas_call | solution.py:388
  222.6 0.9 place_half.2.refs_4_
  223.7 0.9 place_half.3
  (51 shorter events, 2.6 us)
Async XLA Ops:
  4.4 85.3 %all-to-all-start = ((bf16[32,2,2,16,768]{4,3,2,1,0:T(8,128)(2,1)}), bf16[32,2,2,16,768]{4,3,2,1,0:T(8,128)(2,1)S(1)}, u32[]{:S(2)}, u32[]{:S(2)}) async-start(bf16[32,2,2,16,768]{4,3,2,1,0:T(8,128)(2,1)} %first_parts.1), calls=%async_computation | async-start | bytes 6291456 | tf_op jit(solution)/shard_map/all_to_all | solution.py:400
  17.2 1.4 copy-start
  18.6 1.3 copy-start.4
  19.9 69.9 %copy-start.11 = (bf16[8,128,128]{2,1,0:T(8,128)(2,1)S(1)}, bf16[8,128,128]{2,1,0:T(8,128)(2,1)}, u32[]{:S(2)}) copy-start(bf16[8,128,128]{2,1,0:T(8,128)(2,1)} %l_ref.5) | copy-start | bytes 786436
  21.3 1.1 copy-start.8
  91.4 1.1 copy-start.7
  92.6 38.4 %all-to-all-start.1 = ((bf16[32,32,768]{2,1,0:T(8,128)(2,1)}), bf16[32,32,768]{2,1,0:T(8,128)(2,1)}, u32[]{:S(2)}, u32[]{:S(2)}) async-start(bf16[32,32,768]{2,1,0:T(8,128)(2,1)} %copy-done.7), calls=%async_computation.1 | async-start | bytes 3145728 | tf_op jit(solution)/shard_map/all_to_all | solution.py:400
  98.7 4.0 %copy-start.5 = (bf16[768,768]{1,0:T(8,128)(2,1)S(1)}, bf16[768,768]{1,0:T(8,128)(2,1)}, u32[]{:S(2)}) copy-start(bf16[768,768]{1,0:T(8,128)(2,1)} %w_ref.5) | copy-start | bytes 3538948
  102.7 3.2 %copy-start.13 = (f32[4,576,128]{2,1,0:T(8,128)}, f32[4,576,128]{2,1,0:T(8,128)S(1)}, u32[]{:S(2)}) copy-start(f32[4,576,128]{2,1,0:T(8,128)S(1)} %get-tuple-element.50.mine_ref) | copy-start | bytes 3538948
  105.9 0.8 copy-start.15
  106.7 17.7 %collective-permute-start = (bf16[16,2,192,128]{3,2,1,0:T(8,128)(2,1)S(1)}, bf16[16,2,192,128]{3,2,1,0:T(8,128)(2,1)S(1)}, u32[]{:S(2)}, u32[]{:S(2)}) collective-permute-start(bf16[16,2,192,128]{3,2,1,0:T(8,128)(2,1)S(1)} %get-tuple-element.49.own_ref), channel_id=1, source_target_pairs={{0,1},{1,0},{2,3},{3,2},{4,5},{5,4},{6,7},{7,6},{8,9},{9,8},{10,11... | collective-permute-start | bytes 4718600 | tf_op jit(solution)/shard_map/ppermute | solution.py:404
  107.0 4.3 %collective-permute-start.1 = (bf16[4,576,128]{2,1,0:T(8,128)(2,1)}, bf16[4,576,128]{2,1,0:T(8,128)(2,1)}, u32[]{:S(2)}, u32[]{:S(2)}) collective-permute-start(bf16[4,576,128]{2,1,0:T(8,128)(2,1)} %get-tuple-element.51), channel_id=1, source_target_pairs={{0,1},{1,0},{2,3},{3,2},{4,5},{5,4},{6,7},{7,6},{8,9},{9,8},{10,11... | collective-permute-start | bytes 1769480 | tf_op jit(solution)/shard_map/ppermute | solution.py:404
  111.3 1.3 copy-start.14
  113.8 6.5 %collective-permute-start.2 = (bf16[576,128]{1,0:T(8,128)(2,1)S(1)}, bf16[576,128]{1,0:T(8,128)(2,1)S(1)}, u32[]{:S(2)}, u32[]{:S(2)}) collective-permute-start(bf16[576,128]{1,0:T(8,128)(2,1)S(1)} %get-tuple-element.53), channel_id=1, source_target_pairs={{0,32},{32,64},{64,96},{96,0},{1,33},{33,65},{65,97},{97,1},{2,34}... | collective-permute-start | bytes 442376 | tf_op jit(solution)/shard_map/ppermute | solution.py:409
  114.9 9.5 %collective-permute-start.3 = (bf16[576,128]{1,0:T(8,128)(2,1)S(1)}, bf16[576,128]{1,0:T(8,128)(2,1)S(1)}, u32[]{:S(2)}, u32[]{:S(2)}) collective-permute-start(bf16[576,128]{1,0:T(8,128)(2,1)S(1)} %get-tuple-element.54), channel_id=1, source_target_pairs={{0,64},{32,96},{64,0},{96,32},{1,65},{33,97},{65,1},{97,33},{2,66}... | collective-permute-start | bytes 442376 | tf_op jit(solution)/shard_map/ppermute | solution.py:409
  117.5 7.0 %collective-permute-start.4 = (bf16[576,128]{1,0:T(8,128)(2,1)S(1)}, bf16[576,128]{1,0:T(8,128)(2,1)S(1)}, u32[]{:S(2)}, u32[]{:S(2)}) collective-permute-start(bf16[576,128]{1,0:T(8,128)(2,1)S(1)} %get-tuple-element.55), channel_id=1, source_target_pairs={{0,96},{32,0},{64,32},{96,64},{1,97},{33,1},{65,33},{97,65},{2,98}... | collective-permute-start | bytes 442376 | tf_op jit(solution)/shard_map/ppermute | solution.py:409
  131.0 7.0 %copy-start.9 = (bf16[4,256,768]{2,1,0:T(8,128)(2,1)S(1)}, bf16[4,256,768]{2,1,0:T(8,128)(2,1)}, u32[]{:S(2)}) copy-start(bf16[4,256,768]{2,1,0:T(8,128)(2,1)} %copy-done.8) | copy-start | bytes 4718596
  131.0 53.2 %all-to-all-start.2 = ((bf16[16,432,128]{2,1,0:T(8,128)(2,1)}), bf16[16,432,128]{2,1,0:T(8,128)(2,1)S(1)}, u32[]{:S(2)}, u32[]{:S(2)}) async-start(bf16[16,432,128]{2,1,0:T(8,128)(2,1)} %join_two.1), calls=%async_computation.2 | async-start | bytes 3538944 | tf_op jit(solution)/shard_map/all_to_all | solution.py:400
  138.0 1.0 copy-start.16
  139.0 21.6 %copy-start.6 = (bf16[768,768]{1,0:T(8,128)(2,1)S(1)}, bf16[768,768]{1,0:T(8,128)(2,1)}, u32[]{:S(2)}) copy-start(bf16[768,768]{1,0:T(8,128)(2,1)} %w_ref.5) | copy-start | bytes 3538948
  139.0 21.6 %copy-start.12 = (bf16[4,256,256]{2,1,0:T(8,128)(2,1)S(1)}, bf16[4,256,256]{2,1,0:T(8,128)(2,1)}, u32[]{:S(2)}) copy-start(bf16[4,256,256]{2,1,0:T(8,128)(2,1)} %r_ref.3) | copy-start | bytes 1572868
  141.6 12.0 %collective-permute-start.5 = (bf16[768,128]{1,0:T(8,128)(2,1)S(1)}, bf16[768,128]{1,0:T(8,128)(2,1)S(1)}, u32[]{:S(2)}, u32[]{:S(2)}) collective-permute-start(bf16[768,128]{1,0:T(8,128)(2,1)S(1)} %get-tuple-element.61), channel_id=1, source_target_pairs={{0,32},{32,64},{64,96},{96,0},{1,33},{33,65},{65,97},{97,1},{2,34}... | collective-permute-start | bytes 589832 | tf_op jit(solution)/shard_map/ppermute | solution.py:409
  142.8 16.4 %collective-permute-start.6 = (bf16[768,128]{1,0:T(8,128)(2,1)S(1)}, bf16[768,128]{1,0:T(8,128)(2,1)S(1)}, u32[]{:S(2)}, u32[]{:S(2)}) collective-permute-start(bf16[768,128]{1,0:T(8,128)(2,1)S(1)} %get-tuple-element.62), channel_id=1, source_target_pairs={{0,64},{32,96},{64,0},{96,32},{1,65},{33,97},{65,1},{97,33},{2,66}... | collective-permute-start | bytes 589832 | tf_op jit(solution)/shard_map/ppermute | solution.py:409
  150.7 8.5 %collective-permute-start.7 = (bf16[768,128]{1,0:T(8,128)(2,1)S(1)}, bf16[768,128]{1,0:T(8,128)(2,1)S(1)}, u32[]{:S(2)}, u32[]{:S(2)}) collective-permute-start(bf16[768,128]{1,0:T(8,128)(2,1)S(1)} %get-tuple-element.63), channel_id=1, source_target_pairs={{0,96},{32,0},{64,32},{96,64},{1,97},{33,1},{65,33},{97,65},{2,98}... | collective-permute-start | bytes 589832 | tf_op jit(solution)/shard_map/ppermute | solution.py:409
  159.2 24.8 %collective-permute-start.8 = (bf16[768,128]{1,0:T(8,128)(2,1)S(1)}, bf16[768,128]{1,0:T(8,128)(2,1)S(1)}, u32[]{:S(2)}, u32[]{:S(2)}) collective-permute-start(bf16[768,128]{1,0:T(8,128)(2,1)S(1)} %add_convert_fusion.1), channel_id=1, source_target_pairs={{0,128},{128,0},{1,129},{129,1},{2,130},{130,2},{3,131},{131,3},{4... | collective-permute-start | bytes 589832 | tf_op jit(solution)/shard_map/ppermute | solution.py:409
  163.3 1.6 copy-start.2
  185.0 23.6 %all-to-all-start.3 = ((bf16[32,48,128]{2,1,0:T(8,128)(2,1)}), bf16[32,48,128]{2,1,0:T(8,128)(2,1)S(1)}, u32[]{:S(2)}, u32[]{:S(2)}) async-start(bf16[32,48,128]{2,1,0:T(8,128)(2,1)} %weight_sum.1), calls=%async_computation.3 | async-start | bytes 786432 | tf_op jit(solution)/shard_map/all_to_all | solution.py:400
  193.1 7.0 %collective-permute-start.10 = (bf16[768,128]{1,0:T(8,128)(2,1)S(1)}, bf16[768,128]{1,0:T(8,128)(2,1)S(1)}, u32[]{:S(2)}, u32[]{:S(2)}) collective-permute-start(bf16[768,128]{1,0:T(8,128)(2,1)S(1)} %add_convert_fusion.own_ref), channel_id=1, source_target_pairs={{0,64},{32,96},{64,0},{96,32},{1,65},{33,97},{65,1},{97,33},{2,66}... | collective-permute-start | bytes 589832 | tf_op jit(solution)/shard_map/ppermute | solution.py:409
  195.8 11.8 %collective-permute-start.11 = (bf16[768,128]{1,0:T(8,128)(2,1)S(1)}, bf16[768,128]{1,0:T(8,128)(2,1)S(1)}, u32[]{:S(2)}, u32[]{:S(2)}) collective-permute-start(bf16[768,128]{1,0:T(8,128)(2,1)S(1)} %add_convert_fusion.own_ref), channel_id=1, source_target_pairs={{0,96},{32,0},{64,32},{96,64},{1,97},{33,1},{65,33},{97,65},{2,98}... | collective-permute-start | bytes 589832 | tf_op jit(solution)/shard_map/ppermute | solution.py:409
  198.9 8.6 %collective-permute-start.9 = (bf16[768,128]{1,0:T(8,128)(2,1)S(1)}, bf16[768,128]{1,0:T(8,128)(2,1)S(1)}, u32[]{:S(2)}, u32[]{:S(2)}) collective-permute-start(bf16[768,128]{1,0:T(8,128)(2,1)S(1)} %add_convert_fusion.own_ref), channel_id=1, source_target_pairs={{0,32},{32,64},{64,96},{96,0},{1,33},{33,65},{65,97},{97,1},{2,34}... | collective-permute-start | bytes 589832 | tf_op jit(solution)/shard_map/ppermute | solution.py:409
  208.5 8.5 %copy-start.1 = (bf16[1,4,256,768]{3,2,1,0:T(8,128)(2,1)S(1)}, bf16[1,4,256,768]{3,2,1,0:T(8,128)(2,1)}, u32[]{:S(2)}) copy-start(bf16[1,4,256,768]{3,2,1,0:T(8,128)(2,1)} %param.5) | copy-start | bytes 4718596
  208.5 8.5 %copy-start.10 = (bf16[1,4,256,768]{3,2,1,0:T(8,128)(2,1)S(1)}, bf16[1,4,256,768]{3,2,1,0:T(8,128)(2,1)}, u32[]{:S(2)}) copy-start(bf16[1,4,256,768]{3,2,1,0:T(8,128)(2,1)} %param.6) | copy-start | bytes 4718596
  208.7 12.9 %collective-permute-start.12 = (bf16[576,128]{1,0:T(8,128)(2,1)S(1)}, bf16[576,128]{1,0:T(8,128)(2,1)S(1)}, u32[]{:S(2)}, u32[]{:S(2)}) collective-permute-start(bf16[576,128]{1,0:T(8,128)(2,1)S(1)} %bitcast.18), channel_id=1, source_target_pairs={{0,32},{32,64},{64,96},{96,0},{1,33},{33,65},{65,97},{97,1},{2,34}... | collective-permute-start | bytes 442376 | tf_op jit(solution)/shard_map/ppermute | solution.py:409
  209.4 12.2 %collective-permute-start.13 = (bf16[576,128]{1,0:T(8,128)(2,1)S(1)}, bf16[576,128]{1,0:T(8,128)(2,1)S(1)}, u32[]{:S(2)}, u32[]{:S(2)}) collective-permute-start(bf16[576,128]{1,0:T(8,128)(2,1)S(1)} %bitcast.19), channel_id=1, source_target_pairs={{0,64},{32,96},{64,0},{96,32},{1,65},{33,97},{65,1},{97,33},{2,66}... | collective-permute-start | bytes 442376 | tf_op jit(solution)/shard_map/ppermute | solution.py:409
  213.4 8.2 %collective-permute-start.14 = (bf16[576,128]{1,0:T(8,128)(2,1)S(1)}, bf16[576,128]{1,0:T(8,128)(2,1)S(1)}, u32[]{:S(2)}, u32[]{:S(2)}) collective-permute-start(bf16[576,128]{1,0:T(8,128)(2,1)S(1)} %bitcast.20), channel_id=1, source_target_pairs={{0,96},{32,0},{64,32},{96,64},{1,97},{33,1},{65,33},{97,65},{2,98}... | collective-permute-start | bytes 442376 | tf_op jit(solution)/shard_map/ppermute | solution.py:409
  213.4 10.2 %collective-permute-start.15 = (bf16[576,128]{1,0:T(8,128)(2,1)S(1)}, bf16[576,128]{1,0:T(8,128)(2,1)S(1)}, u32[]{:S(2)}, u32[]{:S(2)}) collective-permute-start(bf16[576,128]{1,0:T(8,128)(2,1)S(1)} %bitcast.21), channel_id=1, source_target_pairs={{0,1},{1,0},{2,3},{3,2},{4,5},{5,4},{6,7},{7,6},{8,9},{9,8},{10,11... | collective-permute-start | bytes 442376 | tf_op jit(solution)/shard_map/ppermute | solution.py:404
  217.0 1.9 copy-start.3
  221.6 1.9 collective-permute-start.16
  222.1 1.4 collective-permute-start.17
  222.2 1.5 collective-permute-start.18
